TPU v7x, 32 devices: a whole 2x2x4 slice. The times are simulated.
32 devices in a mesh: grp: 4 (over y, x), slab: 8 (over z, core).
Axes of the slice: x: 2, y: 2, z: 4, core: 2. Of those that a mesh axis runs over, the one named last changes fastest.
Arguments:
- margin: bfloat16 [128, 5, 128, 128], P(('grp', 'slab')), may hold values from -2 to 2
- factor: bfloat16 [128, 5, 128, 128], P(('grp', 'slab')), may hold values from -2 to 2
- pattern: int32 [128, 5], P(('grp', 'slab')), may hold values from 0 to 1, as said below
Outputs:
- refined: bfloat16 [128, 5, 128, 128], P(('grp', 'slab'))
- defect_norm: float32 [], replicated
Inputs may be any that keep to these rules, and one draw needn't show every extreme that they name: The pattern is symmetric: pattern[j, o] equals pattern[j + o - 2, 4 - o]. The diagonal block (o = 2) is always present and blocks whose row lies outside the matrix are absent; the share of present blocks varies from region to region.
All inputs are finite; a program needn't handle non-finite values.
Results may differ from a plain program's by a relative error of at most 0.0054.
Values may be sent and summed in bfloat16 or wider, within the bound.
No kernel may reach another device: no remote copies, remote signals or barrier semaphores. Data moves between devices by JAX's collectives and lax.ppermute only.
A program may use at most 64 MiB of HBM per device.

v0:
```python
import jax
import jax.numpy as jnp
from jax import lax
from jax.sharding import PartitionSpec as P


def padded(cells, sides, width):
    for axis, dim in sides:
        count = lax.axis_size(axis)
        ends = count - 1
        head = lax.slice_in_dim(cells, 0, width, axis=dim)
        tail = lax.slice_in_dim(cells, cells.shape[dim] - width, cells.shape[dim], axis=dim)
        cells = jnp.concatenate(
            [
                lax.ppermute(tail, axis, [(i, (i + 1) % count) for i in range(ends)]),
                cells,
                lax.ppermute(head, axis, [((i + 1) % count, i) for i in range(ends)]),
            ],
            axis=dim,
        )
    return cells


def image_terms(band_half):
    return [
        [
            (inner_lag, outer_lag - inner_lag + band_half, inner_lag + band_half)
            for inner_lag in range(
                max(-band_half, outer_lag - band_half), min(band_half, outer_lag + band_half) + 1
            )
        ]
        for outer_lag in range(-2 * band_half, 2 * band_half + 1)
    ]


def defect_terms(band_half):
    return [
        [
            (outer_lag, inner_lag - outer_lag + band_half, inner_lag + 2 * band_half)
            for inner_lag in range(outer_lag - band_half, outer_lag + band_half + 1)
        ]
        for outer_lag in range(-band_half, band_half + 1)
    ]


def near_terms(band_half):
    return [
        [
            (inner_lag, outer_lag - inner_lag + band_half, inner_lag + band_half)
            for inner_lag in range(
                max(-band_half, outer_lag - band_half), min(band_half, outer_lag + band_half) + 1
            )
        ]
        for outer_lag in range(-band_half, band_half + 1)
    ]


def band_product(left_ext, right_own, term_list, transpose_left, band_half, columns):
    left_stack = jnp.stack(
        [
            left_ext[band_half + column_shift : band_half + column_shift + columns, left_offset]
            for column_shift, left_offset, right_offset in term_list
        ],
        axis=1,
    )
    right_stack = jnp.stack(
        [right_own[:, right_offset] for column_shift, left_offset, right_offset in term_list],
        axis=1,
    )
    einsum_form = "cbkm,cbkn->cmn" if transpose_left else "cbmk,cbkn->cmn"
    return jnp.einsum(einsum_form, left_stack, right_stack, preferred_element_type=jnp.float32)


def stack_offsets(left_ext, right_own, term_lists, transpose_left, band_half, columns):
    outputs = [
        band_product(left_ext, right_own, term_list, transpose_left, band_half, columns)
        for term_list in term_lists
    ]
    return jnp.stack(outputs, axis=1)


def defect_halo(defect, band_half):
    return padded(defect, ((("grp", "slab"), 0),), band_half)


def defect_measure(defect, columns, block_size):
    partial_sum = jnp.sum(jnp.square(defect.astype(jnp.float32)))
    squares_sum = lax.psum(partial_sum, ("grp", "slab"))
    entries = columns * lax.axis_size("grp") * lax.axis_size("slab") * block_size
    return jnp.sqrt(squares_sum / entries)


def per_device(margin, factor, pattern):
    columns = margin.shape[0]
    offsets = margin.shape[1]
    band_half = (offsets - 1) // 2
    block_size = margin.shape[2]
    present = pattern.astype(jnp.bfloat16)[:, :, None, None]
    mask_here = present.astype(jnp.float32)
    first_col = lax.axis_index(("grp", "slab")) * columns
    quarter_len = columns * lax.axis_size("slab")
    block_rows = (
        first_col
        + jnp.arange(columns, dtype=jnp.int32)[:, None]
        + jnp.arange(offsets, dtype=jnp.int32)[None, :]
        - band_half
    )
    in_quarter = (block_rows // quarter_len == lax.axis_index("grp")).astype(jnp.bfloat16)[
        :, :, None, None
    ]
    s_eff = margin * present
    z_eff = factor * present * in_quarter
    centre = (jnp.arange(offsets, dtype=jnp.int32) == band_half).astype(jnp.float32)[
        None, :, None, None
    ] * jnp.eye(block_size, dtype=jnp.float32)[None, None]
    joined = jnp.concatenate((s_eff, z_eff), axis=1)
    joined_ext = padded(joined, ((("grp", "slab"), 0),), band_half)
    s_ext = joined_ext[:, :offsets]
    z_ext = joined_ext[:, offsets:]
    applied = stack_offsets(s_ext, z_eff, image_terms(band_half), False, band_half, columns).astype(
        jnp.bfloat16
    )
    defect = (
        mask_here
        * (
            centre
            - stack_offsets(z_ext, applied, defect_terms(band_half), True, band_half, columns)
        )
    ).astype(jnp.bfloat16)
    defect_norm = defect_measure(defect, columns, block_size)
    d_ext = defect_halo(defect, band_half)
    square = (
        mask_here * stack_offsets(d_ext, defect, near_terms(band_half), False, band_half, columns)
    ).astype(jnp.bfloat16)
    first_part = stack_offsets(z_ext, defect, near_terms(band_half), False, band_half, columns)
    second_part = stack_offsets(z_ext, square, near_terms(band_half), False, band_half, columns)
    refined = (
        mask_here * (z_eff.astype(jnp.float32) + 0.5 * first_part + 0.375 * second_part)
    ).astype(jnp.bfloat16)
    return (refined, defect_norm)


def solution(mesh):
    return jax.shard_map(
        per_device,
        mesh=mesh,
        in_specs=(
            P(("grp", "slab"), None, None, None),
            P(("grp", "slab"), None, None, None),
            P(("grp", "slab"), None),
        ),
        out_specs=(P(("grp", "slab"), None, None, None), P()),
        check_vma=False,
    )
```

profile of v0, /device:TPU:0, one launch (start us, length us, event | category | flops | bytes accessed | tf_op | source)
XLA Modules:
  0.0 102.0 jit_solution(2944456633847166172)
XLA Ops:
  0.7 0.7 convert_element_type.44
  1.4 0.1 copy.6
  1.5 1.5 %copy_multiply_fusion = (bf16[4,5,128,128]{3,2,0,1:T(8,128)(2,1)S(1)}, bf16[4,5,128,128]{3,2,0,1:T(8,128)(2,1)S(1)}) fusion(bf16[4,5,128,128]{3,2,1,0:T(8,128)(2,1)} %param.3, bf16[4,5]{0,1:T(8,128)(2,1)S(1)} %copy.6, bf16[4,5]{0,1:T(8,128)(2,1)S(1)} %fusion.189, bf16[4,5,128,128]{3,2,1,0:T(8,128)(2,1)} %param.4), kind=kLoop, calls=%fused_computation.102 | loop fusion | flops 983040 | bytes 2621520 | tf_op jit(solution)/shard_map/mul | solution.py:111
  2.9 1.0 pad_maximum_fusion.1
  3.9 2.4 %collective-permute-start = (bf16[2,10,128,128]{3,2,0,1:T(8,128)(2,1)}, bf16[2,10,128,128]{3,2,0,1:T(8,128)(2,1)S(1)}, u32[]{:S(2)}, u32[]{:S(2)}) collective-permute-start(bf16[2,10,128,128]{3,2,0,1:T(8,128)(2,1)} %get-tuple-element.39), channel_id=1, source_target_pairs={{0,1},{1,2},{2,3},{3,4},{4,5},{5,6},{6,7},{7,8},{8,9},{9,10},{10,1... | collective-permute-start | bytes 1966088 | tf_op jit(solution)/shard_map/ppermute | solution.py:15
  6.3 1.3 %collective-permute-start.1 = (bf16[2,10,128,128]{3,2,0,1:T(8,128)(2,1)S(1)}, bf16[2,10,128,128]{3,2,0,1:T(8,128)(2,1)S(1)}, u32[]{:S(2)}, u32[]{:S(2)}) collective-permute-start(bf16[2,10,128,128]{3,2,0,1:T(8,128)(2,1)S(1)} %get-tuple-element.38), channel_id=1, source_target_pairs={{1,0},{2,1},{3,2},{4,3},{5,4},{6,5},{7,6},{8,7},{9,8},{10,9},{11,1... | collective-permute-start | bytes 1966088 | tf_op jit(solution)/shard_map/ppermute | solution.py:17
  7.6 0.1 copy.5
  7.7 0.1 broadcast_multiply_fusion
  7.8 0.4 collective-permute-done
  8.2 4.3 %collective-permute-done.1 = bf16[2,10,128,128]{3,2,0,1:T(8,128)(2,1)S(1)} collective-permute-done((bf16[2,10,128,128]{3,2,0,1:T(8,128)(2,1)S(1)}, bf16[2,10,128,128]{3,2,0,1:T(8,128)(2,1)S(1)}, u32[]{:S(2)}, u32[]{:S(2)}) %collective-permute-start.1) | collective-permute-done | bytes 655392 | tf_op jit(solution)/shard_map/ppermute | solution.py:17
  12.4 0.4 pad_maximum_fusion
  12.9 0.2 fusion.34
  13.1 0.3 fusion.211
  13.4 0.7 fusion.212
  14.2 1.0 fusion.210
  15.2 0.2 constant_dynamic-update-slice_fusion.8
  15.4 0.3 constant_dynamic-update-slice_fusion.13
  15.7 0.4 constant_dynamic-update-slice_fusion.18
  16.1 0.4 constant_dynamic-update-slice_fusion.22
  16.5 0.4 constant_dynamic-update-slice_fusion.21
  17.0 0.3 constant_dynamic-update-slice_fusion.20
  17.3 0.3 constant_dynamic-update-slice_fusion.19
  17.5 0.2 fusion.36
  17.7 0.4 fusion.3
  18.1 0.4 fusion.2
  18.6 0.4 fusion.19
  19.0 0.4 fusion.1
  19.4 0.4 fusion
  19.8 1.2 %multiply_reduce_fusion = (f32[]{:T(128)}, bf16[4,5,128,128]{3,2,0,1:T(8,128)(2,1)S(1)}) fusion(f32[4,5,128,128]{3,2,0,1:T(8,128)S(1)} %fusion, f32[5,128,128]{2,1,0:T(8,128)S(1)} %broadcast_multiply_fusion, f32[4,5]{0,1:T(8,128)S(1)} %copy.5), kind=kLoop, calls=%fused_computation.8 | loop fusion | flops 1966079 | bytes 2293844 | tf_op jit(solution)/shard_map/reduce_sum | solution.py:87
  20.9 0.9 fusion.214
  21.8 17.2 %collective-permute-start.2 = (bf16[2,5,128,128]{3,2,0,1:T(8,128)(2,1)}, bf16[2,5,128,128]{3,2,0,1:T(8,128)(2,1)}, u32[]{:S(2)}, u32[]{:S(2)}) collective-permute-start(bf16[2,5,128,128]{3,2,0,1:T(8,128)(2,1)} %get-tuple-element.51), channel_id=1, source_target_pairs={{0,1},{1,2},{2,3},{3,4},{4,5},{5,6},{6,7},{7,8},{8,9},{9,10},{10,1... | collective-permute-start | bytes 983048 | tf_op jit(solution)/shard_map/ppermute | solution.py:15
  39.0 1.3 %collective-permute-start.3 = (bf16[2,5,128,128]{3,2,0,1:T(8,128)(2,1)}, bf16[2,5,128,128]{3,2,0,1:T(8,128)(2,1)}, u32[]{:S(2)}, u32[]{:S(2)}) collective-permute-start(bf16[2,5,128,128]{3,2,0,1:T(8,128)(2,1)} %get-tuple-element.50), channel_id=1, source_target_pairs={{1,0},{2,1},{3,2},{4,3},{5,4},{6,5},{7,6},{8,7},{9,8},{10,9},{11,1... | collective-permute-start | bytes 983048 | tf_op jit(solution)/shard_map/ppermute | solution.py:17
  40.4 0.3 fusion.15
  40.7 0.3 fusion.14
  41.0 0.3 fusion.18
  41.3 0.3 fusion.13
  41.6 42.6 %psum.7 = f32[]{:T(128)} all-reduce(f32[]{:T(128)} %get-tuple-element.4), channel_id=1, replica_groups=mesh['grp'=4,'slab'=8] {'grp','slab'}, use_global_device_ids=true, to_apply=%region_1.2 | all-reduce | flops 1 | bytes 8 | tf_op jit(solution)/shard_map/psum | solution.py:88
  84.9 1.3 %fusion.12 = f32[4,5,128,128]{3,2,0,1:T(8,128)S(1)} fusion(f32[4,5,128,128]{3,2,0,1:T(8,128)S(1)} %fusion.13, bf16[4,5,128,128]{3,2,0,1:T(8,128)(2,1)S(1)} %get-tuple-element.5, bf16[4,1,128,128]{3,2,0,1:T(8,128)(2,1)} %get-tuple-element.11, bf16[4,1,128,128]{3,2,0,1:T(8,128)(2,1)} %get-tuple-element.6, bf16[4,1,128,128]{3,2,0,1:T(8,128)(2,1)} %get-tuple-element.40), kind=kOutput, calls=%fused_computation.39 | convolution fusion | flops 50724864 | bytes 1048576 | tf_op jit(solution)/shard_map/cbmk,cbkn->cmn/dot_general | solution.py:71
  86.2 0.9 fusion.213
  87.1 0.8 maximum_dynamic-update-slice_fusion.2
  87.9 0.8 maximum_dynamic-update-slice_fusion.1
  88.7 0.9 maximum_dynamic-update-slice_fusion
  89.5 1.2 %fusion.11 = f32[4,5,128,128]{3,2,0,1:T(8,128)S(1)} fusion(bf16[4,5,128,128]{3,2,0,1:T(8,128)(2,1)S(1)} %get-tuple-element.5, bf16[2,5,128,128]{3,2,0,1:T(8,128)(2,1)} %collective-permute-done.2, bf16[4,1,128,128]{3,2,0,1:T(8,128)(2,1)S(1)} %get-tuple-element.49), kind=kOutput, calls=%fused_computation.37 | convolution fusion | flops 53870592 | bytes 1769472 | tf_op jit(solution)/shard_map/cbmk,cbkn->cmn/dot_general | solution.py:71
  90.8 1.3 %fusion.10 = f32[4,5,128,128]{3,2,0,1:T(8,128)S(1)} fusion(f32[4,5,128,128]{3,2,0,1:T(8,128)S(1)} %fusion.11, bf16[2,5,128,128]{3,2,0,1:T(8,128)(2,1)} %collective-permute-done.3, bf16[4,5,128,128]{3,2,0,1:T(8,128)(2,1)S(1)} %get-tuple-element.5, bf16[2,5,128,128]{3,2,0,1:T(8,128)(2,1)} %collective-permute-done.2, ...), kind=kOutput, calls=%fused_computation.35 | convolution fusion | flops 72876032 | bytes 2228224 | tf_op jit(solution)/shard_map/cbmk,cbkn->cmn/dot_general | solution.py:71
  92.1 0.3 fusion.17
  92.4 1.3 %fusion.9 = f32[4,5,128,128]{3,2,0,1:T(8,128)S(1)} fusion(f32[4,5,128,128]{3,2,0,1:T(8,128)S(1)} %fusion.17, bf16[2,5,128,128]{3,2,0,1:T(8,128)(2,1)} %collective-permute-done.3, bf16[4,5,128,128]{3,2,0,1:T(8,128)(2,1)S(1)} %get-tuple-element.5, bf16[2,5,128,128]{3,2,0,1:T(8,128)(2,1)} %collective-permute-done.2, ...), kind=kOutput, calls=%fused_computation.33 | convolution fusion | flops 72876032 | bytes 2228224 | tf_op jit(solution)/shard_map/cbmk,cbkn->cmn/dot_general | solution.py:71
  93.7 1.3 %fusion.8 = f32[4,5,128,128]{3,2,0,1:T(8,128)S(1)} fusion(f32[4,5,128,128]{3,2,0,1:T(8,128)S(1)} %fusion.9, bf16[2,5,128,128]{3,2,0,1:T(8,128)(2,1)} %collective-permute-done.3, bf16[4,5,128,128]{3,2,0,1:T(8,128)(2,1)S(1)} %get-tuple-element.5, bf16[4,1,128,128]{3,2,0,1:T(8,128)(2,1)S(1)} %get-tuple-element.45), kind=kOutput, calls=%fused_computation.31 | convolution fusion | flops 53870592 | bytes 1769472 | tf_op jit(solution)/shard_map/cbmk,cbkn->cmn/dot_general | solution.py:71
  95.0 0.2 multiply_convert_fusion.1
  95.2 0.7 copy-done.3
  95.9 0.1 copy-done.5
  95.9 0.1 copy-done.12
  96.0 0.3 fusion.7
  96.3 0.6 copy-done.1
  96.9 0.1 copy-done.10
  97.0 0.3 fusion.6
  97.4 0.3 fusion.16
  97.7 0.5 copy-done.8
  98.2 0.1 copy-done.16
  98.3 0.1 copy-done.18
  98.4 0.3 fusion.5
  98.7 0.6 copy-done.6
  99.4 0.3 fusion.4
  99.7 0.4 multiply_convert_fusion
  100.0 0.9 copy.63
  (43 shorter events, 0.4 us)
Async XLA Ops:
  3.9 4.3 %collective-permute-start = (bf16[2,10,128,128]{3,2,0,1:T(8,128)(2,1)}, bf16[2,10,128,128]{3,2,0,1:T(8,128)(2,1)S(1)}, u32[]{:S(2)}, u32[]{:S(2)}) collective-permute-start(bf16[2,10,128,128]{3,2,0,1:T(8,128)(2,1)} %get-tuple-element.39), channel_id=1, source_target_pairs={{0,1},{1,2},{2,3},{3,4},{4,5},{5,6},{6,7},{7,8},{8,9},{9,10},{10,1... | collective-permute-start | bytes 1966088 | tf_op jit(solution)/shard_map/ppermute | solution.py:15
  6.3 6.1 %collective-permute-start.1 = (bf16[2,10,128,128]{3,2,0,1:T(8,128)(2,1)S(1)}, bf16[2,10,128,128]{3,2,0,1:T(8,128)(2,1)S(1)}, u32[]{:S(2)}, u32[]{:S(2)}) collective-permute-start(bf16[2,10,128,128]{3,2,0,1:T(8,128)(2,1)S(1)} %get-tuple-element.38), channel_id=1, source_target_pairs={{1,0},{2,1},{3,2},{4,3},{5,4},{6,5},{7,6},{8,7},{9,8},{10,9},{11,1... | collective-permute-start | bytes 1966088 | tf_op jit(solution)/shard_map/ppermute | solution.py:17
  13.4 27.0 %copy-start.2 = (bf16[4,1,128,128]{3,2,0,1:T(8,128)(2,1)}, bf16[4,1,128,128]{3,2,0,1:T(8,128)(2,1)S(1)}, u32[]{:S(2)}) copy-start(bf16[4,1,128,128]{3,2,0,1:T(8,128)(2,1)S(1)} %get-tuple-element.32) | copy-start | bytes 393220
  13.4 27.0 %copy-start.4 = (bf16[4,1,128,128]{3,2,0,1:T(8,128)(2,1)}, bf16[4,1,128,128]{3,2,0,1:T(8,128)(2,1)S(1)}, u32[]{:S(2)}) copy-start(bf16[4,1,128,128]{3,2,0,1:T(8,128)(2,1)S(1)} %get-tuple-element.33) | copy-start | bytes 393220
  13.4 27.3 %copy-start = (bf16[4,1,128,128]{3,2,0,1:T(8,128)(2,1)}, bf16[4,1,128,128]{3,2,0,1:T(8,128)(2,1)S(1)}, u32[]{:S(2)}) copy-start(bf16[4,1,128,128]{3,2,0,1:T(8,128)(2,1)S(1)} %get-tuple-element.23) | copy-start | bytes 393220
  14.2 26.2 %copy-start.11 = (bf16[4,1,128,128]{3,2,0,1:T(8,128)(2,1)}, bf16[4,1,128,128]{3,2,0,1:T(8,128)(2,1)S(1)}, u32[]{:S(2)}) copy-start(bf16[4,1,128,128]{3,2,0,1:T(8,128)(2,1)S(1)} %get-tuple-element.44) | copy-start | bytes 393220
  14.2 26.5 %copy-start.9 = (bf16[4,1,128,128]{3,2,0,1:T(8,128)(2,1)}, bf16[4,1,128,128]{3,2,0,1:T(8,128)(2,1)S(1)}, u32[]{:S(2)}) copy-start(bf16[4,1,128,128]{3,2,0,1:T(8,128)(2,1)S(1)} %get-tuple-element.43) | copy-start | bytes 393220
  14.2 27.1 %copy-start.7 = (bf16[4,1,128,128]{3,2,0,1:T(8,128)(2,1)}, bf16[4,1,128,128]{3,2,0,1:T(8,128)(2,1)S(1)}, u32[]{:S(2)}) copy-start(bf16[4,1,128,128]{3,2,0,1:T(8,128)(2,1)S(1)} %get-tuple-element.41) | copy-start | bytes 393220
  15.2 25.5 %copy-start.19 = (bf16[4,1,128,128]{3,2,0,1:T(8,128)(2,1)}, bf16[4,1,128,128]{3,2,0,1:T(8,128)(2,1)S(1)}, u32[]{:S(2)}) copy-start(bf16[4,1,128,128]{3,2,0,1:T(8,128)(2,1)S(1)} %get-tuple-element.10) | copy-start | bytes 393220
  15.2 26.1 %copy-start.15 = (bf16[4,1,128,128]{3,2,0,1:T(8,128)(2,1)}, bf16[4,1,128,128]{3,2,0,1:T(8,128)(2,1)S(1)}, u32[]{:S(2)}) copy-start(bf16[4,1,128,128]{3,2,0,1:T(8,128)(2,1)S(1)} %get-tuple-element.7) | copy-start | bytes 393220
  15.2 26.1 %copy-start.17 = (bf16[4,1,128,128]{3,2,0,1:T(8,128)(2,1)}, bf16[4,1,128,128]{3,2,0,1:T(8,128)(2,1)S(1)}, u32[]{:S(2)}) copy-start(bf16[4,1,128,128]{3,2,0,1:T(8,128)(2,1)S(1)} %get-tuple-element.8) | copy-start | bytes 393220
  21.8 64.4 %collective-permute-start.2 = (bf16[2,5,128,128]{3,2,0,1:T(8,128)(2,1)}, bf16[2,5,128,128]{3,2,0,1:T(8,128)(2,1)}, u32[]{:S(2)}, u32[]{:S(2)}) collective-permute-start(bf16[2,5,128,128]{3,2,0,1:T(8,128)(2,1)} %get-tuple-element.51), channel_id=1, source_target_pairs={{0,1},{1,2},{2,3},{3,4},{4,5},{5,6},{6,7},{7,8},{8,9},{9,10},{10,1... | collective-permute-start | bytes 983048 | tf_op jit(solution)/shard_map/ppermute | solution.py:15
  39.0 48.9 %collective-permute-start.3 = (bf16[2,5,128,128]{3,2,0,1:T(8,128)(2,1)}, bf16[2,5,128,128]{3,2,0,1:T(8,128)(2,1)}, u32[]{:S(2)}, u32[]{:S(2)}) collective-permute-start(bf16[2,5,128,128]{3,2,0,1:T(8,128)(2,1)} %get-tuple-element.50), channel_id=1, source_target_pairs={{1,0},{2,1},{3,2},{4,3},{5,4},{6,5},{7,6},{8,7},{9,8},{10,9},{11,1... | collective-permute-start | bytes 983048 | tf_op jit(solution)/shard_map/ppermute | solution.py:17
  95.0 0.9 copy-start.3
  95.0 1.0 copy-start.5
  95.0 1.0 copy-start.12
  96.0 0.9 copy-start.1
  96.0 1.0 copy-start.10
  96.0 1.0 %copy-start.20 = (bf16[4,1,128,128]{3,2,0,1:T(8,128)(2,1)S(1)}, bf16[4,1,128,128]{3,2,0,1:T(8,128)(2,1)}, u32[]{:S(2)}) copy-start(bf16[4,1,128,128]{3,2,0,1:T(8,128)(2,1)} %copy-done.19) | copy-start | bytes 393220
  97.3 0.9 copy-start.8
  97.3 1.0 copy-start.16
  97.3 1.0 copy-start.18
  98.4 0.9 copy-start.6
  98.4 1.0 copy-start.13
  98.4 1.0 %copy-start.14 = (bf16[4,1,128,128]{3,2,0,1:T(8,128)(2,1)S(1)}, bf16[4,1,128,128]{3,2,0,1:T(8,128)(2,1)}, u32[]{:S(2)}) copy-start(bf16[4,1,128,128]{3,2,0,1:T(8,128)(2,1)} %get-tuple-element.11) | copy-start | bytes 393220
where the time goes:
time: 103 us; the launch traced here: 102 us
  blocking collectives  42.6 us (41%)
  starting transfers between devices  22.2 us (22%)
  matrix products  13.9 us (13%)
  other arithmetic  8.69 us (8%)
  local copies, waits for them, and re-layouts  7.08 us (7%)
  waiting for transfers between devices  4.64 us (5%)
  between operations  2.95 us (3%)
    psum x1, blocking collectives, defect_measure(): squares_sum = lax.psum(partial_sum, ('grp', 'slab'))  42.6 us
    ppermute x2, starting transfers between devices, padded(): lax.ppermute(tail, axis, [(i, (i + 1) % count) for i in range(ends)])  19.6 us
    dot_general x29, matrix products, band_product(): jnp.einsum(einsum_form, left_stack, right_stack, preferred_element_type=j...  13.9 us
    ppermute x2, waiting for transfers between devices, padded(): lax.ppermute(head, axis, [((i + 1) % count, i) for i in range(ends)])  4.27 us
    unnamed x47, local copies, waits for them, and re-layouts  4.01 us
    ppermute x2, starting transfers between devices, padded(): lax.ppermute(head, axis, [((i + 1) % count, i) for i in range(ends)])  2.57 us
  transfers between devices with their start and end apart: 4, of which 2 were waited for; matrix products, arithmetic and copies ran while one was open for 4% of the time, Pallas kernels for 0%

commit v1 on v0

--- a/solution.py
+++ b/solution.py
@@ -85,7 +85,9 @@
 
 def defect_measure(defect, columns, block_size):
     partial_sum = jnp.sum(jnp.square(defect.astype(jnp.float32)))
-    squares_sum = lax.psum(partial_sum, ("grp", "slab"))
+    count = lax.axis_size("grp") * lax.axis_size("slab")
+    spread = jnp.broadcast_to(partial_sum, (count, 128))
+    squares_sum = jnp.sum(lax.all_to_all(spread, ("grp", "slab"), 0, 0, tiled=True)[:, 0])
     entries = columns * lax.axis_size("grp") * lax.axis_size("slab") * block_size
     return jnp.sqrt(squares_sum / entries)
 

time: 103 us -> 73.5 us (0.71)
  blocking collectives: 42.6 us -> 0 us
  starting transfers between devices: 22.2 us -> 27.5 us
  local copies, waits for them, and re-layouts: 7.08 us -> 10.5 us
  waiting for transfers between devices: 4.64 us -> 6.8 us
  other arithmetic: 8.69 us -> 10 us
    psum x1 -> x0, blocking collectives: 42.6 us -> none  [defect_measure(): squares_sum = lax.psum(partial_sum, ('grp', 'slab'))]
    all_to_all x0 -> x1, starting transfers between devices: none -> 5.37 us  [defect_measure(): lax.all_to_all(spread, ('grp', 'slab'), 0, 0, tiled=True)[:, 0]]
    all_to_all x0 -> x1, waiting for transfers between devices: none -> 2.16 us  [defect_measure(): lax.all_to_all(spread, ('grp', 'slab'), 0, 0, tiled=True)[:, 0]]
    unnamed x47 -> x41, local copies, waits for them, and re-layouts: 4.01 us -> 5.39 us
    reduce_sum x0 -> x1, other arithmetic: none -> 1.33 us  [defect_measure(): jnp.sum(lax.all_to_all(spread, ('grp', 'slab'), 0, 0, tiled=True)[:, 0])]
    broadcast_in_dim x0 -> x1, local copies, waits for them, and re-layouts: none -> 1.26 us  [defect_measure(): spread = jnp.broadcast_to(partial_sum, (count, 128))]
  transfers between devices with their start and end apart: 4 -> 5, of which waited for: 2 -> 3; matrix products, arithmetic and copies ran while one was open for 4% -> 11% of each run, Pallas kernels for 0% -> 0%
where the time goes in v1:
time: 73.5 us; the launch traced here: 72.7 us
  starting transfers between devices  27.5 us (37%)
  matrix products  14.9 us (20%)
  local copies, waits for them, and re-layouts  10.5 us (14%)
  other arithmetic  10 us (14%)
  waiting for transfers between devices  6.8 us (9%)
  between operations  2.88 us (4%)
    ppermute x2, starting transfers between devices, padded(): lax.ppermute(tail, axis, [(i, (i + 1) % count) for i in range(ends)])  19.6 us
    dot_general x29, matrix products, band_product(): jnp.einsum(einsum_form, left_stack, right_stack, preferred_element_type=j...  14.9 us
    unnamed x41, local copies, waits for them, and re-layouts  5.39 us
    all_to_all x1, starting transfers between devices, defect_measure(): lax.all_to_all(spread, ('grp', 'slab'), 0, 0, tiled=True)[:, 0]  5.37 us
    ppermute x2, waiting for transfers between devices, padded(): lax.ppermute(head, axis, [((i + 1) % count, i) for i in range(ends)])  4.27 us
    ppermute x2, starting transfers between devices, padded(): lax.ppermute(head, axis, [((i + 1) % count, i) for i in range(ends)])  2.57 us
    all_to_all x1, waiting for transfers between devices, defect_measure(): lax.all_to_all(spread, ('grp', 'slab'), 0, 0, tiled=True)[:, 0]  2.16 us
    slice x2, local copies, waits for them, and re-layouts, band_product(): left_ext[band_half + column_shift:band_half + column_shift + columns, lef...  1.92 us
  transfers between devices with their start and end apart: 5, of which 3 were waited for; matrix products, arithmetic and copies ran while one was open for 11% of the time, Pallas kernels for 0%

profile of v1, /device:TPU:0, one launch (start us, length us, event | category | flops | bytes accessed | tf_op | source)
XLA Modules:
  0.0 72.7 jit_solution(6882989062648699837)
XLA Ops:
  0.7 0.7 convert_element_type.44
  1.4 0.1 copy.124
  1.5 1.5 %copy_multiply_fusion = (bf16[4,5,128,128]{3,2,0,1:T(8,128)(2,1)S(1)}, bf16[4,5,128,128]{3,2,0,1:T(8,128)(2,1)S(1)}) fusion(bf16[4,5,128,128]{3,2,1,0:T(8,128)(2,1)} %param.3, bf16[4,5]{0,1:T(8,128)(2,1)S(1)} %copy.124, bf16[4,5]{0,1:T(8,128)(2,1)S(1)} %fusion.189, bf16[4,5,128,128]{3,2,1,0:T(8,128)(2,1)} %param.4), kind=kLoop, calls=%fused_computation.102 | loop fusion | flops 983040 | bytes 2621520 | tf_op jit(solution)/shard_map/mul | solution.py:113
  2.9 1.0 %pad_maximum_fusion.1 = (bf16[2,10,128,128]{3,2,0,1:T(8,128)(2,1)S(1)}, bf16[2,10,128,128]{3,2,0,1:T(8,128)(2,1)}) fusion(bf16[4,5,128,128]{3,2,0,1:T(8,128)(2,1)S(1)} %get-tuple-element.85, bf16[4,5,128,128]{3,2,0,1:T(8,128)(2,1)S(1)} %get-tuple-element.84), kind=kLoop, calls=%fused_computation.101 | loop fusion | flops 655360 | bytes 2621440 | tf_op jit(solution)/shard_map/concatenate | solution.py:118
  3.9 2.4 %collective-permute-start = (bf16[2,10,128,128]{3,2,0,1:T(8,128)(2,1)}, bf16[2,10,128,128]{3,2,0,1:T(8,128)(2,1)S(1)}, u32[]{:S(2)}, u32[]{:S(2)}) collective-permute-start(bf16[2,10,128,128]{3,2,0,1:T(8,128)(2,1)} %get-tuple-element.43), channel_id=1, source_target_pairs={{0,1},{1,2},{2,3},{3,4},{4,5},{5,6},{6,7},{7,8},{8,9},{9,10},{10,1... | collective-permute-start | bytes 1966088 | tf_op jit(solution)/shard_map/ppermute | solution.py:15
  6.3 1.3 %collective-permute-start.1 = (bf16[2,10,128,128]{3,2,0,1:T(8,128)(2,1)S(1)}, bf16[2,10,128,128]{3,2,0,1:T(8,128)(2,1)S(1)}, u32[]{:S(2)}, u32[]{:S(2)}) collective-permute-start(bf16[2,10,128,128]{3,2,0,1:T(8,128)(2,1)S(1)} %get-tuple-element.42), channel_id=1, source_target_pairs={{1,0},{2,1},{3,2},{4,3},{5,4},{6,5},{7,6},{8,7},{9,8},{10,9},{11,1... | collective-permute-start | bytes 1966088 | tf_op jit(solution)/shard_map/ppermute | solution.py:17
  7.6 0.1 copy.123
  7.7 0.1 broadcast_multiply_fusion
  7.8 0.4 collective-permute-done
  8.2 4.3 %collective-permute-done.1 = bf16[2,10,128,128]{3,2,0,1:T(8,128)(2,1)S(1)} collective-permute-done((bf16[2,10,128,128]{3,2,0,1:T(8,128)(2,1)S(1)}, bf16[2,10,128,128]{3,2,0,1:T(8,128)(2,1)S(1)}, u32[]{:S(2)}, u32[]{:S(2)}) %collective-permute-start.1) | collective-permute-done | bytes 655392 | tf_op jit(solution)/shard_map/ppermute | solution.py:17
  12.4 0.4 pad_maximum_fusion
  12.9 0.2 fusion.34
  13.1 0.9 %fusion.211 = (bf16[4,1,128,128]{3,2,0,1:T(8,128)(2,1)S(1)}, bf16[4,5,128,128]{3,2,0,1:T(8,128)(2,1)S(1)}, bf16[4,1,128,128]{3,2,0,1:T(8,128)(2,1)S(1)}, bf16[4,...) fusion(bf16[6,10,128,128]{3,2,0,1:T(8,128)(2,1)S(1)} %get-tuple, ...), kind=kLoop, calls=%fused_computation.302 | loop fusion | bytes 3670016 | tf_op jit(solution)/shard_map/slice | solution.py:61
  14.0 0.9 %fusion.212 = (bf16[4,1,128,128]{3,2,0,1:T(8,128)(2,1)}, bf16[4,1,128,128]{3,2,0,1:T(8,128)(2,1)}, bf16[4,5,128,128]{3,2,0,1:T(8,128)(2,1)S(1)}, bf16[4,1,128,12...) fusion(bf16[4,5,128,128]{3,2,0,1:T(8,128)(2,1)S(1)} %get-tuple-, ...), kind=kLoop, calls=%fused_computation.303 | loop fusion | bytes 2621440 | tf_op jit(solution)/shard_map/slice | solution.py:67
  14.9 1.0 %fusion.210 = (bf16[4,1,128,128]{3,2,0,1:T(8,128)(2,1)}, bf16[4,1,128,128]{3,2,0,1:T(8,128)(2,1)}, bf16[4,1,128,128]{3,2,0,1:T(8,128)(2,1)}, bf16[4,5,128,128]{3...) fusion(bf16[6,10,128,128]{3,2,0,1:T(8,128)(2,1)S(1)} %get-tuple, ...), kind=kLoop, calls=%fused_computation.301 | loop fusion | bytes 3670016 | tf_op jit(solution)/shard_map/slice | solution.py:61
  15.9 0.2 constant_dynamic-update-slice_fusion.8
  16.2 0.3 constant_dynamic-update-slice_fusion.13
  16.5 0.4 constant_dynamic-update-slice_fusion.18
  16.8 0.4 constant_dynamic-update-slice_fusion.22
  17.3 0.4 constant_dynamic-update-slice_fusion.21
  17.7 0.3 constant_dynamic-update-slice_fusion.20
  18.0 0.3 constant_dynamic-update-slice_fusion.19
  18.3 0.2 fusion.36
  18.5 0.4 fusion.3
  18.9 0.4 fusion.2
  19.3 0.4 fusion.19
  19.7 0.4 fusion.1
  20.1 0.4 fusion
  20.5 1.2 %multiply_reduce_fusion = (f32[]{:T(128)}, bf16[4,5,128,128]{3,2,0,1:T(8,128)(2,1)S(1)}) fusion(f32[4,5,128,128]{3,2,0,1:T(8,128)S(1)} %fusion, f32[5,128,128]{2,1,0:T(8,128)S(1)} %broadcast_multiply_fusion, f32[4,5]{0,1:T(8,128)S(1)} %copy.123), kind=kLoop, calls=%fused_computation.8 | loop fusion | flops 1966079 | bytes 2293844 | tf_op jit(solution)/shard_map/reduce_sum | solution.py:87
  21.7 0.9 %fusion.214 = (bf16[2,5,128,128]{3,2,0,1:T(8,128)(2,1)}, bf16[2,5,128,128]{3,2,0,1:T(8,128)(2,1)}) fusion(bf16[4,5,128,128]{3,2,0,1:T(8,128)(2,1)S(1)} %get-tuple-element.9), kind=kLoop, calls=%fused_computation.305 | loop fusion | bytes 1310720 | tf_op jit(solution)/shard_map/slice | solution.py:11
  22.5 17.2 %collective-permute-start.2 = (bf16[2,5,128,128]{3,2,0,1:T(8,128)(2,1)}, bf16[2,5,128,128]{3,2,0,1:T(8,128)(2,1)}, u32[]{:S(2)}, u32[]{:S(2)}) collective-permute-start(bf16[2,5,128,128]{3,2,0,1:T(8,128)(2,1)} %get-tuple-element.55), channel_id=1, source_target_pairs={{0,1},{1,2},{2,3},{3,4},{4,5},{5,6},{6,7},{7,8},{8,9},{9,10},{10,1... | collective-permute-start | bytes 983048 | tf_op jit(solution)/shard_map/ppermute | solution.py:15
  39.7 1.3 %collective-permute-start.3 = (bf16[2,5,128,128]{3,2,0,1:T(8,128)(2,1)}, bf16[2,5,128,128]{3,2,0,1:T(8,128)(2,1)}, u32[]{:S(2)}, u32[]{:S(2)}) collective-permute-start(bf16[2,5,128,128]{3,2,0,1:T(8,128)(2,1)} %get-tuple-element.54), channel_id=1, source_target_pairs={{1,0},{2,1},{3,2},{4,3},{5,4},{6,5},{7,6},{8,7},{9,8},{10,9},{11,1... | collective-permute-start | bytes 983048 | tf_op jit(solution)/shard_map/ppermute | solution.py:17
  41.0 1.3 %broadcast_in_dim.2 = f32[32,1,128]{2,1,0:T(1,128)} broadcast(f32[]{:T(128)} %get-tuple-element.8), dimensions={} | broadcast | bytes 16388 | tf_op jit(solution)/shard_map/broadcast_in_dim | solution.py:89
  42.3 5.4 %all-to-all-start = ((f32[32,1,128]{2,1,0:T(1,128)}), f32[32,1,128]{2,1,0:T(1,128)}, u32[]{:S(2)}, u32[]{:S(2)}) async-start(f32[32,1,128]{2,1,0:T(1,128)} %broadcast_in_dim.2), calls=%async_computation | async-start | bytes 32768 | tf_op jit(solution)/shard_map/all_to_all | solution.py:90
  47.7 1.3 %fusion.15 = f32[4,5,128,128]{3,2,0,1:T(8,128)S(1)} fusion(bf16[4,5,128,128]{3,2,0,1:T(8,128)(2,1)S(1)} %get-tuple-element.9, bf16[4,1,128,128]{3,2,0,1:T(8,128)(2,1)} %get-tuple-element.48, bf16[4,1,128,128]{3,2,0,1:T(8,128)(2,1)} %get-tuple-element.36, bf16[4,1,128,128]{3,2,0,1:T(8,128)(2,1)} %get-tuple-element.37), kind=kOutput, calls=%fused_computation.45 | convolution fusion | flops 50724864 | bytes 1048576 | tf_op jit(solution)/shard_map/cbmk,cbkn->cmn/dot_general | solution.py:71
  49.0 1.3 %fusion.14 = f32[4,5,128,128]{3,2,0,1:T(8,128)S(1)} fusion(f32[4,5,128,128]{3,2,0,1:T(8,128)S(1)} %fusion.15, bf16[4,5,128,128]{3,2,0,1:T(8,128)(2,1)S(1)} %get-tuple-element.9, bf16[4,1,128,128]{3,2,0,1:T(8,128)(2,1)} %get-tuple-element.14, bf16[4,1,128,128]{3,2,0,1:T(8,128)(2,1)} %get-tuple-element.47, ...), kind=kOutput, calls=%fused_computation.43 | convolution fusion | flops 67895296 | bytes 1310720 | tf_op jit(solution)/shard_map/cbmk,cbkn->cmn/dot_general | solution.py:71
  50.3 0.3 fusion.18
  50.7 0.5 copy-done.5
  51.3 0.3 fusion.13
  51.6 0.6 copy-done.3
  52.4 0.3 fusion.12
  52.6 2.2 %all-to-all-done = f32[32,1,128]{2,1,0:T(1,128)} async-done(((f32[32,1,128]{2,1,0:T(1,128)}), f32[32,1,128]{2,1,0:T(1,128)}, u32[]{:S(2)}, u32[]{:S(2)}) %all-to-all-start) | async-done | bytes 16416 | tf_op jit(solution)/shard_map/all_to_all | solution.py:90
  54.8 1.3 %slice_reduce_fusion = f32[]{:T(128)} fusion(f32[32,128]{1,0:T(8,128)} %bitcast.60), kind=kLoop, calls=%fused_computation.267 | loop fusion | flops 31 | bytes 132 | tf_op jit(solution)/shard_map/reduce_sum | solution.py:90
  56.8 0.9 %fusion.213 = (bf16[4,1,128,128]{3,2,0,1:T(8,128)(2,1)S(1)}, bf16[4,5,128,128]{3,2,0,1:T(8,128)(2,1)S(1)}, bf16[4,1,128,128]{3,2,0,1:T(8,128)(2,1)S(1)}, bf16[4,...) fusion(bf16[4,5,128,128]{3,2,0,1:T(8,128)(2,1)S(1)} %get-tuple-element.9, ...), kind=kLoop, calls=%fused_computation.304 | loop fusion | flops 262143 | bytes 2162688 | tf_op jit(solution)/shard_map/slice | solution.py:67
  57.7 0.8 %maximum_dynamic-update-slice_fusion.2 = bf16[4,5,128,128]{3,2,0,1:T(8,128)(2,1)S(1)} fusion(bf16[4,5,128,128]{3,2,0,1:T(8,128)(2,1)S(1)} %get-tuple-element.50, bf16[4,5,128,128]{3,2,0,1:T(8,128)(2,1)S(1)} %get-tuple-element.9, bf16[2,5,128,128]{3,2,0,1:T(8,128)(2,1)} %collective-permute-done.2), kind=kLoop, calls=%fused_computation.218 | loop fusion | flops 262144 | bytes 1114112
  58.5 0.8 %maximum_dynamic-update-slice_fusion.1 = bf16[4,5,128,128]{3,2,0,1:T(8,128)(2,1)S(1)} fusion(bf16[4,5,128,128]{3,2,0,1:T(8,128)(2,1)S(1)} %slice_dynamic-update-slice_fusion, bf16[2,5,128,128]{3,2,0,1:T(8,128)(2,1)} %collective-permute-done.3, bf16[4,5,128,128]{3,2,0,1:T(8,128)(2,1)S(1)} %get-tuple-element.9), kind=kLoop, calls=%fused_computation.216 | loop fusion | flops 262144 | bytes 1114112
  59.3 0.9 %maximum_dynamic-update-slice_fusion = bf16[4,5,128,128]{3,2,0,1:T(8,128)(2,1)S(1)} fusion(bf16[4,5,128,128]{3,2,0,1:T(8,128)(2,1)S(1)} %maximum_dynamic-update-slice_fusion.1, bf16[2,5,128,128]{3,2,0,1:T(8,128)(2,1)} %collective-permute-done.3, bf16[4,5,128,128]{3,2,0,1:T(8,128)(2,1)S(1)} %get-tuple-element.9), kind=kLoop, calls=%fused_computation.215 | loop fusion | flops 262144 | bytes 1114112 | tf_op jit(solution)/shard_map/stack | solution.py:59
  60.2 1.3 %fusion.11 = f32[4,5,128,128]{3,2,0,1:T(8,128)S(1)} fusion(bf16[4,5,128,128]{3,2,0,1:T(8,128)(2,1)S(1)} %get-tuple-element.9, bf16[2,5,128,128]{3,2,0,1:T(8,128)(2,1)} %collective-permute-done.2, bf16[4,1,128,128]{3,2,0,1:T(8,128)(2,1)S(1)} %get-tuple-element.53), kind=kOutput, calls=%fused_computation.37 | convolution fusion | flops 53870592 | bytes 1769472 | tf_op jit(solution)/shard_map/cbmk,cbkn->cmn/dot_general | solution.py:71
  61.4 1.3 %fusion.10 = f32[4,5,128,128]{3,2,0,1:T(8,128)S(1)} fusion(f32[4,5,128,128]{3,2,0,1:T(8,128)S(1)} %fusion.11, bf16[2,5,128,128]{3,2,0,1:T(8,128)(2,1)} %collective-permute-done.3, bf16[4,5,128,128]{3,2,0,1:T(8,128)(2,1)S(1)} %get-tuple-element.9, bf16[2,5,128,128]{3,2,0,1:T(8,128)(2,1)} %collective-permute-done.2, ...), kind=kOutput, calls=%fused_computation.35 | convolution fusion | flops 72876032 | bytes 2228224 | tf_op jit(solution)/shard_map/cbmk,cbkn->cmn/dot_general | solution.py:71
  62.7 0.3 fusion.17
  63.1 1.3 %fusion.9 = f32[4,5,128,128]{3,2,0,1:T(8,128)S(1)} fusion(f32[4,5,128,128]{3,2,0,1:T(8,128)S(1)} %fusion.17, bf16[2,5,128,128]{3,2,0,1:T(8,128)(2,1)} %collective-permute-done.3, bf16[4,5,128,128]{3,2,0,1:T(8,128)(2,1)S(1)} %get-tuple-element.9, bf16[2,5,128,128]{3,2,0,1:T(8,128)(2,1)} %collective-permute-done.2, ...), kind=kOutput, calls=%fused_computation.33 | convolution fusion | flops 72876032 | bytes 2228224 | tf_op jit(solution)/shard_map/cbmk,cbkn->cmn/dot_general | solution.py:71
  64.3 1.3 %fusion.8 = f32[4,5,128,128]{3,2,0,1:T(8,128)S(1)} fusion(f32[4,5,128,128]{3,2,0,1:T(8,128)S(1)} %fusion.9, bf16[2,5,128,128]{3,2,0,1:T(8,128)(2,1)} %collective-permute-done.3, bf16[4,5,128,128]{3,2,0,1:T(8,128)(2,1)S(1)} %get-tuple-element.9, bf16[4,1,128,128]{3,2,0,1:T(8,128)(2,1)S(1)} %get-tuple-element.49), kind=kOutput, calls=%fused_computation.31 | convolution fusion | flops 53870592 | bytes 1769472 | tf_op jit(solution)/shard_map/cbmk,cbkn->cmn/dot_general | solution.py:71
  65.6 0.2 multiply_convert_fusion.1
  65.8 0.7 copy-done.1
  66.6 0.3 fusion.7
  66.9 0.6 copy-done
  67.7 0.3 fusion.6
  68.0 0.3 fusion.16
  68.3 0.5 copy-done.6
  69.0 0.3 fusion.5
  69.3 0.6 copy-done.4
  70.0 0.3 fusion.4
  70.3 0.4 multiply_convert_fusion
  70.7 0.9 %copy.133 = bf16[4,5,128,128]{3,2,1,0:T(8,128)(2,1)} copy(bf16[4,5,128,128]{3,2,0,1:T(8,128)(2,1)S(1)} %multiply_convert_fusion) | data formatting | bytes 1310720
  (40 shorter events, 0.9 us)
Async XLA Ops:
  3.9 4.3 %collective-permute-start = (bf16[2,10,128,128]{3,2,0,1:T(8,128)(2,1)}, bf16[2,10,128,128]{3,2,0,1:T(8,128)(2,1)S(1)}, u32[]{:S(2)}, u32[]{:S(2)}) collective-permute-start(bf16[2,10,128,128]{3,2,0,1:T(8,128)(2,1)} %get-tuple-element.43), channel_id=1, source_target_pairs={{0,1},{1,2},{2,3},{3,4},{4,5},{5,6},{6,7},{7,8},{8,9},{9,10},{10,1... | collective-permute-start | bytes 1966088 | tf_op jit(solution)/shard_map/ppermute | solution.py:15
  6.3 6.1 %collective-permute-start.1 = (bf16[2,10,128,128]{3,2,0,1:T(8,128)(2,1)S(1)}, bf16[2,10,128,128]{3,2,0,1:T(8,128)(2,1)S(1)}, u32[]{:S(2)}, u32[]{:S(2)}) collective-permute-start(bf16[2,10,128,128]{3,2,0,1:T(8,128)(2,1)S(1)} %get-tuple-element.42), channel_id=1, source_target_pairs={{1,0},{2,1},{3,2},{4,3},{5,4},{6,5},{7,6},{8,7},{9,8},{10,9},{11,1... | collective-permute-start | bytes 1966088 | tf_op jit(solution)/shard_map/ppermute | solution.py:17
  22.5 34.3 %collective-permute-start.2 = (bf16[2,5,128,128]{3,2,0,1:T(8,128)(2,1)}, bf16[2,5,128,128]{3,2,0,1:T(8,128)(2,1)}, u32[]{:S(2)}, u32[]{:S(2)}) collective-permute-start(bf16[2,5,128,128]{3,2,0,1:T(8,128)(2,1)} %get-tuple-element.55), channel_id=1, source_target_pairs={{0,1},{1,2},{2,3},{3,4},{4,5},{5,6},{6,7},{7,8},{8,9},{9,10},{10,1... | collective-permute-start | bytes 983048 | tf_op jit(solution)/shard_map/ppermute | solution.py:15
  39.7 18.8 %collective-permute-start.3 = (bf16[2,5,128,128]{3,2,0,1:T(8,128)(2,1)}, bf16[2,5,128,128]{3,2,0,1:T(8,128)(2,1)}, u32[]{:S(2)}, u32[]{:S(2)}) collective-permute-start(bf16[2,5,128,128]{3,2,0,1:T(8,128)(2,1)} %get-tuple-element.54), channel_id=1, source_target_pairs={{1,0},{2,1},{3,2},{4,3},{5,4},{6,5},{7,6},{8,7},{9,8},{10,9},{11,1... | collective-permute-start | bytes 983048 | tf_op jit(solution)/shard_map/ppermute | solution.py:17
  42.3 12.5 %all-to-all-start = ((f32[32,1,128]{2,1,0:T(1,128)}), f32[32,1,128]{2,1,0:T(1,128)}, u32[]{:S(2)}, u32[]{:S(2)}) async-start(f32[32,1,128]{2,1,0:T(1,128)} %broadcast_in_dim.2), calls=%async_computation | async-start | bytes 32768 | tf_op jit(solution)/shard_map/all_to_all | solution.py:90
  50.3 0.9 %copy-start.5 = (bf16[4,1,128,128]{3,2,0,1:T(8,128)(2,1)S(1)}, bf16[4,1,128,128]{3,2,0,1:T(8,128)(2,1)}, u32[]{:S(2)}) copy-start(bf16[4,1,128,128]{3,2,0,1:T(8,128)(2,1)} %get-tuple-element.45) | copy-start | bytes 393220
  50.3 1.0 %copy-start.13 = (bf16[4,1,128,128]{3,2,0,1:T(8,128)(2,1)S(1)}, bf16[4,1,128,128]{3,2,0,1:T(8,128)(2,1)}, u32[]{:S(2)}) copy-start(bf16[4,1,128,128]{3,2,0,1:T(8,128)(2,1)} %get-tuple-element.11) | copy-start | bytes 393220
  50.3 1.0 %copy-start.15 = (bf16[4,1,128,128]{3,2,0,1:T(8,128)(2,1)S(1)}, bf16[4,1,128,128]{3,2,0,1:T(8,128)(2,1)}, u32[]{:S(2)}) copy-start(bf16[4,1,128,128]{3,2,0,1:T(8,128)(2,1)} %get-tuple-element.12) | copy-start | bytes 393220
  51.3 0.9 %copy-start.3 = (bf16[4,1,128,128]{3,2,0,1:T(8,128)(2,1)S(1)}, bf16[4,1,128,128]{3,2,0,1:T(8,128)(2,1)}, u32[]{:S(2)}) copy-start(bf16[4,1,128,128]{3,2,0,1:T(8,128)(2,1)} %get-tuple-element.44) | copy-start | bytes 393220
  51.3 1.0 %copy-start.9 = (bf16[4,1,128,128]{3,2,0,1:T(8,128)(2,1)S(1)}, bf16[4,1,128,128]{3,2,0,1:T(8,128)(2,1)}, u32[]{:S(2)}) copy-start(bf16[4,1,128,128]{3,2,0,1:T(8,128)(2,1)} %get-tuple-element.10) | copy-start | bytes 393220
  51.3 1.0 %copy-start.11 = (bf16[4,1,128,128]{3,2,0,1:T(8,128)(2,1)S(1)}, bf16[4,1,128,128]{3,2,0,1:T(8,128)(2,1)}, u32[]{:S(2)}) copy-start(bf16[4,1,128,128]{3,2,0,1:T(8,128)(2,1)} %get-tuple-element.15) | copy-start | bytes 393220
  65.6 0.9 %copy-start.1 = (bf16[4,1,128,128]{3,2,0,1:T(8,128)(2,1)S(1)}, bf16[4,1,128,128]{3,2,0,1:T(8,128)(2,1)}, u32[]{:S(2)}) copy-start(bf16[4,1,128,128]{3,2,0,1:T(8,128)(2,1)} %get-tuple-element.36) | copy-start | bytes 393220
  65.6 1.0 %copy-start.2 = (bf16[4,1,128,128]{3,2,0,1:T(8,128)(2,1)S(1)}, bf16[4,1,128,128]{3,2,0,1:T(8,128)(2,1)}, u32[]{:S(2)}) copy-start(bf16[4,1,128,128]{3,2,0,1:T(8,128)(2,1)} %get-tuple-element.37) | copy-start | bytes 393220
  65.6 1.0 %copy-start.8 = (bf16[4,1,128,128]{3,2,0,1:T(8,128)(2,1)S(1)}, bf16[4,1,128,128]{3,2,0,1:T(8,128)(2,1)}, u32[]{:S(2)}) copy-start(bf16[4,1,128,128]{3,2,0,1:T(8,128)(2,1)} %get-tuple-element.48) | copy-start | bytes 393220
  66.6 0.9 %copy-start = (bf16[4,1,128,128]{3,2,0,1:T(8,128)(2,1)S(1)}, bf16[4,1,128,128]{3,2,0,1:T(8,128)(2,1)}, u32[]{:S(2)}) copy-start(bf16[4,1,128,128]{3,2,0,1:T(8,128)(2,1)} %get-tuple-element.27) | copy-start | bytes 393220
  66.6 1.0 %copy-start.7 = (bf16[4,1,128,128]{3,2,0,1:T(8,128)(2,1)S(1)}, bf16[4,1,128,128]{3,2,0,1:T(8,128)(2,1)}, u32[]{:S(2)}) copy-start(bf16[4,1,128,128]{3,2,0,1:T(8,128)(2,1)} %get-tuple-element.47) | copy-start | bytes 393220
  66.6 1.0 %copy-start.17 = (bf16[4,1,128,128]{3,2,0,1:T(8,128)(2,1)S(1)}, bf16[4,1,128,128]{3,2,0,1:T(8,128)(2,1)}, u32[]{:S(2)}) copy-start(bf16[4,1,128,128]{3,2,0,1:T(8,128)(2,1)} %get-tuple-element.14) | copy-start | bytes 393220
  68.0 0.9 %copy-start.6 = (bf16[4,1,128,128]{3,2,0,1:T(8,128)(2,1)S(1)}, bf16[4,1,128,128]{3,2,0,1:T(8,128)(2,1)}, u32[]{:S(2)}) copy-start(bf16[4,1,128,128]{3,2,0,1:T(8,128)(2,1)} %get-tuple-element.45) | copy-start | bytes 393220
  68.0 1.0 %copy-start.14 = (bf16[4,1,128,128]{3,2,0,1:T(8,128)(2,1)S(1)}, bf16[4,1,128,128]{3,2,0,1:T(8,128)(2,1)}, u32[]{:S(2)}) copy-start(bf16[4,1,128,128]{3,2,0,1:T(8,128)(2,1)} %get-tuple-element.11) | copy-start | bytes 393220
  68.0 1.0 %copy-start.16 = (bf16[4,1,128,128]{3,2,0,1:T(8,128)(2,1)S(1)}, bf16[4,1,128,128]{3,2,0,1:T(8,128)(2,1)}, u32[]{:S(2)}) copy-start(bf16[4,1,128,128]{3,2,0,1:T(8,128)(2,1)} %get-tuple-element.12) | copy-start | bytes 393220
  69.0 0.9 %copy-start.4 = (bf16[4,1,128,128]{3,2,0,1:T(8,128)(2,1)S(1)}, bf16[4,1,128,128]{3,2,0,1:T(8,128)(2,1)}, u32[]{:S(2)}) copy-start(bf16[4,1,128,128]{3,2,0,1:T(8,128)(2,1)} %get-tuple-element.44) | copy-start | bytes 393220
  69.0 1.0 %copy-start.10 = (bf16[4,1,128,128]{3,2,0,1:T(8,128)(2,1)S(1)}, bf16[4,1,128,128]{3,2,0,1:T(8,128)(2,1)}, u32[]{:S(2)}) copy-start(bf16[4,1,128,128]{3,2,0,1:T(8,128)(2,1)} %get-tuple-element.10) | copy-start | bytes 393220
  69.0 1.0 %copy-start.12 = (bf16[4,1,128,128]{3,2,0,1:T(8,128)(2,1)S(1)}, bf16[4,1,128,128]{3,2,0,1:T(8,128)(2,1)}, u32[]{:S(2)}) copy-start(bf16[4,1,128,128]{3,2,0,1:T(8,128)(2,1)} %get-tuple-element.15) | copy-start | bytes 393220

commit v2 on v0

v2 whole, which is shorter than its diff:
```python
import functools

import jax
import jax.numpy as jnp
from jax import lax
from jax.experimental import pallas as pl
from jax.experimental.pallas import tpu as pltpu
from jax.sharding import PartitionSpec as P

AXES = ("grp", "slab")
ANY = pl.BlockSpec(memory_space=pl.ANY)
VMEM = pl.BlockSpec(memory_space=pltpu.VMEM)
SMEM = pl.BlockSpec(memory_space=pltpu.SMEM)
VMEM_LIMIT = 40 * 1024 * 1024


def place():
    slab = lax.axis_index("slab")
    return lax.axis_index("grp"), slab, lax.rem(slab, 2)


def keep(flag, block):
    return jnp.where(flag, block, jnp.zeros_like(block))


def in_quarter(row, quarter_len):
    return jnp.logical_and(row >= 0, row < quarter_len)


def factor_present(pattern, slab, columns, quarter_len, column, offset, band_half):
    row = slab * columns + column + offset - band_half
    return jnp.logical_and(pattern[column, offset] != 0, in_quarter(row, quarter_len))


def pack_kernel(quarter_len, margin, factor, pattern, near, far, cross, cells, sems):
    columns, offsets = margin.shape[0], margin.shape[1]
    band_half = (offsets - 1) // 2
    _, slab, odd = place()
    last = columns - band_half
    near_first = jnp.where(odd == 1, 0, last)
    far_first = last - near_first
    starts = (near_first, far_first)
    loads = []
    for side, first in enumerate(starts):
        for kind, source in enumerate((margin, factor)):
            copy = pltpu.make_async_copy(
                source.at[pl.ds(first, band_half)], cells.at[side, kind], sems.at[side, kind]
            )
            copy.start()
            loads.append(copy)
    for side in (1, 0):
        for kind in range(2):
            loads[2 * side + kind].wait()
            for t in range(band_half):
                for o in range(offsets):
                    column = starts[side] + t
                    if kind == 0:
                        flag = pattern[column, o] != 0
                    else:
                        flag = factor_present(
                            pattern, slab, columns, quarter_len, column, o, band_half
                        )
                    block = keep(flag, cells[side, kind, t, o])
                    (near, far)[side][kind, t, o] = block
                    u = t + o - band_half
                    if side == 1 and kind == 1 and 0 <= u < band_half:
                        cross[t, u] = block


def pack(margin, factor, pattern, quarter_len):
    columns, offsets, block, _ = margin.shape
    band_half = (offsets - 1) // 2
    message = jax.ShapeDtypeStruct((2, band_half, offsets, block, block), margin.dtype)
    return pl.pallas_call(
        functools.partial(pack_kernel, quarter_len),
        out_shape=(
            message,
            message,
            jax.ShapeDtypeStruct((band_half, band_half, block, block), margin.dtype),
        ),
        in_specs=[ANY, ANY, SMEM],
        out_specs=(VMEM, VMEM, VMEM),
        scratch_shapes=[
            pltpu.VMEM((2,) + message.shape, margin.dtype),
            pltpu.SemaphoreType.DMA((2, 2)),
        ],
        compiler_params=pltpu.CompilerParams(vmem_limit_bytes=VMEM_LIMIT),
        name="pack",
    )(margin, factor, pattern)


def spread_column(dense, first_row, first_lane, block, band_half, offsets, read):
    zeros = jnp.zeros((block, block), dense.dtype)
    for t in range(band_half):
        for a in range(3 * band_half):
            o = a - t
            value = read(t, o) if 0 <= o < offsets else zeros
            dense[
                first_row + a * block : first_row + (a + 1) * block,
                first_lane + t * block : first_lane + (t + 1) * block,
            ] = value


def defect_kernel(
    quarter_len,
    margin,
    factor,
    pattern,
    near,
    far,
    cross,
    defect,
    near_out,
    far_out,
    spread,
    own,
    halo,
    crossed,
    s_dense,
    z_dense,
    z_turned,
    image,
    sems,
):
    columns, offsets, block, _ = margin.shape
    band_half = (offsets - 1) // 2
    tile = band_half * block
    count = columns // band_half
    _, slab, odd = place()
    near_side = 1 - odd
    far_side = odd
    copies = [
        pltpu.make_async_copy(margin, own.at[0], sems.at[0]),
        pltpu.make_async_copy(factor, own.at[1], sems.at[1]),
        pltpu.make_async_copy(near, halo.at[near_side], sems.at[2]),
        pltpu.make_async_copy(far, halo.at[far_side], sems.at[3]),
        pltpu.make_async_copy(cross, crossed, sems.at[4]),
    ]
    for copy in copies:
        copy.start()
    copies[0].wait()
    copies[1].wait()

    def spot(pair):
        return (pair + 1) * tile

    def own_margin(c, t, o):
        column = c * band_half + t
        return keep(pattern[column, o] != 0, own[0, column, o])

    def own_factor(c, t, o):
        column = c * band_half + t
        flag = factor_present(pattern, slab, columns, quarter_len, column, o, band_half)
        return keep(flag, own[1, column, o])

    def turn(pair):
        for r in (pair - 1, pair, pair + 1):
            cell = z_dense[(r + 2) * tile : (r + 3) * tile, spot(pair) : spot(pair) + tile]
            z_turned[spot(pair) : spot(pair) + tile, (r + 2) * tile : (r + 3) * tile] = cell.T

    for c in range(count):
        for dense, read in ((s_dense, own_margin), (z_dense, own_factor)):
            spread_column(
                dense, spot(c), spot(c), block, band_half, offsets, functools.partial(read, c)
            )
        turn(c)
    for copy in copies[2:]:
        copy.wait()
    for t in range(band_half):
        for u in range(band_half):
            o = u - t + band_half
            halo[far_side, 1, t, o] = halo[far_side, 1, t, o] + crossed[t, u]
    for side, pair in ((0, -1), (1, count)):
        for kind, dense in ((0, s_dense), (1, z_dense)):
            spread_column(
                dense,
                spot(pair),
                spot(pair),
                block,
                band_half,
                offsets,
                lambda t, o: halo[side, kind, t, o],
            )
        turn(pair)

    eye = (
        lax.broadcasted_iota(jnp.int32, (block, block), 0)
        == lax.broadcasted_iota(jnp.int32, (block, block), 1)
    ).astype(jnp.float32)
    squares = jnp.zeros((8, block), jnp.float32)
    for c in range(count):
        for r in range(c - 2, c + 3):
            low, high = max(r - 1, c - 1), min(r + 1, c + 1) + 1
            image[c, (r - c + 2) * tile : (r - c + 3) * tile] = jnp.dot(
                s_dense[(r + 2) * tile : (r + 3) * tile, spot(low) : spot(high)],
                z_dense[(low + 2) * tile : (high + 2) * tile, spot(c) : spot(c) + tile],
                preferred_element_type=jnp.float32,
            ).astype(image.dtype)
        for i in range(c - 1, c + 2):
            product = jnp.dot(
                z_turned[spot(i) : spot(i) + tile, (i + 1) * tile : (i + 4) * tile],
                image[c, (i - c + 1) * tile : (i - c + 4) * tile],
                preferred_element_type=jnp.float32,
            )
            for u in range(band_half):
                for t in range(band_half):
                    o = (i - c) * band_half + u - t + band_half
                    rows = slice((i - c + 1) * tile + u * block, (i - c + 1) * tile + (u + 1) * block)
                    lanes = slice(t * block, (t + 1) * block)
                    if not 0 <= o < offsets:
                        defect[c, rows, lanes] = jnp.zeros((block, block), defect.dtype)
                        continue
                    value = -product[u * block : (u + 1) * block, lanes]
                    if o == band_half:
                        value = eye + value
                    value = keep(pattern[c * band_half + t, o] != 0, value).astype(defect.dtype)
                    defect[c, rows, lanes] = value
                    wide = value.astype(jnp.float32)
                    squares = squares + jnp.sum((wide * wide).reshape(-1, 8, block), axis=0)
    spread[...] = jnp.broadcast_to(jnp.sum(squares, axis=0, keepdims=True)[None], spread.shape)

    @pl.when(odd == 1)
    def _():
        near_out[...] = defect[0, : 2 * tile]
        far_out[...] = defect[count - 1, tile:]

    @pl.when(odd == 0)
    def _():
        near_out[...] = defect[count - 1, tile:]
        far_out[...] = defect[0, : 2 * tile]


def defect_step(margin, factor, pattern, near, far, cross, quarter_len, devices):
    columns, offsets, block, _ = margin.shape
    band_half = (offsets - 1) // 2
    tile = band_half * block
    count = columns // band_half
    kind = margin.dtype
    message = jax.ShapeDtypeStruct((2 * tile, tile), kind)
    products = count * 18
    return pl.pallas_call(
        functools.partial(defect_kernel, quarter_len),
        out_shape=(
            jax.ShapeDtypeStruct((count, 3 * tile, tile), kind),
            message,
            message,
            jax.ShapeDtypeStruct((devices, 1, block), jnp.float32),
        ),
        in_specs=[ANY, ANY, SMEM, ANY, ANY, ANY],
        out_specs=(VMEM, VMEM, VMEM, VMEM),
        scratch_shapes=[
            pltpu.VMEM((2,) + margin.shape, kind),
            pltpu.VMEM((2,) + near.shape, kind),
            pltpu.VMEM(cross.shape, kind),
            pltpu.VMEM(((count + 4) * tile, (count + 2) * tile), kind),
            pltpu.VMEM(((count + 4) * tile, (count + 2) * tile), kind),
            pltpu.VMEM(((count + 2) * tile, (count + 4) * tile), kind),
            pltpu.VMEM((count, 5 * tile, tile), kind),
            pltpu.SemaphoreType.DMA((5,)),
        ],
        compiler_params=pltpu.CompilerParams(vmem_limit_bytes=VMEM_LIMIT),
        cost_estimate=pl.CostEstimate(
            flops=products * 2 * tile**3, bytes_accessed=4 * 2**20, transcendentals=0
        ),
        name="defect",
    )(margin, factor, pattern, near, far, cross)


def refine_kernel(
    quarter_len,
    entries,
    factor,
    pattern,
    near,
    far,
    cross,
    defect,
    near_defect,
    far_defect,
    gathered,
    refined,
    norm,
    own,
    halo,
    crossed,
    z_dense,
    d_dense,
    square,
    sems,
):
    columns, offsets, block, _ = factor.shape
    band_half = (offsets - 1) // 2
    tile = band_half * block
    count = columns // band_half
    _, slab, odd = place()
    near_side = 1 - odd
    far_side = odd
    edge = count * tile
    near_row = pl.multiple_of(near_side * edge, tile)
    near_lane = pl.multiple_of(near_side * (edge + tile), tile)
    far_row = pl.multiple_of(far_side * edge, tile)
    far_lane = pl.multiple_of(far_side * (edge + tile), tile)
    copies = [
        pltpu.make_async_copy(factor, own, sems.at[0]),
        pltpu.make_async_copy(near.at[1], halo.at[near_side], sems.at[1]),
        pltpu.make_async_copy(far.at[1], halo.at[far_side], sems.at[2]),
        pltpu.make_async_copy(cross, crossed, sems.at[3]),
        pltpu.make_async_copy(
            near_defect,
            d_dense.at[pl.ds(near_row, 2 * tile), pl.ds(near_lane, tile)],
            sems.at[4],
        ),
        pltpu.make_async_copy(
            far_defect, d_dense.at[pl.ds(far_row, 2 * tile), pl.ds(far_lane, tile)], sems.at[5]
        ),
    ]
    for c in range(count):
        copies.append(
            pltpu.make_async_copy(
                defect.at[c],
                d_dense.at[c * tile : (c + 3) * tile, (c + 1) * tile : (c + 2) * tile],
                sems.at[6 + c],
            )
        )
    for copy in copies:
        copy.start()
    total = jnp.sum(gathered[...]) * (1.0 / entries)
    norm[...] = jnp.sqrt(jnp.full(norm.shape, total, jnp.float32))

    def own_factor(c, t, o):
        column = c * band_half + t
        flag = factor_present(pattern, slab, columns, quarter_len, column, o, band_half)
        return keep(flag, own[column, o])

    copies[0].wait()
    for c in range(count):
        spread_column(
            z_dense,
            (c + 1) * tile,
            (c + 1) * tile,
            block,
            band_half,
            offsets,
            functools.partial(own_factor, c),
        )
    for copy in copies[1:4]:
        copy.wait()
    for t in range(band_half):
        for u in range(band_half):
            o = u - t + band_half
            halo[far_side, t, o] = halo[far_side, t, o] + crossed[t, u]
    for side, pair in ((0, -1), (1, count)):
        spread_column(
            z_dense,
            (pair + 1) * tile,
            (pair + 1) * tile,
            block,
            band_half,
            offsets,
            lambda t, o: halo[side, t, o],
        )
    for copy in copies[4:]:
        copy.wait()

    for c in range(count):
        lanes_c = slice((c + 1) * tile, (c + 2) * tile)
        for i in range(c - 1, c + 2):
            low, high = max(i, c) - 1, min(i, c) + 2
            product = jnp.dot(
                d_dense[(i + 1) * tile : (i + 2) * tile, (low + 1) * tile : (high + 1) * tile],
                d_dense[(low + 1) * tile : (high + 1) * tile, lanes_c],
                preferred_element_type=jnp.float32,
            )
            for u in range(band_half):
                for t in range(band_half):
                    o = (i - c) * band_half + u - t + band_half
                    rows = slice((i - c + 1) * tile + u * block, (i - c + 1) * tile + (u + 1) * block)
                    lanes = slice(t * block, (t + 1) * block)
                    if not 0 <= o < offsets:
                        square[c, rows, lanes] = jnp.zeros((block, block), square.dtype)
                        continue
                    value = product[u * block : (u + 1) * block, lanes]
                    square[c, rows, lanes] = keep(
                        pattern[c * band_half + t, o] != 0, value
                    ).astype(square.dtype)
        for i in range(c - 1, c + 2):
            low, high = max(i, c) - 1, min(i, c) + 2
            left = z_dense[(i + 2) * tile : (i + 3) * tile, (low + 1) * tile : (high + 1) * tile]
            first = jnp.dot(
                left,
                d_dense[(low + 1) * tile : (high + 1) * tile, lanes_c],
                preferred_element_type=jnp.float32,
            )
            second = jnp.dot(
                left,
                square[c, (low - c + 1) * tile : (high - c + 1) * tile],
                preferred_element_type=jnp.float32,
            )
            for u in range(band_half):
                for t in range(band_half):
                    o = (i - c) * band_half + u - t + band_half
                    if not 0 <= o < offsets:
                        continue
                    part = (slice(u * block, (u + 1) * block), slice(t * block, (t + 1) * block))
                    base = z_dense[
                        (i + 2) * tile + u * block : (i + 2) * tile + (u + 1) * block,
                        (c + 1) * tile + t * block : (c + 1) * tile + (t + 1) * block,
                    ].astype(jnp.float32)
                    value = base + 0.5 * first[part] + 0.375 * second[part]
                    column = c * band_half + t
                    refined[column, o] = keep(pattern[column, o] != 0, value).astype(refined.dtype)


def refine_step(
    factor, pattern, near, far, cross, defect, near_defect, far_defect, gathered, quarter_len, entries
):
    columns, offsets, block, _ = factor.shape
    band_half = (offsets - 1) // 2
    tile = band_half * block
    count = columns // band_half
    kind = factor.dtype
    products = count * 21
    return pl.pallas_call(
        functools.partial(refine_kernel, quarter_len, entries),
        out_shape=(
            jax.ShapeDtypeStruct(factor.shape, kind),
            jax.ShapeDtypeStruct((1, block), jnp.float32),
        ),
        in_specs=[ANY, SMEM, ANY, ANY, ANY, ANY, ANY, ANY, VMEM],
        out_specs=(VMEM, VMEM),
        scratch_shapes=[
            pltpu.VMEM(factor.shape, kind),
            pltpu.VMEM((2,) + near.shape[1:], kind),
            pltpu.VMEM(cross.shape, kind),
            pltpu.VMEM(((count + 4) * tile, (count + 2) * tile), kind),
            pltpu.VMEM(((count + 2) * tile, (count + 2) * tile), kind),
            pltpu.VMEM((count, 3 * tile, tile), kind),
            pltpu.SemaphoreType.DMA((6 + count,)),
        ],
        compiler_params=pltpu.CompilerParams(vmem_limit_bytes=VMEM_LIMIT),
        cost_estimate=pl.CostEstimate(
            flops=products * 2 * tile**3, bytes_accessed=4 * 2**20, transcendentals=0
        ),
        name="refine",
    )(factor, pattern, near, far, cross, defect, near_defect, far_defect, gathered)


def swaps(pairs):
    return [pair for i, j in pairs for pair in ((i, j), (j, i))]


def per_device(margin, factor, pattern):
    columns, offsets, block, _ = margin.shape
    slabs = lax.axis_size("slab")
    devices = lax.axis_size("grp") * slabs
    quarter_len = columns * slabs
    near_pairs = [(i, i + 1) for i in range(0, devices - 1, 2)]
    far_pairs = [(i, i + 1) for i in range(1, devices - 1, 2)]
    inner_pairs = [(i, j) for i, j in far_pairs if j % slabs]
    cross_pairs = [(i, j) for i, j in far_pairs if not j % slabs]
    near, far, cross = pack(margin, factor, pattern, quarter_len)
    far = lax.ppermute(far, AXES, swaps(inner_pairs))
    cross = lax.ppermute(cross, AXES, swaps(cross_pairs))
    near = lax.ppermute(near, AXES, swaps(near_pairs))
    defect, near_defect, far_defect, spread = defect_step(
        margin, factor, pattern, near, far, cross, quarter_len, devices
    )
    far_defect = lax.ppermute(far_defect, AXES, swaps(far_pairs))
    near_defect = lax.ppermute(near_defect, AXES, swaps(near_pairs))
    gathered = lax.all_to_all(spread, AXES, 0, 0, tiled=True)
    refined, norm = refine_step(
        factor,
        pattern,
        near,
        far,
        cross,
        defect,
        near_defect,
        far_defect,
        gathered,
        quarter_len,
        columns * devices * block,
    )
    return refined, norm[0, 0]


def solution(mesh):
    return jax.shard_map(
        per_device,
        mesh=mesh,
        in_specs=(
            P(AXES, None, None, None),
            P(AXES, None, None, None),
            P(AXES, None),
        ),
        out_specs=(P(AXES, None, None, None), P()),
        check_vma=False,
    )
```

time: 103 us -> 44 us (0.43)
  blocking collectives: 42.6 us -> 14.7 us
  matrix products: 13.9 us -> 0 us
  Pallas kernels: 0 us -> 9.9 us
  other arithmetic: 8.69 us -> 0 us
  starting transfers between devices: 22.2 us -> 15.3 us
  waiting for transfers between devices: 4.64 us -> 0.21 us
  local copies, waits for them, and re-layouts: 7.08 us -> 2.86 us
  between operations: 2.95 us -> 0.72 us
    psum x1 -> x0, blocking collectives: 42.6 us -> none  [defect_measure(): squares_sum = lax.psum(partial_sum, ('grp', 'slab'))]
    all_to_all x0 -> x1, blocking collectives: none -> 14.7 us  [per_device(): gathered = lax.all_to_all(spread, AXES, 0, 0, tiled=True)]
    dot_general x29 -> x0, matrix products: 13.9 us -> none  [band_product(): jnp.einsum(einsum_form, left_stack, right_stack, preferred_element_type=j...]
    pallas_call x0 -> x3, Pallas kernels: none -> 9.9 us  [the longest x1 4.59 us: refine_step(): pl.pallas_call(functools.partial(refine_kernel, quarter_len, entries), ou...]
    ppermute x4 -> x5, starting transfers between devices: 22.2 us -> 15.3 us  [the longest x1 12.6 us: per_device(): near_defect = lax.ppermute(near_defect, AXES, swaps(near_pairs))]
    ppermute x4 -> x5, waiting for transfers between devices: 4.64 us -> 0.21 us  [the longest x1 0.19 us: per_device(): near = lax.ppermute(near, AXES, swaps(near_pairs))]
    slice x4 -> x0, local copies, waits for them, and re-layouts: 2.86 us -> none  [the longest x2 1.23 us: band_product(): left_ext[band_half + column_shift:band_half + column_shift + columns, lef...]
    mul x2 -> x0, other arithmetic: 1.56 us -> none  [the longest x1 1.47 us: per_device(): s_eff = margin * present]
  transfers between devices with their start and end apart: 4 -> 5, of which waited for: 2 -> 1; matrix products, arithmetic and copies ran while one was open for 4% -> 0% of each run, Pallas kernels for 0% -> 0%
where the time goes in v2:
time: 44 us; the launch traced here: 43.7 us
  starting transfers between devices  15.3 us (35%)
  blocking collectives  14.7 us (33%)
  Pallas kernels  9.9 us (22%)
  local copies, waits for them, and re-layouts  2.86 us (6%)
  between operations  0.72 us (2%)
    all_to_all x1, blocking collectives, per_device(): gathered = lax.all_to_all(spread, AXES, 0, 0, tiled=True)  14.7 us
    ppermute x1, starting transfers between devices, per_device(): near_defect = lax.ppermute(near_defect, AXES, swaps(near_pairs))  12.6 us
    pallas_call x1, Pallas kernels, refine_step(): pl.pallas_call(functools.partial(refine_kernel, quarter_len, entries), ou...  4.59 us
    pallas_call x1, Pallas kernels, defect_step(): pl.pallas_call(functools.partial(defect_kernel, quarter_len), out_shape=(...  3.97 us
    unnamed x10, local copies, waits for them, and re-layouts  2.86 us
    pallas_call x1, Pallas kernels, pack(): pl.pallas_call(functools.partial(pack_kernel, quarter_len), out_shape=(me...  1.35 us
  transfers between devices with their start and end apart: 5, of which 1 were waited for; matrix products, arithmetic and copies ran while one was open for 0% of the time, Pallas kernels for 0%

profile of v2, /device:TPU:0, one launch (start us, length us, event | category | flops | bytes accessed | tf_op | source)
XLA Modules:
  0.0 43.7 jit_solution(2444530008229770070)
XLA Ops:
  0.6 0.0 copy-start
  0.6 1.1 %copy-done = bf16[4,5,128,128]{3,2,1,0:T(8,128)(2,1)S(1)} copy-done((bf16[4,5,128,128]{3,2,1,0:T(8,128)(2,1)S(1)}, bf16[4,5,128,128]{3,2,1,0:T(8,128)(2,1)}, u32[]{:S(2)}) %copy-start) | copy-done | bytes 655384
  1.7 0.0 copy-start.1
  1.7 1.1 %copy-done.1 = bf16[4,5,128,128]{3,2,1,0:T(8,128)(2,1)S(1)} copy-done((bf16[4,5,128,128]{3,2,1,0:T(8,128)(2,1)S(1)}, bf16[4,5,128,128]{3,2,1,0:T(8,128)(2,1)}, u32[]{:S(2)}) %copy-start.1) | copy-done | bytes 655384
  2.8 0.0 copy-start.3
  2.8 0.7 %copy-done.3 = s32[4,5]{1,0:T(4,128)S(1)} copy-done((s32[4,5]{1,0:T(4,128)S(1)}, s32[4,5]{1,0:T(4,128)}, u32[]{:S(2)}) %copy-start.3) | copy-done | bytes 104
  3.5 1.4 %pack.1 = (bf16[2,2,5,128,128]{4,3,2,1,0:T(8,128)(2,1)S(1)}, bf16[2,2,5,128,128]{4,3,2,1,0:T(8,128)(2,1)S(1)}, bf16[2,2,128,128]{3,2,1,0:T(8,128)(2,1)S(1)}) custom-call(bf16[4,5,128,128]{3,2,1,0:T(8,128)(2,1)S(1)} %copy-done, bf16[4,5,128,128]{3,2,1,0:T(8,128)(2,1)S(1)} %copy-done.1, s32[4,5]{1,0:T(4,128)S(1)} %copy-done.3), custom_call_target="tpu_custom_call" | custom-call | tf_op jit(solution)/shard_map/pack/pallas_call | solution.py:74
  4.8 0.5 %collective-permute-start = (bf16[2,2,5,128,128]{4,3,2,1,0:T(8,128)(2,1)S(1)}, bf16[2,2,5,128,128]{4,3,2,1,0:T(8,128)(2,1)S(1)}, u32[]{:S(2)}, u32[]{:S(2)}) collective-permute-start(bf16[2,2,5,128,128]{4,3,2,1,0:T(8,128)(2,1)S(1)} %get-tuple-element.11), channel_id=1, source_target_pairs={{0,1},{1,0},{2,3},{3,2},{4,5},{5,4},{6,7},{7,6},{8,9},{9,8},{10,11... | collective-permute-start | bytes 1966088 | tf_op jit(solution)/shard_map/ppermute | solution.py:464
  5.4 0.7 %collective-permute-start.1 = (bf16[2,2,5,128,128]{4,3,2,1,0:T(8,128)(2,1)S(1)}, bf16[2,2,5,128,128]{4,3,2,1,0:T(8,128)(2,1)S(1)}, u32[]{:S(2)}, u32[]{:S(2)}) collective-permute-start(bf16[2,2,5,128,128]{4,3,2,1,0:T(8,128)(2,1)S(1)} %get-tuple-element.12), channel_id=1, source_target_pairs={{1,2},{2,1},{3,4},{4,3},{5,6},{6,5},{9,10},{10,9},{11,12},{12,11},... | collective-permute-start | bytes 1966088 | tf_op jit(solution)/shard_map/ppermute | solution.py:462
  6.1 0.0 copy-start.2
  6.1 0.8 %collective-permute-start.2 = (bf16[2,2,128,128]{3,2,1,0:T(8,128)(2,1)S(1)}, bf16[2,2,128,128]{3,2,1,0:T(8,128)(2,1)S(1)}, u32[]{:S(2)}, u32[]{:S(2)}) collective-permute-start(bf16[2,2,128,128]{3,2,1,0:T(8,128)(2,1)S(1)} %get-tuple-element.13), channel_id=1, source_target_pairs={{7,8},{8,7},{15,16},{16,15},{23,24},{24,23}} | collective-permute-start | bytes 393224 | tf_op jit(solution)/shard_map/ppermute | solution.py:463
  6.9 0.0 collective-permute-done.2.cross
  6.9 0.2 collective-permute-done.near
  7.1 0.0 collective-permute-done.1.far
  7.1 4.0 %defect.1 = (bf16[2,768,256]{2,1,0:T(8,128)(2,1)S(1)}, bf16[512,256]{1,0:T(8,128)(2,1)S(1)}, bf16[512,256]{1,0:T(8,128)(2,1)S(1)}, f32[32,1,128]{2,1,0:T(1,128)S(1)}) custom-call(bf16[4,5,128,128]{3,2,1,0:T(8,128)(2,1)S(1)} %copy-done, bf16[4,5,128,128]{3,2,1,0:T(8,128)(2,1)S(1)} %copy-done.1, s32[4,5]{1,0:T(4,128)S(1)} %copy-done.3, ...), custom_call_target="tpu_custom_call" | custom-call | flops 1207959552 | bytes 4194304 | tf_op jit(solution)/shard_map/defect/pallas_call | solution.py:241
  11.1 12.6 %collective-permute-start.3 = (bf16[512,256]{1,0:T(8,128)(2,1)S(1)}, bf16[512,256]{1,0:T(8,128)(2,1)S(1)}, u32[]{:S(2)}, u32[]{:S(2)}) collective-permute-start(bf16[512,256]{1,0:T(8,128)(2,1)S(1)} %get-tuple-element.15), channel_id=1, source_target_pairs={{0,1},{1,0},{2,3},{3,2},{4,5},{5,4},{6,7},{7,6},{8,9},{9,8},{10,11... | collective-permute-start | bytes 786440 | tf_op jit(solution)/shard_map/ppermute | solution.py:469
  23.7 0.7 %collective-permute-start.4 = (bf16[512,256]{1,0:T(8,128)(2,1)S(1)}, bf16[512,256]{1,0:T(8,128)(2,1)S(1)}, u32[]{:S(2)}, u32[]{:S(2)}) collective-permute-start(bf16[512,256]{1,0:T(8,128)(2,1)S(1)} %get-tuple-element.16), channel_id=1, source_target_pairs={{1,2},{2,1},{3,4},{4,3},{5,6},{6,5},{7,8},{8,7},{9,10},{10,9},{11,... | collective-permute-start | bytes 786440 | tf_op jit(solution)/shard_map/ppermute | solution.py:468
  24.3 0.0 copy-start.4
  24.3 14.7 %all_to_all.5.gathered = f32[32,1,128]{2,1,0:T(1,128)S(1)} all-to-all(f32[32,1,128]{2,1,0:T(1,128)S(1)} %get-tuple-element.17), channel_id=1, replica_groups=mesh['grp'=4,'slab'=8] {'grp','slab'}, dimensions={0} | all-to-all | bytes 32768 | tf_op jit(solution)/shard_map/all_to_all | solution.py:470
  39.1 0.0 collective-permute-done.3.near_defect
  39.1 0.0 collective-permute-done.4.far_defect
  39.1 0.0 copy-done.2
  39.1 0.0 copy-done.4
  39.1 4.6 %refine.1 = (bf16[4,5,128,128]{3,2,1,0:T(8,128)(2,1)}, f32[1,128]{1,0:T(1,128)}) custom-call(bf16[4,5,128,128]{3,2,1,0:T(8,128)(2,1)S(1)} %copy-done.2, s32[4,5]{1,0:T(4,128)S(1)} %copy-done.4, bf16[2,2,5,128,128]{4,3,2,1,0:T(8,128)(2,1)S(1)} %collective-permute-done.near, bf16[2,2,5,128,128]{4,3,2,1,0:T(8,128)(2,1)S(1)} %collective-permute-done.1.far, ...), custom_call_target="tpu_custom_call" | custom-call | flops 1409286144 | bytes 4194304 | tf_op jit(solution)/shard_map/refine/pallas_call | solution.py:423
Async XLA Ops:
  0.6 1.1 %copy-start = (bf16[4,5,128,128]{3,2,1,0:T(8,128)(2,1)S(1)}, bf16[4,5,128,128]{3,2,1,0:T(8,128)(2,1)}, u32[]{:S(2)}) copy-start(bf16[4,5,128,128]{3,2,1,0:T(8,128)(2,1)} %margin.3) | copy-start | bytes 1966084
  1.7 1.1 %copy-start.1 = (bf16[4,5,128,128]{3,2,1,0:T(8,128)(2,1)S(1)}, bf16[4,5,128,128]{3,2,1,0:T(8,128)(2,1)}, u32[]{:S(2)}) copy-start(bf16[4,5,128,128]{3,2,1,0:T(8,128)(2,1)} %factor.5) | copy-start | bytes 1966084
  2.8 0.7 %copy-start.3 = (s32[4,5]{1,0:T(4,128)S(1)}, s32[4,5]{1,0:T(4,128)}, u32[]{:S(2)}) copy-start(s32[4,5]{1,0:T(4,128)} %pattern.5) | copy-start | bytes 244
  4.8 2.2 %collective-permute-start = (bf16[2,2,5,128,128]{4,3,2,1,0:T(8,128)(2,1)S(1)}, bf16[2,2,5,128,128]{4,3,2,1,0:T(8,128)(2,1)S(1)}, u32[]{:S(2)}, u32[]{:S(2)}) collective-permute-start(bf16[2,2,5,128,128]{4,3,2,1,0:T(8,128)(2,1)S(1)} %get-tuple-element.11), channel_id=1, source_target_pairs={{0,1},{1,0},{2,3},{3,2},{4,5},{5,4},{6,7},{7,6},{8,9},{9,8},{10,11... | collective-permute-start | bytes 1966088 | tf_op jit(solution)/shard_map/ppermute | solution.py:464
  5.4 1.7 %collective-permute-start.1 = (bf16[2,2,5,128,128]{4,3,2,1,0:T(8,128)(2,1)S(1)}, bf16[2,2,5,128,128]{4,3,2,1,0:T(8,128)(2,1)S(1)}, u32[]{:S(2)}, u32[]{:S(2)}) collective-permute-start(bf16[2,2,5,128,128]{4,3,2,1,0:T(8,128)(2,1)S(1)} %get-tuple-element.12), channel_id=1, source_target_pairs={{1,2},{2,1},{3,4},{4,3},{5,6},{6,5},{9,10},{10,9},{11,12},{12,11},... | collective-permute-start | bytes 1966088 | tf_op jit(solution)/shard_map/ppermute | solution.py:462
  6.1 33.0 %copy-start.2 = (bf16[4,5,128,128]{3,2,1,0:T(8,128)(2,1)S(1)}, bf16[4,5,128,128]{3,2,1,0:T(8,128)(2,1)}, u32[]{:S(2)}) copy-start(bf16[4,5,128,128]{3,2,1,0:T(8,128)(2,1)} %factor.5) | copy-start | bytes 1966084
  6.1 0.8 %collective-permute-start.2 = (bf16[2,2,128,128]{3,2,1,0:T(8,128)(2,1)S(1)}, bf16[2,2,128,128]{3,2,1,0:T(8,128)(2,1)S(1)}, u32[]{:S(2)}, u32[]{:S(2)}) collective-permute-start(bf16[2,2,128,128]{3,2,1,0:T(8,128)(2,1)S(1)} %get-tuple-element.13), channel_id=1, source_target_pairs={{7,8},{8,7},{15,16},{16,15},{23,24},{24,23}} | collective-permute-start | bytes 393224 | tf_op jit(solution)/shard_map/ppermute | solution.py:463
  11.1 28.0 %collective-permute-start.3 = (bf16[512,256]{1,0:T(8,128)(2,1)S(1)}, bf16[512,256]{1,0:T(8,128)(2,1)S(1)}, u32[]{:S(2)}, u32[]{:S(2)}) collective-permute-start(bf16[512,256]{1,0:T(8,128)(2,1)S(1)} %get-tuple-element.15), channel_id=1, source_target_pairs={{0,1},{1,0},{2,3},{3,2},{4,5},{5,4},{6,7},{7,6},{8,9},{9,8},{10,11... | collective-permute-start | bytes 786440 | tf_op jit(solution)/shard_map/ppermute | solution.py:469
  23.7 15.4 %collective-permute-start.4 = (bf16[512,256]{1,0:T(8,128)(2,1)S(1)}, bf16[512,256]{1,0:T(8,128)(2,1)S(1)}, u32[]{:S(2)}, u32[]{:S(2)}) collective-permute-start(bf16[512,256]{1,0:T(8,128)(2,1)S(1)} %get-tuple-element.16), channel_id=1, source_target_pairs={{1,2},{2,1},{3,4},{4,3},{5,6},{6,5},{7,8},{8,7},{9,10},{10,9},{11,... | collective-permute-start | bytes 786440 | tf_op jit(solution)/shard_map/ppermute | solution.py:468
  24.3 14.8 %copy-start.4 = (s32[4,5]{1,0:T(4,128)S(1)}, s32[4,5]{1,0:T(4,128)}, u32[]{:S(2)}) copy-start(s32[4,5]{1,0:T(4,128)} %pattern.5) | copy-start | bytes 244

commit v3 on v0

v3 whole, which is shorter than its diff:
```python
import functools

import jax
import jax.numpy as jnp
from jax import lax
from jax.experimental import pallas as pl
from jax.experimental.pallas import tpu as pltpu
from jax.sharding import PartitionSpec as P


AXES = ("grp", "slab")
HBM = pl.BlockSpec(memory_space=pltpu.HBM)
VMEM = pl.BlockSpec(memory_space=pltpu.VMEM)
SMEM = pl.BlockSpec(memory_space=pltpu.SMEM)
PARAMS = pltpu.CompilerParams(vmem_limit_bytes=32 * 1024 * 1024)
FLAG_ROWS = 16


class Sizes:
    def __init__(self, shape, quarter_len, devices):
        self.columns, self.offsets, self.block, _ = shape
        self.half = (self.offsets - 1) // 2
        self.tile = self.half * self.block
        self.cells = self.half * self.offsets
        self.flag_blocks = -(-self.half * self.half * FLAG_ROWS // self.block)
        self.quarter_len = quarter_len
        self.devices = devices
        self.entries = self.columns * devices * self.block

    def cost(self, products, moved):
        return pl.CostEstimate(
            flops=products * 2 * self.tile**3, bytes_accessed=moved * 2**20, transcendentals=0
        )

    def tiles(self, count, dtype):
        return jax.ShapeDtypeStruct((count, self.tile, self.tile), dtype)


def odd_device():
    return lax.rem(lax.axis_index("slab"), 2)


def half_starts(z):
    near = jnp.where(odd_device() == 1, 0, z.columns - z.half)
    return near, z.columns - z.half - near


def keep(flag, value):
    return jnp.where(flag, value, jnp.zeros_like(value))


def dot(left, right):
    return jnp.dot(left, right, preferred_element_type=jnp.float32)


def chain_tile(true_tile):
    return jnp.where(odd_device() == 1, 2 - true_tile, true_tile)


def expand(z, out, read):
    block = z.block
    for t in range(z.half):
        for a in range(3 * z.half):
            o = a - t
            u = a % z.half
            if 0 <= o < z.offsets:
                value = read(t, o)
            else:
                value = jnp.zeros((block, block), out.dtype)
            out[
                chain_tile(a // z.half),
                u * block : (u + 1) * block,
                t * block : (t + 1) * block,
            ] = value


def offset_of(z, e, t, u):
    return jnp.where(odd_device() == 1, 1 - e, e - 1) * z.half + u - t + z.half


def flag_of(z, pattern, first, e, t, u):
    o = offset_of(z, e, t, u)
    inside = jnp.logical_and(o >= 0, o < z.offsets)
    return jnp.logical_and(inside, pattern[first + t, jnp.clip(o, 0, z.offsets - 1)] != 0)


def masked(z, value, flag):
    block = z.block
    rows = []
    for u in range(z.half):
        rows.append(
            jnp.concatenate(
                [
                    keep(
                        flag(t, u),
                        value[u * block : (u + 1) * block, t * block : (t + 1) * block],
                    )
                    for t in range(z.half)
                ],
                axis=1,
            )
        )
    return jnp.concatenate(rows, axis=0)


def own_masked(z, pattern, first, e, value):
    return masked(z, value, lambda t, u: flag_of(z, pattern, first, e, t, u))


def identity(z):
    shape = (z.tile, z.tile)
    rows = lax.broadcasted_iota(jnp.int32, shape, 0)
    return (rows == lax.broadcasted_iota(jnp.int32, shape, 1)).astype(jnp.float32)


def sum_squares(z, value):
    wide = value.astype(jnp.float32)
    return jnp.sum((wide * wide).reshape(-1, 8, z.tile), axis=0)


def store_half(z, pattern, first, tiles, cells):
    block = z.block
    for t in range(z.half):
        for o in range(z.offsets):
            a = t + o
            u = a % z.half
            value = tiles[
                chain_tile(a // z.half),
                u * block : (u + 1) * block,
                t * block : (t + 1) * block,
            ]
            cells[t, o] = keep(pattern[first + t, o] != 0, value).astype(cells.dtype)


def pack_kernel(z, margin, factor, pattern_in, near, far, cross, cells, pattern, sems):
    near_first, far_first = half_starts(z)
    first_row = lax.axis_index("slab") * z.columns
    fetch = pltpu.make_async_copy(pattern_in, pattern, sems.at[4])
    fetch.start()
    plan = ((margin, far_first), (factor, far_first), (margin, near_first), (factor, near_first))
    copies = [
        pltpu.make_async_copy(source.at[pl.ds(first, z.half)], cells.at[k], sems.at[k])
        for k, (source, first) in enumerate(plan)
    ]
    for copy in copies:
        copy.start()
    fetch.wait()
    for k, (source, first) in enumerate(plan):
        copies[k].wait()
        for t in range(z.half):
            for o in range(z.offsets):
                flag = pattern[first + t, o] != 0
                if k % 2:
                    row = first_row + first + t + o - z.half
                    inside = jnp.logical_and(row >= 0, row < z.quarter_len)
                    flag = jnp.logical_and(flag, inside)
                value = keep(flag, cells[k, t, o])
                cell = t * z.offsets + o
                u = cell % z.offsets + t - z.half
                if k == 0:
                    far[cell] = value
                    near[2 * z.cells + cell] = value
                elif k == 1:
                    far[z.cells + cell] = value
                    if 0 <= u < z.half:
                        cross[t, u] = value
                else:
                    near[(k - 2) * z.cells + cell] = value
    per_block = z.block // FLAG_ROWS
    for f in range(z.flag_blocks * per_block):
        t, u = f // z.half, f % z.half
        value = jnp.zeros((FLAG_ROWS, z.block), near.dtype)
        if t < z.half:
            value = keep(pattern[near_first + t, u - t + z.half] != 0, jnp.ones_like(value))
        low = f % per_block * FLAG_ROWS
        near[3 * z.cells + f // per_block, low : low + FLAG_ROWS] = value


def pack(z, margin, factor, pattern):
    kind = margin.dtype
    return pl.pallas_call(
        functools.partial(pack_kernel, z),
        out_shape=(
            jax.ShapeDtypeStruct((3 * z.cells + z.flag_blocks, z.block, z.block), kind),
            jax.ShapeDtypeStruct((2 * z.cells, z.block, z.block), kind),
            jax.ShapeDtypeStruct((z.half, z.half, z.block, z.block), kind),
        ),
        in_specs=[HBM, HBM, HBM],
        out_specs=(VMEM, VMEM, VMEM),
        scratch_shapes=[
            pltpu.VMEM((4, z.half, z.offsets, z.block, z.block), kind),
            pltpu.SMEM(pattern.shape, pattern.dtype),
            pltpu.SemaphoreType.DMA((5,)),
        ],
        compiler_params=PARAMS,
        name="pack",
    )(margin, factor, pattern)


def inner_kernel(
    z, pattern, near, far, beside, z_cols, turned, p_part, d_part, d_near, d_beside, squares,
    s_cols, z_turned, image,
):
    near_first, _ = half_starts(z)
    kind = near.dtype

    def cells_of(ref, base):
        return lambda t, o: ref[base + t * z.offsets + o]

    expand(z, s_cols.at[0], cells_of(far, 0))
    expand(z, s_cols.at[1], cells_of(near, 0))
    expand(z, s_cols.at[2], cells_of(beside, 0))
    expand(z, s_cols.at[3], cells_of(beside, 2 * z.cells))
    expand(z, z_cols.at[0], cells_of(far, z.cells))
    expand(z, z_cols.at[1], cells_of(near, z.cells))
    expand(z, z_cols.at[2], cells_of(beside, z.cells))
    for x in range(3):
        for e in range(3):
            z_turned[x, e] = z_cols[x, e].T
    turned[0] = z_turned[0, 0]
    turned[1] = z_turned[0, 1]
    turned[2] = z_turned[1, 0]

    def image_tile(y, c):
        total = None
        for inner in range(max(c - 1, y - 1, 1), min(c + 1, y + 1) + 1):
            term = dot(s_cols[inner - 1, y - inner + 1], z_cols[c - 1, inner - c + 1])
            total = term if total is None else total + term
        return total

    def turned_sum(i, c, rows):
        total = None
        for m in rows:
            term = dot(z_turned[i - 1, m - i + 1], image[c - 1, m])
            total = term if total is None else total + term
        return total

    p_part[0] = image_tile(0, 1)
    p_part[1] = image_tile(1, 1)
    for c, rows in ((1, (2, 3)), (2, (0, 1, 2, 3, 4)), (3, (1, 2, 3, 4))):
        for y in rows:
            image[c - 1, y] = image_tile(y, c).astype(kind)
    d_part[0] = turned_sum(1, 1, (2,))
    d_part[1] = turned_sum(2, 1, (2, 3))
    eye = identity(z)
    total = jnp.zeros((8, z.tile), jnp.float32)
    for i in (1, 2, 3):
        value = -turned_sum(i, 2, (i - 1, i, i + 1))
        if i == 2:
            value = eye + value
        value = own_masked(z, pattern, near_first, i - 1, value).astype(kind)
        d_near[i - 1] = value
        total = total + sum_squares(z, value)
    squares[...] = total

    def side_flag(t, u):
        o = offset_of(z, 0, t, u)
        inside = jnp.logical_and(o >= 0, o < z.offsets)
        back = jnp.clip(z.offsets - 1 - o, 0, z.offsets - 1)
        return jnp.logical_and(inside, pattern[near_first + u, back] != 0)

    d_beside[0] = masked(z, -turned_sum(2, 3, (1, 2, 3)), side_flag).astype(kind)
    value = eye - turned_sum(3, 3, (2, 3, 4))
    block = z.block
    per_block = block // FLAG_ROWS
    for t in range(z.half):
        for u in range(z.half):
            f = t * z.half + u
            low = f % per_block * FLAG_ROWS
            flags = beside[3 * z.cells + f // per_block, low : low + FLAG_ROWS]
            flag = flags.astype(jnp.float32)[:1]
            part = (slice(u * block, (u + 1) * block), slice(t * block, (t + 1) * block))
            d_beside[1, part[0], part[1]] = (value[part] * flag).astype(kind)


def inner_step(z, pattern, near, far, beside):
    kind = near.dtype
    tile = z.tile
    return pl.pallas_call(
        functools.partial(inner_kernel, z),
        out_shape=(
            jax.ShapeDtypeStruct((3, 3, tile, tile), kind),
            z.tiles(3, kind),
            z.tiles(2, jnp.float32),
            z.tiles(2, jnp.float32),
            z.tiles(3, kind),
            z.tiles(2, kind),
            jax.ShapeDtypeStruct((8, tile), jnp.float32),
        ),
        in_specs=[SMEM, VMEM, VMEM, VMEM],
        out_specs=(VMEM,) * 7,
        scratch_shapes=[
            pltpu.VMEM((4, 3, tile, tile), kind),
            pltpu.VMEM((3, 3, tile, tile), kind),
            pltpu.VMEM((3, 5, tile, tile), kind),
        ],
        compiler_params=PARAMS,
        cost_estimate=z.cost(42, 8),
        name="inner",
    )(pattern, near, far, beside)


def outer_kernel(
    z, pattern, far, cross, z_cols, turned, p_part, d_part, squares, d_far, d_out, z_far, spread, s_far
):
    _, far_first = half_starts(z)
    kind = far.dtype

    def factor_cell(t, o):
        value = far[z.cells + t * z.offsets + o]
        u = o + t - z.half
        if 0 <= u < z.half:
            value = value + cross[t, u]
        return value

    expand(z, s_far, lambda t, o: far[t * z.offsets + o])
    expand(z, z_far, factor_cell)
    link = z_cols[0, 0]
    image = (
        dot(s_far[0], link).astype(kind),
        (dot(s_far[1], link) + p_part[0]).astype(kind),
        (dot(s_far[2], link) + p_part[1]).astype(kind),
    )
    values = (
        -(dot(z_far[0].T, image[0]) + dot(z_far[1].T, image[1]) + dot(z_far[2].T, image[2])),
        identity(z) - (dot(turned[0], image[1]) + dot(turned[1], image[2]) + d_part[0]),
        -(dot(turned[2], image[2]) + d_part[1]),
    )
    total = squares[...]
    for e, value in enumerate(values):
        value = own_masked(z, pattern, far_first, e, value).astype(kind)
        d_far[e] = value
        if e < 2:
            d_out[e] = value
        total = total + sum_squares(z, value)
    lanes = jnp.sum(total, axis=0, keepdims=True)
    folded = lanes[:, : z.block]
    for t in range(1, z.half):
        folded = folded + lanes[:, t * z.block : (t + 1) * z.block]
    spread[...] = jnp.broadcast_to(folded[None], spread.shape)


def outer_step(z, pattern, far, cross, z_cols, turned, p_part, d_part, squares):
    kind = far.dtype
    return pl.pallas_call(
        functools.partial(outer_kernel, z),
        out_shape=(
            z.tiles(3, kind),
            z.tiles(2, kind),
            z.tiles(3, kind),
            jax.ShapeDtypeStruct((z.devices, 1, z.block), jnp.float32),
        ),
        in_specs=[SMEM] + [VMEM] * 7,
        out_specs=(VMEM,) * 4,
        scratch_shapes=[pltpu.VMEM((3, z.tile, z.tile), kind)],
        compiler_params=PARAMS,
        cost_estimate=z.cost(9, 4),
        name="outer",
    )(pattern, far, cross, z_cols, turned, p_part, d_part, squares)


def middle_kernel(
    z, pattern, z_cols, z_far, d_far, d_near, d_beside, refined, base, e_part, square, tiles, cells, sem
):
    near_first, far_first = half_starts(z)
    factor = (z_far, z_cols.at[0], z_cols.at[1], z_cols.at[2])
    defect = (None, d_far, d_near, d_beside)

    def product(left, i, c, right, first=0):
        total = None
        for k in range(max(first, i - 1, c - 1), min(i + 1, c + 1) + 1):
            term = dot(left[k][i - k + 1], right[k - c + 1])
            total = term if total is None else total + term
        return total

    for i in (1, 2, 3):
        value = product(defect, i, 2, d_near, 1)
        square[i - 1] = own_masked(z, pattern, near_first, i - 1, value).astype(square.dtype)
    for i in (1, 2, 3):
        tiles[i - 1] = (
            z_cols[1, i - 1].astype(jnp.float32)
            + 0.5 * product(factor, i, 2, d_near)
            + 0.375 * product(factor, i, 2, square)
        )
    store_half(z, pattern, near_first, tiles, cells)
    copy = pltpu.make_async_copy(cells, refined.at[pl.ds(near_first, z.half)], sem)
    copy.start()
    for i in (0, 1, 2):
        base[i] = z_cols[0, i].astype(jnp.float32) + 0.5 * product(factor, i, 1, d_far)
        e_part[i] = product(defect, i, 1, d_far, 1)
    copy.wait()


def middle_step(z, pattern, z_cols, z_far, d_far, d_near, d_beside):
    kind = z_far.dtype
    shape = (z.columns, z.offsets, z.block, z.block)
    return pl.pallas_call(
        functools.partial(middle_kernel, z),
        out_shape=(
            jax.ShapeDtypeStruct(shape, kind),
            z.tiles(3, jnp.float32),
            z.tiles(3, jnp.float32),
        ),
        in_specs=[SMEM] + [VMEM] * 5,
        out_specs=(HBM, VMEM, VMEM),
        scratch_shapes=[
            pltpu.VMEM((3, z.tile, z.tile), kind),
            pltpu.VMEM((3, z.tile, z.tile), jnp.float32),
            pltpu.VMEM((z.half,) + shape[1:], kind),
            pltpu.SemaphoreType.DMA(()),
        ],
        compiler_params=PARAMS,
        cost_estimate=z.cost(33, 6),
        name="middle",
    )(pattern, z_cols, z_far, d_far, d_near, d_beside)


def last_kernel(
    z, pattern, z_cols, z_far, d_far, d_in, base, e_part, gathered, _, refined, norm, square, tiles, cells,
    sem,
):
    _, far_first = half_starts(z)
    factor = (z_far, z_cols.at[0], z_cols.at[1])
    values = (
        e_part[0] + dot(d_in[1], d_far[0]),
        e_part[1] + dot(d_in[0], d_far[0]),
        e_part[2],
    )
    for i, value in enumerate(values):
        square[i] = own_masked(z, pattern, far_first, i, value).astype(square.dtype)
    for i in (0, 1, 2):
        total = None
        for k in range(max(0, i - 1), min(2, i + 1) + 1):
            term = dot(factor[k][i - k + 1], square[k])
            total = term if total is None else total + term
        tiles[i] = base[i] + 0.375 * total
    store_half(z, pattern, far_first, tiles, cells)
    copy = pltpu.make_async_copy(cells, refined.at[pl.ds(far_first, z.half)], sem)
    copy.start()
    mean = jnp.sum(gathered[...]) * (1.0 / z.entries)
    norm[...] = jnp.sqrt(jnp.full(norm.shape, mean, jnp.float32))
    copy.wait()


def last_step(z, pattern, z_cols, z_far, d_far, d_in, base, e_part, gathered, refined):
    kind = refined.dtype
    return pl.pallas_call(
        functools.partial(last_kernel, z),
        out_shape=(
            jax.ShapeDtypeStruct(refined.shape, kind),
            jax.ShapeDtypeStruct((1, z.block), jnp.float32),
        ),
        in_specs=[SMEM] + [VMEM] * 7 + [HBM],
        out_specs=(HBM, VMEM),
        scratch_shapes=[
            pltpu.VMEM((3, z.tile, z.tile), kind),
            pltpu.VMEM((3, z.tile, z.tile), jnp.float32),
            pltpu.VMEM((z.half,) + refined.shape[1:], kind),
            pltpu.SemaphoreType.DMA(()),
        ],
        input_output_aliases={8: 0},
        compiler_params=PARAMS,
        cost_estimate=z.cost(9, 4),
        name="last",
    )(pattern, z_cols, z_far, d_far, d_in, base, e_part, gathered, refined)


def swaps(pairs):
    return [pair for i, j in pairs for pair in ((i, j), (j, i))]


def per_device(margin, factor, pattern):
    slabs = lax.axis_size("slab")
    devices = lax.axis_size("grp") * slabs
    z = Sizes(margin.shape, margin.shape[0] * slabs, devices)
    if slabs % 2 or z.columns != 2 * z.half:
        raise ValueError("sizes")
    near_pairs = [(i, i + 1) for i in range(0, devices - 1, 2)]
    far_pairs = [(i, i + 1) for i in range(1, devices - 1, 2)]
    inner_pairs = [(i, j) for i, j in far_pairs if j % slabs]
    cross_pairs = [(i, j) for i, j in far_pairs if not j % slabs]
    near, far, cross = pack(z, margin, factor, pattern)
    beyond = lax.ppermute(far, AXES, swaps(inner_pairs))
    across = lax.ppermute(cross, AXES, swaps(cross_pairs))
    beside = lax.ppermute(near, AXES, swaps(near_pairs))
    z_cols, turned, p_part, d_part, d_near, d_beside, squares = inner_step(
        z, pattern, near, far, beside
    )
    d_far, d_out, z_far, spread = outer_step(
        z, pattern, beyond, across, z_cols, turned, p_part, d_part, squares
    )
    d_in = lax.ppermute(d_out, AXES, swaps(far_pairs))
    gathered = lax.all_to_all(spread, AXES, 0, 0, tiled=True)
    refined, base, e_part = middle_step(z, pattern, z_cols, z_far, d_far, d_near, d_beside)
    refined, norm = last_step(
        z, pattern, z_cols, z_far, d_far, d_in, base, e_part, gathered, refined
    )
    return refined, norm[0, 0]


def solution(mesh):
    return jax.shard_map(
        per_device,
        mesh=mesh,
        in_specs=(
            P(AXES, None, None, None),
            P(AXES, None, None, None),
            P(AXES, None),
        ),
        out_specs=(P(AXES, None, None, None), P()),
        check_vma=False,
    )
```

time: 103 us -> 40.6 us (0.39)
  blocking collectives: 42.6 us -> 0 us
  matrix products: 13.9 us -> 0 us
  Pallas kernels: 0 us -> 10.9 us
  other arithmetic: 8.69 us -> 0 us
  starting transfers between devices: 22.2 us -> 19.4 us
  between operations: 2.95 us -> 0.74 us
  waiting for transfers between devices: 4.64 us -> 2.92 us
    psum x1 -> x0, blocking collectives: 42.6 us -> none  [defect_measure(): squares_sum = lax.psum(partial_sum, ('grp', 'slab'))]
    ppermute x4, starting transfers between devices: 22.2 us -> 3.23 us  [the longest x1 1.35 us: per_device(): d_in = lax.ppermute(d_out, AXES, swaps(far_pairs))]
    all_to_all x0 -> x1, starting transfers between devices: none -> 16.2 us  [per_device(): gathered = lax.all_to_all(spread, AXES, 0, 0, tiled=True)]
    dot_general x29 -> x0, matrix products: 13.9 us -> none  [band_product(): jnp.einsum(einsum_form, left_stack, right_stack, preferred_element_type=j...]
    pallas_call x0 -> x5, Pallas kernels: none -> 10.9 us  [the longest x1 2.94 us: last_step(): pl.pallas_call(functools.partial(last_kernel, z), out_shape=(jax.ShapeDty...]
    ppermute x4, waiting for transfers between devices: 4.64 us -> 0.87 us  [the longest x1 0.86 us: per_device(): beside = lax.ppermute(near, AXES, swaps(near_pairs))]
    slice x4 -> x0, local copies, waits for them, and re-layouts: 2.86 us -> none  [the longest x2 1.23 us: band_product(): left_ext[band_half + column_shift:band_half + column_shift + columns, lef...]
    unnamed x47 -> x20, local copies, waits for them, and re-layouts: 4.01 us -> 6.17 us
  transfers between devices with their start and end apart: 4 -> 5, of which waited for: 2 -> 2; matrix products, arithmetic and copies ran while one was open for 4% -> 0% of each run, Pallas kernels for 0% -> 12%
where the time goes in v3:
time: 40.6 us; the launch traced here: 40.1 us
  starting transfers between devices  19.4 us (48%)
  Pallas kernels  10.9 us (27%)
  local copies, waits for them, and re-layouts  6.17 us (15%)
  waiting for transfers between devices  2.92 us (7%)
  between operations  0.74 us (2%)
    all_to_all x1, starting transfers between devices, per_device(): gathered = lax.all_to_all(spread, AXES, 0, 0, tiled=True)  16.2 us
    unnamed x20, local copies, waits for them, and re-layouts  6.17 us
    pallas_call x1, Pallas kernels, last_step(): pl.pallas_call(functools.partial(last_kernel, z), out_shape=(jax.ShapeDty...  2.94 us
    pallas_call x1, Pallas kernels, inner_step(): pl.pallas_call(functools.partial(inner_kernel, z), out_shape=(jax.ShapeDt...  2.54 us
    pallas_call x1, Pallas kernels, middle_step(): pl.pallas_call(functools.partial(middle_kernel, z), out_shape=(jax.ShapeD...  2.45 us
    all_to_all x1, waiting for transfers between devices, per_device(): gathered = lax.all_to_all(spread, AXES, 0, 0, tiled=True)  2.05 us
    pallas_call x1, Pallas kernels, outer_step(): pl.pallas_call(functools.partial(outer_kernel, z), out_shape=(z.tiles(3,...  2.02 us
    ppermute x1, starting transfers between devices, per_device(): d_in = lax.ppermute(d_out, AXES, swaps(far_pairs))  1.35 us
  transfers between devices with their start and end apart: 5, of which 2 were waited for; matrix products, arithmetic and copies ran while one was open for 0% of the time, Pallas kernels for 12%

profile of v3, /device:TPU:0, one launch (start us, length us, event | category | flops | bytes accessed | tf_op | source)
XLA Modules:
  0.0 40.1 jit_solution(1373269304535898511)
XLA Ops:
  0.6 0.0 copy-start
  0.6 1.1 %copy-done = bf16[4,5,128,128]{3,2,1,0:T(8,128)(2,1)S(1)} copy-done((bf16[4,5,128,128]{3,2,1,0:T(8,128)(2,1)S(1)}, bf16[4,5,128,128]{3,2,1,0:T(8,128)(2,1)}, u32[]{:S(2)}) %copy-start) | copy-done | bytes 655384
  1.7 0.0 copy-start.1
  1.7 1.1 %copy-done.1 = bf16[4,5,128,128]{3,2,1,0:T(8,128)(2,1)S(1)} copy-done((bf16[4,5,128,128]{3,2,1,0:T(8,128)(2,1)S(1)}, bf16[4,5,128,128]{3,2,1,0:T(8,128)(2,1)}, u32[]{:S(2)}) %copy-start.1) | copy-done | bytes 655384
  2.8 0.0 copy-start.2
  2.8 0.7 %copy-done.2 = s32[4,5]{1,0:T(4,128)S(1)} copy-done((s32[4,5]{1,0:T(4,128)S(1)}, s32[4,5]{1,0:T(4,128)}, u32[]{:S(2)}) %copy-start.2) | copy-done | bytes 104
  3.5 0.0 copy-start.3
  3.5 1.0 %pack.1 = (bf16[31,128,128]{2,1,0:T(8,128)(2,1)S(1)}, bf16[20,128,128]{2,1,0:T(8,128)(2,1)S(1)}, bf16[2,2,128,128]{3,2,1,0:T(8,128)(2,1)S(1)}) custom-call(bf16[4,5,128,128]{3,2,1,0:T(8,128)(2,1)S(1)} %copy-done, bf16[4,5,128,128]{3,2,1,0:T(8,128)(2,1)S(1)} %copy-done.1, s32[4,5]{1,0:T(4,128)S(1)} %copy-done.2), custom_call_target="tpu_custom_call" | custom-call | tf_op jit(solution)/shard_map/pack/pallas_call | solution.py:181
  4.5 0.5 %collective-permute-start = (bf16[31,128,128]{2,1,0:T(8,128)(2,1)S(1)}, bf16[31,128,128]{2,1,0:T(8,128)(2,1)S(1)}, u32[]{:S(2)}, u32[]{:S(2)}) collective-permute-start(bf16[31,128,128]{2,1,0:T(8,128)(2,1)S(1)} %get-tuple-element.21.near), channel_id=1, source_target_pairs={{0,1},{1,0},{2,3},{3,2},{4,5},{5,4},{6,7},{7,6},{8,9},{9,8},{10,11... | collective-permute-start | bytes 3047432 | tf_op jit(solution)/shard_map/ppermute | solution.py:485
  5.0 0.7 %collective-permute-start.1 = (bf16[20,128,128]{2,1,0:T(8,128)(2,1)S(1)}, bf16[20,128,128]{2,1,0:T(8,128)(2,1)S(1)}, u32[]{:S(2)}, u32[]{:S(2)}) collective-permute-start(bf16[20,128,128]{2,1,0:T(8,128)(2,1)S(1)} %get-tuple-element.22.far), channel_id=1, source_target_pairs={{1,2},{2,1},{3,4},{4,3},{5,6},{6,5},{9,10},{10,9},{11,12},{12,11},... | collective-permute-start | bytes 1966088 | tf_op jit(solution)/shard_map/ppermute | solution.py:483
  5.7 0.7 %collective-permute-start.2 = (bf16[2,2,128,128]{3,2,1,0:T(8,128)(2,1)S(1)}, bf16[2,2,128,128]{3,2,1,0:T(8,128)(2,1)S(1)}, u32[]{:S(2)}, u32[]{:S(2)}) collective-permute-start(bf16[2,2,128,128]{3,2,1,0:T(8,128)(2,1)S(1)} %get-tuple-element.24), channel_id=1, source_target_pairs={{7,8},{8,7},{15,16},{16,15},{23,24},{24,23}} | collective-permute-start | bytes 393224 | tf_op jit(solution)/shard_map/ppermute | solution.py:484
  6.4 0.9 %collective-permute-done.beside = bf16[31,128,128]{2,1,0:T(8,128)(2,1)S(1)} collective-permute-done((bf16[31,128,128]{2,1,0:T(8,128)(2,1)S(1)}, bf16[31,128,128]{2,1,0:T(8,128)(2,1)S(1)}, u32[]{:S(2)}, u32[]{:S(2)}) %collective-permute-start) | collective-permute-done | bytes 1015840 | tf_op jit(solution)/shard_map/ppermute | solution.py:485
  7.2 0.0 copy-done.3
  7.2 2.5 %inner.1 = (bf16[3,3,256,256]{3,2,1,0:T(8,128)(2,1)S(1)}, bf16[3,256,256]{2,1,0:T(8,128)(2,1)S(1)}, f32[2,256,256]{2,1,0:T(8,128)S(1)}, f32[2,256,256]{2,1,0:T(8...) custom-call(s32[4,5]{1,0:T(4,128)S(1)} %copy-done.3, ...), custom_call_target="tpu_custom_call" | custom-call | flops 1409286144 | bytes 8388608 | tf_op jit(solution)/shard_map/inner/pallas_call | solution.py:279
  9.8 0.0 copy-start.6
  9.8 0.0 copy-start.8
  9.8 0.0 collective-permute-done.2.cross
  9.8 0.0 collective-permute-done.1.far
  9.8 2.0 %outer.1 = (bf16[3,256,256]{2,1,0:T(8,128)(2,1)S(1)}, bf16[2,256,256]{2,1,0:T(8,128)(2,1)}, bf16[3,256,256]{2,1,0:T(8,128)(2,1)S(1)}, f32[32,1,128]{2,1,0:T(1,128)}) custom-call(s32[4,5]{1,0:T(4,128)S(1)} %copy-done.3, bf16[20,128,128]{2,1,0:T(8,128)(2,1)S(1)} %collective-permute-done.1.far, bf16[2,2,128,128]{3,2,1,0:T(8,128)(2,1)S(1)} %collective-permute-done.2.cross, ...), custom_call_target="tpu_custom_call" | custom-call | flops 301989888 | bytes 4194304 | tf_op jit(solution)/shard_map/outer/pallas_call | solution.py:345
  11.8 0.0 copy-done.6
  11.8 0.0 copy-done.8
  11.8 1.4 %collective-permute-start.3 = (bf16[2,256,256]{2,1,0:T(8,128)(2,1)}, bf16[2,256,256]{2,1,0:T(8,128)(2,1)}, u32[]{:S(2)}, u32[]{:S(2)}) collective-permute-start(bf16[2,256,256]{2,1,0:T(8,128)(2,1)} %get-tuple-element.31), channel_id=1, source_target_pairs={{1,2},{2,1},{3,4},{4,3},{5,6},{6,5},{7,8},{8,7},{9,10},{10,9},{11,... | collective-permute-start | bytes 786440 | tf_op jit(solution)/shard_map/ppermute | solution.py:492
  13.2 16.2 %all-to-all-start = ((f32[32,1,128]{2,1,0:T(1,128)}), f32[32,1,128]{2,1,0:T(1,128)S(1)}, u32[]{:S(2)}, u32[]{:S(2)}) async-start(f32[32,1,128]{2,1,0:T(1,128)} %get-tuple-element.36), calls=%async_computation | async-start | bytes 32768 | tf_op jit(solution)/shard_map/all_to_all | solution.py:493
  29.4 0.0 copy-start.4
  29.4 0.7 %copy-done.4 = s32[4,5]{1,0:T(4,128)S(1)} copy-done((s32[4,5]{1,0:T(4,128)S(1)}, s32[4,5]{1,0:T(4,128)}, u32[]{:S(2)}) %copy-start.4) | copy-done | bytes 104
  30.1 0.0 copy-start.7
  30.1 1.0 %copy-done.7 = bf16[3,256,256]{2,1,0:T(8,128)(2,1)S(1)} copy-done((bf16[3,256,256]{2,1,0:T(8,128)(2,1)S(1)}, bf16[3,256,256]{2,1,0:T(8,128)(2,1)}, u32[]{:S(2)}) %copy-start.7) | copy-done | bytes 393240
  31.1 0.0 copy-start.9
  31.1 0.9 %copy-done.9 = bf16[2,256,256]{2,1,0:T(8,128)(2,1)S(1)} copy-done((bf16[2,256,256]{2,1,0:T(8,128)(2,1)S(1)}, bf16[2,256,256]{2,1,0:T(8,128)(2,1)}, u32[]{:S(2)}) %copy-start.9) | copy-done | bytes 262168
  32.0 2.4 %middle.1 = (bf16[4,5,128,128]{3,2,1,0:T(8,128)(2,1)}, f32[3,256,256]{2,1,0:T(8,128)S(1)}, f32[3,256,256]{2,1,0:T(8,128)S(1)}) custom-call(s32[4,5]{1,0:T(4,128)S(1)} %copy-done.4, bf16[3,3,256,256]{3,2,1,0:T(8,128)(2,1)S(1)} %get-tuple-element.23.z_cols, bf16[3,256,256]{2,1,0:T(8,128)(2,1)S(1)} %get-tuple-element.29.z_far, ...), custom_call_target="tpu_custom_call" | custom-call | flops 1107296256 | bytes 6291456 | tf_op jit(solution)/shard_map/middle/pallas_call | solution.py:397
  34.5 2.0 %all-to-all-done.gathered = f32[32,1,128]{2,1,0:T(1,128)S(1)} async-done(((f32[32,1,128]{2,1,0:T(1,128)}), f32[32,1,128]{2,1,0:T(1,128)S(1)}, u32[]{:S(2)}, u32[]{:S(2)}) %all-to-all-start) | async-done | bytes 16416 | tf_op jit(solution)/shard_map/all_to_all | solution.py:493
  36.5 0.0 collective-permute-done.3.d_in
  36.5 0.0 copy-start.5
  36.5 0.7 %copy-done.5 = s32[4,5]{1,0:T(4,128)S(1)} copy-done((s32[4,5]{1,0:T(4,128)S(1)}, s32[4,5]{1,0:T(4,128)}, u32[]{:S(2)}) %copy-start.5) | copy-done | bytes 104
  37.2 2.9 %last.1 = (bf16[4,5,128,128]{3,2,1,0:T(8,128)(2,1)}, f32[1,128]{1,0:T(1,128)}) custom-call(s32[4,5]{1,0:T(4,128)S(1)} %copy-done.5, bf16[3,3,256,256]{3,2,1,0:T(8,128)(2,1)S(1)} %get-tuple-element.23.z_cols, bf16[3,256,256]{2,1,0:T(8,128)(2,1)S(1)} %get-tuple-element.29.z_far, ...), custom_call_target="tpu_custom_call", output_to_operand_aliasing={{0}: (8, {})} | custom-call | flops 301989888 | bytes 4194304 | tf_op jit(solution)/shard_map/last/pallas_call | solution.py:447
Async XLA Ops:
  0.6 1.1 %copy-start = (bf16[4,5,128,128]{3,2,1,0:T(8,128)(2,1)S(1)}, bf16[4,5,128,128]{3,2,1,0:T(8,128)(2,1)}, u32[]{:S(2)}) copy-start(bf16[4,5,128,128]{3,2,1,0:T(8,128)(2,1)} %margin.1) | copy-start | bytes 1966084
  1.7 1.1 %copy-start.1 = (bf16[4,5,128,128]{3,2,1,0:T(8,128)(2,1)S(1)}, bf16[4,5,128,128]{3,2,1,0:T(8,128)(2,1)}, u32[]{:S(2)}) copy-start(bf16[4,5,128,128]{3,2,1,0:T(8,128)(2,1)} %factor.1) | copy-start | bytes 1966084
  2.8 0.7 %copy-start.2 = (s32[4,5]{1,0:T(4,128)S(1)}, s32[4,5]{1,0:T(4,128)}, u32[]{:S(2)}) copy-start(s32[4,5]{1,0:T(4,128)} %pattern.7) | copy-start | bytes 244
  3.5 3.7 %copy-start.3 = (s32[4,5]{1,0:T(4,128)S(1)}, s32[4,5]{1,0:T(4,128)}, u32[]{:S(2)}) copy-start(s32[4,5]{1,0:T(4,128)} %pattern.7) | copy-start | bytes 244
  4.5 2.8 %collective-permute-start = (bf16[31,128,128]{2,1,0:T(8,128)(2,1)S(1)}, bf16[31,128,128]{2,1,0:T(8,128)(2,1)S(1)}, u32[]{:S(2)}, u32[]{:S(2)}) collective-permute-start(bf16[31,128,128]{2,1,0:T(8,128)(2,1)S(1)} %get-tuple-element.21.near), channel_id=1, source_target_pairs={{0,1},{1,0},{2,3},{3,2},{4,5},{5,4},{6,7},{7,6},{8,9},{9,8},{10,11... | collective-permute-start | bytes 3047432 | tf_op jit(solution)/shard_map/ppermute | solution.py:485
  5.0 4.8 %collective-permute-start.1 = (bf16[20,128,128]{2,1,0:T(8,128)(2,1)S(1)}, bf16[20,128,128]{2,1,0:T(8,128)(2,1)S(1)}, u32[]{:S(2)}, u32[]{:S(2)}) collective-permute-start(bf16[20,128,128]{2,1,0:T(8,128)(2,1)S(1)} %get-tuple-element.22.far), channel_id=1, source_target_pairs={{1,2},{2,1},{3,4},{4,3},{5,6},{6,5},{9,10},{10,9},{11,12},{12,11},... | collective-permute-start | bytes 1966088 | tf_op jit(solution)/shard_map/ppermute | solution.py:483
  5.7 4.1 %collective-permute-start.2 = (bf16[2,2,128,128]{3,2,1,0:T(8,128)(2,1)S(1)}, bf16[2,2,128,128]{3,2,1,0:T(8,128)(2,1)S(1)}, u32[]{:S(2)}, u32[]{:S(2)}) collective-permute-start(bf16[2,2,128,128]{3,2,1,0:T(8,128)(2,1)S(1)} %get-tuple-element.24), channel_id=1, source_target_pairs={{7,8},{8,7},{15,16},{16,15},{23,24},{24,23}} | collective-permute-start | bytes 393224 | tf_op jit(solution)/shard_map/ppermute | solution.py:484
  9.8 2.1 %copy-start.6 = (bf16[3,256,256]{2,1,0:T(8,128)(2,1)}, bf16[3,256,256]{2,1,0:T(8,128)(2,1)S(1)}, u32[]{:S(2)}) copy-start(bf16[3,256,256]{2,1,0:T(8,128)(2,1)S(1)} %get-tuple-element.32.d_near) | copy-start | bytes 1179652
  9.8 2.1 %copy-start.8 = (bf16[2,256,256]{2,1,0:T(8,128)(2,1)}, bf16[2,256,256]{2,1,0:T(8,128)(2,1)S(1)}, u32[]{:S(2)}) copy-start(bf16[2,256,256]{2,1,0:T(8,128)(2,1)S(1)} %get-tuple-element.33.d_beside) | copy-start | bytes 786436
  11.8 24.7 %collective-permute-start.3 = (bf16[2,256,256]{2,1,0:T(8,128)(2,1)}, bf16[2,256,256]{2,1,0:T(8,128)(2,1)}, u32[]{:S(2)}, u32[]{:S(2)}) collective-permute-start(bf16[2,256,256]{2,1,0:T(8,128)(2,1)} %get-tuple-element.31), channel_id=1, source_target_pairs={{1,2},{2,1},{3,4},{4,3},{5,6},{6,5},{7,8},{8,7},{9,10},{10,9},{11,... | collective-permute-start | bytes 786440 | tf_op jit(solution)/shard_map/ppermute | solution.py:492
  13.2 23.3 %all-to-all-start = ((f32[32,1,128]{2,1,0:T(1,128)}), f32[32,1,128]{2,1,0:T(1,128)S(1)}, u32[]{:S(2)}, u32[]{:S(2)}) async-start(f32[32,1,128]{2,1,0:T(1,128)} %get-tuple-element.36), calls=%async_computation | async-start | bytes 32768 | tf_op jit(solution)/shard_map/all_to_all | solution.py:493
  29.4 0.7 %copy-start.4 = (s32[4,5]{1,0:T(4,128)S(1)}, s32[4,5]{1,0:T(4,128)}, u32[]{:S(2)}) copy-start(s32[4,5]{1,0:T(4,128)} %pattern.7) | copy-start | bytes 244
  30.1 1.0 %copy-start.7 = (bf16[3,256,256]{2,1,0:T(8,128)(2,1)S(1)}, bf16[3,256,256]{2,1,0:T(8,128)(2,1)}, u32[]{:S(2)}) copy-start(bf16[3,256,256]{2,1,0:T(8,128)(2,1)} %copy-done.6) | copy-start | bytes 1179652
  31.1 0.9 %copy-start.9 = (bf16[2,256,256]{2,1,0:T(8,128)(2,1)S(1)}, bf16[2,256,256]{2,1,0:T(8,128)(2,1)}, u32[]{:S(2)}) copy-start(bf16[2,256,256]{2,1,0:T(8,128)(2,1)} %copy-done.8) | copy-start | bytes 786436
  36.5 0.7 %copy-start.5 = (s32[4,5]{1,0:T(4,128)S(1)}, s32[4,5]{1,0:T(4,128)}, u32[]{:S(2)}) copy-start(s32[4,5]{1,0:T(4,128)} %pattern.7) | copy-start | bytes 244

commit v4 on v3

--- a/solution.py
+++ b/solution.py
@@ -113,12 +113,20 @@
     return (rows == lax.broadcasted_iota(jnp.int32, shape, 1)).astype(jnp.float32)
 
 
+def tile_product(left, right, i, c, low, high):
+    total = None
+    for k in range(max(low, i - 1, c - 1), min(high, i + 1, c + 1) + 1):
+        term = dot(left[k][i - k + 1], right[k - c + 1])
+        total = term if total is None else total + term
+    return total
+
+
 def sum_squares(z, value):
     wide = value.astype(jnp.float32)
     return jnp.sum((wide * wide).reshape(-1, 8, z.tile), axis=0)
 
 
-def store_half(z, pattern, first, tiles, cells):
+def store_half(z, tiles, cells):
     block = z.block
     for t in range(z.half):
         for o in range(z.offsets):
@@ -129,24 +137,33 @@
                 u * block : (u + 1) * block,
                 t * block : (t + 1) * block,
             ]
-            cells[t, o] = keep(pattern[first + t, o] != 0, value).astype(cells.dtype)
-
-
-def pack_kernel(z, margin, factor, pattern_in, near, far, cross, cells, pattern, sems):
+            cells[t, o] = value.astype(cells.dtype)
+
+
+def mask_kernel(z, pattern, mask_near, mask_far):
+    ones = jnp.ones((z.tile, z.tile), jnp.float32)
+    for out, first in zip((mask_near, mask_far), half_starts(z)):
+        for e in range(3):
+            out[e] = own_masked(z, pattern, first, e, ones).astype(out.dtype)
+
+
+def masks(z, pattern, kind):
+    return pl.pallas_call(
+        functools.partial(mask_kernel, z),
+        out_shape=(z.tiles(3, kind), z.tiles(3, kind)),
+        in_specs=[SMEM],
+        out_specs=(VMEM, VMEM),
+        compiler_params=PARAMS,
+        cost_estimate=z.cost(20, 1),
+        name="masks",
+    )(pattern)
+
+
+def pack_kernel(z, margin, factor, pattern, _near, _far, near, far, cross):
     near_first, far_first = half_starts(z)
     first_row = lax.axis_index("slab") * z.columns
-    fetch = pltpu.make_async_copy(pattern_in, pattern, sems.at[4])
-    fetch.start()
     plan = ((margin, far_first), (factor, far_first), (margin, near_first), (factor, near_first))
-    copies = [
-        pltpu.make_async_copy(source.at[pl.ds(first, z.half)], cells.at[k], sems.at[k])
-        for k, (source, first) in enumerate(plan)
-    ]
-    for copy in copies:
-        copy.start()
-    fetch.wait()
     for k, (source, first) in enumerate(plan):
-        copies[k].wait()
         for t in range(z.half):
             for o in range(z.offsets):
                 flag = pattern[first + t, o] != 0
@@ -154,9 +171,9 @@
                     row = first_row + first + t + o - z.half
                     inside = jnp.logical_and(row >= 0, row < z.quarter_len)
                     flag = jnp.logical_and(flag, inside)
-                value = keep(flag, cells[k, t, o])
+                value = keep(flag, source[first + t, o])
                 cell = t * z.offsets + o
-                u = cell % z.offsets + t - z.half
+                u = o + t - z.half
                 if k == 0:
                     far[cell] = value
                     near[2 * z.cells + cell] = value
@@ -176,7 +193,7 @@
         near[3 * z.cells + f // per_block, low : low + FLAG_ROWS] = value
 
 
-def pack(z, margin, factor, pattern):
+def pack(z, margin, factor, pattern, mask_near, mask_far):
     kind = margin.dtype
     return pl.pallas_call(
         functools.partial(pack_kernel, z),
@@ -185,21 +202,16 @@
             jax.ShapeDtypeStruct((2 * z.cells, z.block, z.block), kind),
             jax.ShapeDtypeStruct((z.half, z.half, z.block, z.block), kind),
         ),
-        in_specs=[HBM, HBM, HBM],
+        in_specs=[VMEM, VMEM, SMEM, VMEM, VMEM],
         out_specs=(VMEM, VMEM, VMEM),
-        scratch_shapes=[
-            pltpu.VMEM((4, z.half, z.offsets, z.block, z.block), kind),
-            pltpu.SMEM(pattern.shape, pattern.dtype),
-            pltpu.SemaphoreType.DMA((5,)),
-        ],
         compiler_params=PARAMS,
         name="pack",
-    )(margin, factor, pattern)
+    )(margin, factor, pattern, mask_near, mask_far)
 
 
 def inner_kernel(
-    z, pattern, near, far, beside, z_cols, turned, p_part, d_part, d_near, d_beside, squares,
-    s_cols, z_turned, image,
+    z, pattern, near, far, beside, z_cols, turned, p_part, d_part, d_near, squares, base_near, e_near,
+    s_cols, z_turned, image, d_beside,
 ):
     near_first, _ = half_starts(z)
     kind = near.dtype
@@ -272,6 +284,14 @@
             part = (slice(u * block, (u + 1) * block), slice(t * block, (t + 1) * block))
             d_beside[1, part[0], part[1]] = (value[part] * flag).astype(kind)
 
+    factor = (None, z_cols.at[0], z_cols.at[1], z_cols.at[2])
+    defect = (None, None, d_near, d_beside)
+    for i in (1, 2, 3):
+        base_near[i - 1] = z_cols[1, i - 1].astype(jnp.float32) + 0.5 * tile_product(
+            factor, d_near, i, 2, 1, 3
+        )
+        e_near[i - 1] = tile_product(defect, d_near, i, 2, 2, 3)
+
 
 def inner_step(z, pattern, near, far, beside):
     kind = near.dtype
@@ -284,25 +304,28 @@
             z.tiles(2, jnp.float32),
             z.tiles(2, jnp.float32),
             z.tiles(3, kind),
-            z.tiles(2, kind),
             jax.ShapeDtypeStruct((8, tile), jnp.float32),
+            z.tiles(3, jnp.float32),
+            z.tiles(3, jnp.float32),
         ),
         in_specs=[SMEM, VMEM, VMEM, VMEM],
-        out_specs=(VMEM,) * 7,
+        out_specs=(VMEM,) * 8,
         scratch_shapes=[
             pltpu.VMEM((4, 3, tile, tile), kind),
             pltpu.VMEM((3, 3, tile, tile), kind),
             pltpu.VMEM((3, 5, tile, tile), kind),
+            pltpu.VMEM((2, tile, tile), kind),
         ],
         compiler_params=PARAMS,
-        cost_estimate=z.cost(42, 8),
+        cost_estimate=z.cost(54, 8),
         name="inner",
     )(pattern, near, far, beside)
 
 
 def outer_kernel(
-    z, pattern, far, cross, z_cols, turned, p_part, d_part, squares, d_far, d_out, z_far, spread, s_far
+    z, pattern, far, cross, z_cols, turned, p_part, d_part, squares, *refs
 ):
+    d_far, d_out, z_far, spread, s_far = refs[-5:]
     _, far_first = half_starts(z)
     kind = far.dtype
 
@@ -340,7 +363,7 @@
     spread[...] = jnp.broadcast_to(folded[None], spread.shape)
 
 
-def outer_step(z, pattern, far, cross, z_cols, turned, p_part, d_part, squares):
+def outer_step(z, pattern, far, cross, z_cols, turned, p_part, d_part, squares, held):
     kind = far.dtype
     return pl.pallas_call(
         functools.partial(outer_kernel, z),
@@ -350,48 +373,40 @@
             z.tiles(3, kind),
             jax.ShapeDtypeStruct((z.devices, 1, z.block), jnp.float32),
         ),
-        in_specs=[SMEM] + [VMEM] * 7,
+        in_specs=[SMEM] + [VMEM] * (7 + len(held)),
         out_specs=(VMEM,) * 4,
         scratch_shapes=[pltpu.VMEM((3, z.tile, z.tile), kind)],
         compiler_params=PARAMS,
         cost_estimate=z.cost(9, 4),
         name="outer",
-    )(pattern, far, cross, z_cols, turned, p_part, d_part, squares)
+    )(pattern, far, cross, z_cols, turned, p_part, d_part, squares, *held)
 
 
 def middle_kernel(
-    z, pattern, z_cols, z_far, d_far, d_near, d_beside, refined, base, e_part, square, tiles, cells, sem
+    z, z_cols, z_far, d_far, d_near, base_near, e_near, mask_near, refined, base, e_part, square, tiles,
+    cells, sem,
 ):
-    near_first, far_first = half_starts(z)
+    near_first, _ = half_starts(z)
     factor = (z_far, z_cols.at[0], z_cols.at[1], z_cols.at[2])
-    defect = (None, d_far, d_near, d_beside)
-
-    def product(left, i, c, right, first=0):
-        total = None
-        for k in range(max(first, i - 1, c - 1), min(i + 1, c + 1) + 1):
-            term = dot(left[k][i - k + 1], right[k - c + 1])
-            total = term if total is None else total + term
-        return total
-
+    defect = (None, d_far, d_near)
     for i in (1, 2, 3):
-        value = product(defect, i, 2, d_near, 1)
-        square[i - 1] = own_masked(z, pattern, near_first, i - 1, value).astype(square.dtype)
+        value = e_near[i - 1]
+        if i < 3:
+            value = value + dot(d_far[i], d_near[0])
+        square[i - 1] = (value * mask_near[i - 1].astype(jnp.float32)).astype(square.dtype)
     for i in (1, 2, 3):
-        tiles[i - 1] = (
-            z_cols[1, i - 1].astype(jnp.float32)
-            + 0.5 * product(factor, i, 2, d_near)
-            + 0.375 * product(factor, i, 2, square)
-        )
-    store_half(z, pattern, near_first, tiles, cells)
+        value = base_near[i - 1] + 0.375 * tile_product(factor, square, i, 2, 1, 3)
+        tiles[i - 1] = value * mask_near[i - 1].astype(jnp.float32)
+    store_half(z, tiles, cells)
     copy = pltpu.make_async_copy(cells, refined.at[pl.ds(near_first, z.half)], sem)
     copy.start()
     for i in (0, 1, 2):
-        base[i] = z_cols[0, i].astype(jnp.float32) + 0.5 * product(factor, i, 1, d_far)
-        e_part[i] = product(defect, i, 1, d_far, 1)
+        base[i] = z_cols[0, i].astype(jnp.float32) + 0.5 * tile_product(factor, d_far, i, 1, 0, 2)
+        e_part[i] = tile_product(defect, d_far, i, 1, 1, 2)
     copy.wait()
 
 
-def middle_step(z, pattern, z_cols, z_far, d_far, d_near, d_beside):
+def middle_step(z, z_cols, z_far, d_far, d_near, base_near, e_near, mask_near):
     kind = z_far.dtype
     shape = (z.columns, z.offsets, z.block, z.block)
     return pl.pallas_call(
@@ -401,7 +416,7 @@
             z.tiles(3, jnp.float32),
             z.tiles(3, jnp.float32),
         ),
-        in_specs=[SMEM] + [VMEM] * 5,
+        in_specs=[VMEM] * 7,
         out_specs=(HBM, VMEM, VMEM),
         scratch_shapes=[
             pltpu.VMEM((3, z.tile, z.tile), kind),
@@ -410,14 +425,14 @@
             pltpu.SemaphoreType.DMA(()),
         ],
         compiler_params=PARAMS,
-        cost_estimate=z.cost(33, 6),
+        cost_estimate=z.cost(21, 6),
         name="middle",
-    )(pattern, z_cols, z_far, d_far, d_near, d_beside)
+    )(z_cols, z_far, d_far, d_near, base_near, e_near, mask_near)
 
 
 def last_kernel(
-    z, pattern, z_cols, z_far, d_far, d_in, base, e_part, gathered, _, refined, norm, square, tiles, cells,
-    sem,
+    z, z_cols, z_far, d_far, d_in, base, e_part, mask_far, gathered, _, refined, norm, square, tiles,
+    cells, sem,
 ):
     _, far_first = half_starts(z)
     factor = (z_far, z_cols.at[0], z_cols.at[1])
@@ -427,14 +442,11 @@
         e_part[2],
     )
     for i, value in enumerate(values):
-        square[i] = own_masked(z, pattern, far_first, i, value).astype(square.dtype)
+        square[i] = (value * mask_far[i].astype(jnp.float32)).astype(square.dtype)
     for i in (0, 1, 2):
-        total = None
-        for k in range(max(0, i - 1), min(2, i + 1) + 1):
-            term = dot(factor[k][i - k + 1], square[k])
-            total = term if total is None else total + term
-        tiles[i] = base[i] + 0.375 * total
-    store_half(z, pattern, far_first, tiles, cells)
+        value = base[i] + 0.375 * tile_product(factor, square, i, 1, 0, 2)
+        tiles[i] = value * mask_far[i].astype(jnp.float32)
+    store_half(z, tiles, cells)
     copy = pltpu.make_async_copy(cells, refined.at[pl.ds(far_first, z.half)], sem)
     copy.start()
     mean = jnp.sum(gathered[...]) * (1.0 / z.entries)
@@ -442,7 +454,7 @@
     copy.wait()
 
 
-def last_step(z, pattern, z_cols, z_far, d_far, d_in, base, e_part, gathered, refined):
+def last_step(z, z_cols, z_far, d_far, d_in, base, e_part, mask_far, gathered, refined):
     kind = refined.dtype
     return pl.pallas_call(
         functools.partial(last_kernel, z),
@@ -450,7 +462,7 @@
             jax.ShapeDtypeStruct(refined.shape, kind),
             jax.ShapeDtypeStruct((1, z.block), jnp.float32),
         ),
-        in_specs=[SMEM] + [VMEM] * 7 + [HBM],
+        in_specs=[VMEM] * 8 + [HBM],
         out_specs=(HBM, VMEM),
         scratch_shapes=[
             pltpu.VMEM((3, z.tile, z.tile), kind),
@@ -462,7 +474,7 @@
         compiler_params=PARAMS,
         cost_estimate=z.cost(9, 4),
         name="last",
-    )(pattern, z_cols, z_far, d_far, d_in, base, e_part, gathered, refined)
+    )(z_cols, z_far, d_far, d_in, base, e_part, mask_far, gathered, refined)
 
 
 def swaps(pairs):
@@ -479,21 +491,25 @@
     far_pairs = [(i, i + 1) for i in range(1, devices - 1, 2)]
     inner_pairs = [(i, j) for i, j in far_pairs if j % slabs]
     cross_pairs = [(i, j) for i, j in far_pairs if not j % slabs]
-    near, far, cross = pack(z, margin, factor, pattern)
+    mask_near, mask_far = masks(z, pattern, margin.dtype)
+    near, far, cross = pack(z, margin, factor, pattern, mask_near, mask_far)
     beyond = lax.ppermute(far, AXES, swaps(inner_pairs))
     across = lax.ppermute(cross, AXES, swaps(cross_pairs))
     beside = lax.ppermute(near, AXES, swaps(near_pairs))
-    z_cols, turned, p_part, d_part, d_near, d_beside, squares = inner_step(
+    z_cols, turned, p_part, d_part, d_near, squares, base_near, e_near = inner_step(
         z, pattern, near, far, beside
     )
+    held = (d_near, base_near, e_near, mask_near, mask_far)
     d_far, d_out, z_far, spread = outer_step(
-        z, pattern, beyond, across, z_cols, turned, p_part, d_part, squares
+        z, pattern, beyond, across, z_cols, turned, p_part, d_part, squares, held
     )
     d_in = lax.ppermute(d_out, AXES, swaps(far_pairs))
     gathered = lax.all_to_all(spread, AXES, 0, 0, tiled=True)
-    refined, base, e_part = middle_step(z, pattern, z_cols, z_far, d_far, d_near, d_beside)
+    refined, base, e_part = middle_step(
+        z, z_cols, z_far, d_far, d_near, base_near, e_near, mask_near
+    )
     refined, norm = last_step(
-        z, pattern, z_cols, z_far, d_far, d_in, base, e_part, gathered, refined
+        z, z_cols, z_far, d_far, d_in, base, e_part, mask_far, gathered, refined
     )
     return refined, norm[0, 0]
 

time: 40.6 us -> 44.8 us (1.10)
  local copies, waits for them, and re-layouts: 6.17 us -> 11.8 us
  waiting for transfers between devices: 2.92 us -> 1.4 us
    unnamed x20 -> x32, local copies, waits for them, and re-layouts: 6.17 us -> 11.8 us
    all_to_all x1, waiting for transfers between devices: 2.05 us -> 0.53 us  [per_device(): gathered = lax.all_to_all(spread, AXES, 0, 0, tiled=True)]
    pallas_call x0 -> x1, Pallas kernels: none -> 0.65 us  [masks(): pl.pallas_call(functools.partial(mask_kernel, z), out_shape=(z.tiles(3, k...]
    pallas_call x1, Pallas kernels: 2.45 us -> 1.8 us  [middle_step(): pl.pallas_call(functools.partial(middle_kernel, z), out_shape=(jax.ShapeD...]
  transfers between devices with their start and end apart: 5 -> 5, of which waited for: 2 -> 2; matrix products, arithmetic and copies ran while one was open for 0% -> 0% of each run, Pallas kernels for 12% -> 11%
where the time goes in v4:
time: 44.8 us; the launch traced here: 44.3 us
  starting transfers between devices  19 us (42%)
  local copies, waits for them, and re-layouts  11.8 us (26%)
  Pallas kernels  11.3 us (25%)
  waiting for transfers between devices  1.4 us (3%)
  between operations  0.77 us (2%)
    all_to_all x1, starting transfers between devices, per_device(): gathered = lax.all_to_all(spread, AXES, 0, 0, tiled=True)  15.8 us
    unnamed x32, local copies, waits for them, and re-layouts  11.8 us
    pallas_call x1, Pallas kernels, last_step(): pl.pallas_call(functools.partial(last_kernel, z), out_shape=(jax.ShapeDty...  2.95 us
    pallas_call x1, Pallas kernels, inner_step(): pl.pallas_call(functools.partial(inner_kernel, z), out_shape=(jax.ShapeDt...  2.92 us
    pallas_call x1, Pallas kernels, outer_step(): pl.pallas_call(functools.partial(outer_kernel, z), out_shape=(z.tiles(3,...  2.03 us
    pallas_call x1, Pallas kernels, middle_step(): pl.pallas_call(functools.partial(middle_kernel, z), out_shape=(jax.ShapeD...  1.8 us
    ppermute x1, starting transfers between devices, per_device(): d_in = lax.ppermute(d_out, AXES, swaps(far_pairs))  1.36 us
    pallas_call x1, Pallas kernels, pack(): pl.pallas_call(functools.partial(pack_kernel, z), out_shape=(jax.ShapeDty...  0.93 us
  transfers between devices with their start and end apart: 5, of which 2 were waited for; matrix products, arithmetic and copies ran while one was open for 0% of the time, Pallas kernels for 11%

profile of v4, /device:TPU:0, one launch (start us, length us, event | category | flops | bytes accessed | tf_op | source)
XLA Modules:
  0.0 44.3 jit_solution(5543399918035438560)
XLA Ops:
  0.6 0.0 copy-start.12
  0.6 0.0 copy-start.15
  0.6 0.7 %copy-done.15 = s32[4,5]{1,0:T(4,128)S(1)} copy-done((s32[4,5]{1,0:T(4,128)S(1)}, s32[4,5]{1,0:T(4,128)}, u32[]{:S(2)}) %copy-start.15) | copy-done | bytes 104
  1.4 0.0 copy-start.13
  1.4 0.7 %masks.1 = (bf16[3,256,256]{2,1,0:T(8,128)(2,1)S(1)}, bf16[3,256,256]{2,1,0:T(8,128)(2,1)S(1)}) custom-call(s32[4,5]{1,0:T(4,128)S(1)} %copy-done.15), custom_call_target="tpu_custom_call" | custom-call | flops 671088640 | bytes 1048576 | tf_op jit(solution)/shard_map/masks/pallas_call | solution.py:151
  2.0 0.0 copy-done.12
  2.1 0.5 %copy-done.13 = bf16[4,5,128,128]{3,2,1,0:T(8,128)(2,1)S(1)} copy-done((bf16[4,5,128,128]{3,2,1,0:T(8,128)(2,1)S(1)}, bf16[4,5,128,128]{3,2,1,0:T(8,128)(2,1)}, u32[]{:S(2)}) %copy-start.13) | copy-done | bytes 655384
  2.5 0.9 %pack.1 = (bf16[31,128,128]{2,1,0:T(8,128)(2,1)S(1)}, bf16[20,128,128]{2,1,0:T(8,128)(2,1)S(1)}, bf16[2,2,128,128]{3,2,1,0:T(8,128)(2,1)S(1)}) custom-call(bf16[4,5,128,128]{3,2,1,0:T(8,128)(2,1)S(1)} %copy-done.12, bf16[4,5,128,128]{3,2,1,0:T(8,128)(2,1)S(1)} %copy-done.13, s32[4,5]{1,0:T(4,128)S(1)} %copy-done.15, ...), custom_call_target="tpu_custom_call" | custom-call | tf_op jit(solution)/shard_map/pack/pallas_call | solution.py:198
  3.5 0.5 %collective-permute-start = (bf16[31,128,128]{2,1,0:T(8,128)(2,1)S(1)}, bf16[31,128,128]{2,1,0:T(8,128)(2,1)S(1)}, u32[]{:S(2)}, u32[]{:S(2)}) collective-permute-start(bf16[31,128,128]{2,1,0:T(8,128)(2,1)S(1)} %get-tuple-element.26.near), channel_id=1, source_target_pairs={{0,1},{1,0},{2,3},{3,2},{4,5},{5,4},{6,7},{7,6},{8,9},{9,8},{10,11... | collective-permute-start | bytes 3047432 | tf_op jit(solution)/shard_map/ppermute | solution.py:498
  4.0 0.7 %collective-permute-start.1 = (bf16[20,128,128]{2,1,0:T(8,128)(2,1)S(1)}, bf16[20,128,128]{2,1,0:T(8,128)(2,1)S(1)}, u32[]{:S(2)}, u32[]{:S(2)}) collective-permute-start(bf16[20,128,128]{2,1,0:T(8,128)(2,1)S(1)} %get-tuple-element.27.far), channel_id=1, source_target_pairs={{1,2},{2,1},{3,4},{4,3},{5,6},{6,5},{9,10},{10,9},{11,12},{12,11},... | collective-permute-start | bytes 1966088 | tf_op jit(solution)/shard_map/ppermute | solution.py:496
  4.7 0.7 %collective-permute-start.2 = (bf16[2,2,128,128]{3,2,1,0:T(8,128)(2,1)S(1)}, bf16[2,2,128,128]{3,2,1,0:T(8,128)(2,1)S(1)}, u32[]{:S(2)}, u32[]{:S(2)}) collective-permute-start(bf16[2,2,128,128]{3,2,1,0:T(8,128)(2,1)S(1)} %get-tuple-element.29), channel_id=1, source_target_pairs={{7,8},{8,7},{15,16},{16,15},{23,24},{24,23}} | collective-permute-start | bytes 393224 | tf_op jit(solution)/shard_map/ppermute | solution.py:497
  5.4 0.9 %collective-permute-done.beside = bf16[31,128,128]{2,1,0:T(8,128)(2,1)S(1)} collective-permute-done((bf16[31,128,128]{2,1,0:T(8,128)(2,1)S(1)}, bf16[31,128,128]{2,1,0:T(8,128)(2,1)S(1)}, u32[]{:S(2)}, u32[]{:S(2)}) %collective-permute-start) | collective-permute-done | bytes 1015840 | tf_op jit(solution)/shard_map/ppermute | solution.py:498
  6.2 2.9 %inner.1 = (bf16[3,3,256,256]{3,2,1,0:T(8,128)(2,1)S(1)}, bf16[3,256,256]{2,1,0:T(8,128)(2,1)S(1)}, f32[2,256,256]{2,1,0:T(8,128)S(1)}, f32[2,256,256]{2,1,0:T(8...) custom-call(s32[4,5]{1,0:T(4,128)S(1)} %copy-done.15, ...), custom_call_target="tpu_custom_call" | custom-call | flops 1811939328 | bytes 8388608 | tf_op jit(solution)/shard_map/inner/pallas_call | solution.py:299
  9.1 0.0 copy-start
  9.2 0.0 collective-permute-done.2.cross
  9.2 0.0 collective-permute-done.1.far
  9.2 2.0 %outer.1 = (bf16[3,256,256]{2,1,0:T(8,128)(2,1)S(1)}, bf16[2,256,256]{2,1,0:T(8,128)(2,1)}, bf16[3,256,256]{2,1,0:T(8,128)(2,1)S(1)}, f32[32,1,128]{2,1,0:T(1,128)S(1)}) custom-call(s32[4,5]{1,0:T(4,128)S(1)} %copy-done.15, bf16[20,128,128]{2,1,0:T(8,128)(2,1)S(1)} %collective-permute-done.1.far, bf16[2,2,128,128]{3,2,1,0:T(8,128)(2,1)S(1)} %collective-permute-done.2.cross, ...), custom_call_target="tpu_custom_call" | custom-call | flops 301989888 | bytes 4194304 | tf_op jit(solution)/shard_map/outer/pallas_call | solution.py:368
  11.2 0.0 copy-done
  11.2 0.0 copy-start.2
  11.2 0.7 %copy-done.2 = bf16[3,256,256]{2,1,0:T(8,128)(2,1)} copy-done((bf16[3,256,256]{2,1,0:T(8,128)(2,1)}, bf16[3,256,256]{2,1,0:T(8,128)(2,1)S(1)}, u32[]{:S(2)}) %copy-start.2) | copy-done | bytes 393240
  12.0 0.0 copy-start.5
  12.0 0.8 %copy-done.5 = bf16[3,256,256]{2,1,0:T(8,128)(2,1)} copy-done((bf16[3,256,256]{2,1,0:T(8,128)(2,1)}, bf16[3,256,256]{2,1,0:T(8,128)(2,1)S(1)}, u32[]{:S(2)}) %copy-start.5) | copy-done | bytes 393240
  12.8 0.0 copy-start.14
  12.8 1.4 %collective-permute-start.3 = (bf16[2,256,256]{2,1,0:T(8,128)(2,1)}, bf16[2,256,256]{2,1,0:T(8,128)(2,1)}, u32[]{:S(2)}, u32[]{:S(2)}) collective-permute-start(bf16[2,256,256]{2,1,0:T(8,128)(2,1)} %get-tuple-element.39), channel_id=1, source_target_pairs={{1,2},{2,1},{3,4},{4,3},{5,6},{6,5},{7,8},{8,7},{9,10},{10,9},{11,... | collective-permute-start | bytes 786440 | tf_op jit(solution)/shard_map/ppermute | solution.py:506
  14.1 0.0 copy-done.14
  14.1 15.8 %all-to-all-start = ((f32[32,1,128]{2,1,0:T(1,128)}), f32[32,1,128]{2,1,0:T(1,128)S(1)}, u32[]{:S(2)}, u32[]{:S(2)}) async-start(f32[32,1,128]{2,1,0:T(1,128)} %copy-done.14), calls=%async_computation | async-start | bytes 32768 | tf_op jit(solution)/shard_map/all_to_all | solution.py:507
  29.9 0.0 copy-start.1
  29.9 1.0 %copy-done.1 = bf16[3,256,256]{2,1,0:T(8,128)(2,1)S(1)} copy-done((bf16[3,256,256]{2,1,0:T(8,128)(2,1)S(1)}, bf16[3,256,256]{2,1,0:T(8,128)(2,1)}, u32[]{:S(2)}) %copy-start.1) | copy-done | bytes 393240
  30.9 0.0 copy-start.3
  30.9 1.0 %copy-done.3 = bf16[3,256,256]{2,1,0:T(8,128)(2,1)S(1)} copy-done((bf16[3,256,256]{2,1,0:T(8,128)(2,1)S(1)}, bf16[3,256,256]{2,1,0:T(8,128)(2,1)}, u32[]{:S(2)}) %copy-start.3) | copy-done | bytes 393240
  31.9 0.0 copy-start.6
  31.9 1.0 %copy-done.6 = bf16[3,256,256]{2,1,0:T(8,128)(2,1)S(1)} copy-done((bf16[3,256,256]{2,1,0:T(8,128)(2,1)S(1)}, bf16[3,256,256]{2,1,0:T(8,128)(2,1)}, u32[]{:S(2)}) %copy-start.6) | copy-done | bytes 393240
  32.9 1.8 %middle.1 = (bf16[4,5,128,128]{3,2,1,0:T(8,128)(2,1)}, f32[3,256,256]{2,1,0:T(8,128)S(1)}, f32[3,256,256]{2,1,0:T(8,128)S(1)}) custom-call(bf16[3,3,256,256]{3,2,1,0:T(8,128)(2,1)S(1)} %get-tuple-element.28.z_cols, bf16[3,256,256]{2,1,0:T(8,128)(2,1)S(1)} %copy-done.6, bf16[3,256,256]{2,1,0:T(8,128)(2,1)S(1)} %copy-done.3, ...), custom_call_target="tpu_custom_call" | custom-call | flops 704643072 | bytes 6291456 | tf_op jit(solution)/shard_map/middle/pallas_call | solution.py:412
  34.7 0.0 copy-start.8
  34.7 0.9 %copy-done.8 = f32[3,256,256]{2,1,0:T(8,128)} copy-done((f32[3,256,256]{2,1,0:T(8,128)}, f32[3,256,256]{2,1,0:T(8,128)S(1)}, u32[]{:S(2)}) %copy-start.8) | copy-done | bytes 786456
  35.6 0.0 copy-start.10
  35.6 0.9 %copy-done.10 = f32[3,256,256]{2,1,0:T(8,128)} copy-done((f32[3,256,256]{2,1,0:T(8,128)}, f32[3,256,256]{2,1,0:T(8,128)S(1)}, u32[]{:S(2)}) %copy-start.10) | copy-done | bytes 786456
  36.5 0.5 %all-to-all-done.gathered = f32[32,1,128]{2,1,0:T(1,128)S(1)} async-done(((f32[32,1,128]{2,1,0:T(1,128)}), f32[32,1,128]{2,1,0:T(1,128)S(1)}, u32[]{:S(2)}, u32[]{:S(2)}) %all-to-all-start) | async-done | bytes 16416 | tf_op jit(solution)/shard_map/all_to_all | solution.py:507
  37.1 0.0 collective-permute-done.3.d_in
  37.1 0.0 copy-start.4
  37.1 1.0 %copy-done.4 = bf16[3,256,256]{2,1,0:T(8,128)(2,1)S(1)} copy-done((bf16[3,256,256]{2,1,0:T(8,128)(2,1)S(1)}, bf16[3,256,256]{2,1,0:T(8,128)(2,1)}, u32[]{:S(2)}) %copy-start.4) | copy-done | bytes 393240
  38.1 0.0 copy-start.7
  38.1 1.0 %copy-done.7 = bf16[3,256,256]{2,1,0:T(8,128)(2,1)S(1)} copy-done((bf16[3,256,256]{2,1,0:T(8,128)(2,1)S(1)}, bf16[3,256,256]{2,1,0:T(8,128)(2,1)}, u32[]{:S(2)}) %copy-start.7) | copy-done | bytes 393240
  39.1 0.0 copy-start.9
  39.1 1.1 %copy-done.9 = f32[3,256,256]{2,1,0:T(8,128)S(1)} copy-done((f32[3,256,256]{2,1,0:T(8,128)S(1)}, f32[3,256,256]{2,1,0:T(8,128)}, u32[]{:S(2)}) %copy-start.9) | copy-done | bytes 786456
  40.2 0.0 copy-start.11
  40.2 1.1 %copy-done.11 = f32[3,256,256]{2,1,0:T(8,128)S(1)} copy-done((f32[3,256,256]{2,1,0:T(8,128)S(1)}, f32[3,256,256]{2,1,0:T(8,128)}, u32[]{:S(2)}) %copy-start.11) | copy-done | bytes 786456
  41.3 2.9 %last.1 = (bf16[4,5,128,128]{3,2,1,0:T(8,128)(2,1)}, f32[1,128]{1,0:T(1,128)}) custom-call(bf16[3,3,256,256]{3,2,1,0:T(8,128)(2,1)S(1)} %get-tuple-element.28.z_cols, bf16[3,256,256]{2,1,0:T(8,128)(2,1)S(1)} %copy-done.7, bf16[3,256,256]{2,1,0:T(8,128)(2,1)S(1)} %copy-done.4, ...), custom_call_target="tpu_custom_call", output_to_operand_aliasing={{0}: (8, {})} | custom-call | flops 301989888 | bytes 4194304 | tf_op jit(solution)/shard_map/last/pallas_call | solution.py:459
Async XLA Ops:
  0.6 1.4 %copy-start.12 = (bf16[4,5,128,128]{3,2,1,0:T(8,128)(2,1)S(1)}, bf16[4,5,128,128]{3,2,1,0:T(8,128)(2,1)}, u32[]{:S(2)}) copy-start(bf16[4,5,128,128]{3,2,1,0:T(8,128)(2,1)} %margin.1) | copy-start | bytes 1966084
  0.6 0.7 %copy-start.15 = (s32[4,5]{1,0:T(4,128)S(1)}, s32[4,5]{1,0:T(4,128)}, u32[]{:S(2)}) copy-start(s32[4,5]{1,0:T(4,128)} %pattern.7) | copy-start | bytes 244
  1.4 1.1 %copy-start.13 = (bf16[4,5,128,128]{3,2,1,0:T(8,128)(2,1)S(1)}, bf16[4,5,128,128]{3,2,1,0:T(8,128)(2,1)}, u32[]{:S(2)}) copy-start(bf16[4,5,128,128]{3,2,1,0:T(8,128)(2,1)} %factor.1) | copy-start | bytes 1966084
  3.5 2.8 %collective-permute-start = (bf16[31,128,128]{2,1,0:T(8,128)(2,1)S(1)}, bf16[31,128,128]{2,1,0:T(8,128)(2,1)S(1)}, u32[]{:S(2)}, u32[]{:S(2)}) collective-permute-start(bf16[31,128,128]{2,1,0:T(8,128)(2,1)S(1)} %get-tuple-element.26.near), channel_id=1, source_target_pairs={{0,1},{1,0},{2,3},{3,2},{4,5},{5,4},{6,7},{7,6},{8,9},{9,8},{10,11... | collective-permute-start | bytes 3047432 | tf_op jit(solution)/shard_map/ppermute | solution.py:498
  4.0 5.2 %collective-permute-start.1 = (bf16[20,128,128]{2,1,0:T(8,128)(2,1)S(1)}, bf16[20,128,128]{2,1,0:T(8,128)(2,1)S(1)}, u32[]{:S(2)}, u32[]{:S(2)}) collective-permute-start(bf16[20,128,128]{2,1,0:T(8,128)(2,1)S(1)} %get-tuple-element.27.far), channel_id=1, source_target_pairs={{1,2},{2,1},{3,4},{4,3},{5,6},{6,5},{9,10},{10,9},{11,12},{12,11},... | collective-permute-start | bytes 1966088 | tf_op jit(solution)/shard_map/ppermute | solution.py:496
  4.7 4.5 %collective-permute-start.2 = (bf16[2,2,128,128]{3,2,1,0:T(8,128)(2,1)S(1)}, bf16[2,2,128,128]{3,2,1,0:T(8,128)(2,1)S(1)}, u32[]{:S(2)}, u32[]{:S(2)}) collective-permute-start(bf16[2,2,128,128]{3,2,1,0:T(8,128)(2,1)S(1)} %get-tuple-element.29), channel_id=1, source_target_pairs={{7,8},{8,7},{15,16},{16,15},{23,24},{24,23}} | collective-permute-start | bytes 393224 | tf_op jit(solution)/shard_map/ppermute | solution.py:497
  9.1 2.1 %copy-start = (bf16[3,256,256]{2,1,0:T(8,128)(2,1)}, bf16[3,256,256]{2,1,0:T(8,128)(2,1)S(1)}, u32[]{:S(2)}) copy-start(bf16[3,256,256]{2,1,0:T(8,128)(2,1)S(1)} %get-tuple-element.34.refs_0_.d_near) | copy-start | bytes 1179652
  11.2 0.7 %copy-start.2 = (bf16[3,256,256]{2,1,0:T(8,128)(2,1)}, bf16[3,256,256]{2,1,0:T(8,128)(2,1)S(1)}, u32[]{:S(2)}) copy-start(bf16[3,256,256]{2,1,0:T(8,128)(2,1)S(1)} %get-tuple-element.38.d_far) | copy-start | bytes 1179652
  12.0 0.8 %copy-start.5 = (bf16[3,256,256]{2,1,0:T(8,128)(2,1)}, bf16[3,256,256]{2,1,0:T(8,128)(2,1)S(1)}, u32[]{:S(2)}) copy-start(bf16[3,256,256]{2,1,0:T(8,128)(2,1)S(1)} %get-tuple-element.37.z_far) | copy-start | bytes 1179652
  12.8 1.4 %copy-start.14 = (f32[32,1,128]{2,1,0:T(1,128)}, f32[32,1,128]{2,1,0:T(1,128)S(1)}, u32[]{:S(2)}) copy-start(f32[32,1,128]{2,1,0:T(1,128)S(1)} %get-tuple-element.42) | copy-start | bytes 49156
  12.8 24.3 %collective-permute-start.3 = (bf16[2,256,256]{2,1,0:T(8,128)(2,1)}, bf16[2,256,256]{2,1,0:T(8,128)(2,1)}, u32[]{:S(2)}, u32[]{:S(2)}) collective-permute-start(bf16[2,256,256]{2,1,0:T(8,128)(2,1)} %get-tuple-element.39), channel_id=1, source_target_pairs={{1,2},{2,1},{3,4},{4,3},{5,6},{6,5},{7,8},{8,7},{9,10},{10,9},{11,... | collective-permute-start | bytes 786440 | tf_op jit(solution)/shard_map/ppermute | solution.py:506
  14.1 22.9 %all-to-all-start = ((f32[32,1,128]{2,1,0:T(1,128)}), f32[32,1,128]{2,1,0:T(1,128)S(1)}, u32[]{:S(2)}, u32[]{:S(2)}) async-start(f32[32,1,128]{2,1,0:T(1,128)} %copy-done.14), calls=%async_computation | async-start | bytes 32768 | tf_op jit(solution)/shard_map/all_to_all | solution.py:507
  29.9 1.0 %copy-start.1 = (bf16[3,256,256]{2,1,0:T(8,128)(2,1)S(1)}, bf16[3,256,256]{2,1,0:T(8,128)(2,1)}, u32[]{:S(2)}) copy-start(bf16[3,256,256]{2,1,0:T(8,128)(2,1)} %copy-done) | copy-start | bytes 1179652
  30.9 1.0 %copy-start.3 = (bf16[3,256,256]{2,1,0:T(8,128)(2,1)S(1)}, bf16[3,256,256]{2,1,0:T(8,128)(2,1)}, u32[]{:S(2)}) copy-start(bf16[3,256,256]{2,1,0:T(8,128)(2,1)} %copy-done.2) | copy-start | bytes 1179652
  31.9 1.0 %copy-start.6 = (bf16[3,256,256]{2,1,0:T(8,128)(2,1)S(1)}, bf16[3,256,256]{2,1,0:T(8,128)(2,1)}, u32[]{:S(2)}) copy-start(bf16[3,256,256]{2,1,0:T(8,128)(2,1)} %copy-done.5) | copy-start | bytes 1179652
  34.7 0.9 %copy-start.8 = (f32[3,256,256]{2,1,0:T(8,128)}, f32[3,256,256]{2,1,0:T(8,128)S(1)}, u32[]{:S(2)}) copy-start(f32[3,256,256]{2,1,0:T(8,128)S(1)} %get-tuple-element.40.base) | copy-start | bytes 2359300
  35.6 0.9 %copy-start.10 = (f32[3,256,256]{2,1,0:T(8,128)}, f32[3,256,256]{2,1,0:T(8,128)S(1)}, u32[]{:S(2)}) copy-start(f32[3,256,256]{2,1,0:T(8,128)S(1)} %get-tuple-element.41.e_part) | copy-start | bytes 2359300
  37.1 1.0 %copy-start.4 = (bf16[3,256,256]{2,1,0:T(8,128)(2,1)S(1)}, bf16[3,256,256]{2,1,0:T(8,128)(2,1)}, u32[]{:S(2)}) copy-start(bf16[3,256,256]{2,1,0:T(8,128)(2,1)} %copy-done.2) | copy-start | bytes 1179652
  38.1 1.0 %copy-start.7 = (bf16[3,256,256]{2,1,0:T(8,128)(2,1)S(1)}, bf16[3,256,256]{2,1,0:T(8,128)(2,1)}, u32[]{:S(2)}) copy-start(bf16[3,256,256]{2,1,0:T(8,128)(2,1)} %copy-done.5) | copy-start | bytes 1179652
  39.1 1.1 %copy-start.9 = (f32[3,256,256]{2,1,0:T(8,128)S(1)}, f32[3,256,256]{2,1,0:T(8,128)}, u32[]{:S(2)}) copy-start(f32[3,256,256]{2,1,0:T(8,128)} %copy-done.8) | copy-start | bytes 2359300
  40.2 1.1 %copy-start.11 = (f32[3,256,256]{2,1,0:T(8,128)S(1)}, f32[3,256,256]{2,1,0:T(8,128)}, u32[]{:S(2)}) copy-start(f32[3,256,256]{2,1,0:T(8,128)} %copy-done.10) | copy-start | bytes 2359300

commit v5 on v4

--- a/solution.py
+++ b/solution.py
@@ -325,7 +325,7 @@
 def outer_kernel(
     z, pattern, far, cross, z_cols, turned, p_part, d_part, squares, *refs
 ):
-    d_far, d_out, z_far, spread, s_far = refs[-5:]
+    d_far, d_out, z_far, all_squares, s_far = refs[-5:]
     _, far_first = half_starts(z)
     kind = far.dtype
 
@@ -356,11 +356,7 @@
         if e < 2:
             d_out[e] = value
         total = total + sum_squares(z, value)
-    lanes = jnp.sum(total, axis=0, keepdims=True)
-    folded = lanes[:, : z.block]
-    for t in range(1, z.half):
-        folded = folded + lanes[:, t * z.block : (t + 1) * z.block]
-    spread[...] = jnp.broadcast_to(folded[None], spread.shape)
+    all_squares[...] = total
 
 
 def outer_step(z, pattern, far, cross, z_cols, turned, p_part, d_part, squares, held):
@@ -371,7 +367,7 @@
             z.tiles(3, kind),
             z.tiles(2, kind),
             z.tiles(3, kind),
-            jax.ShapeDtypeStruct((z.devices, 1, z.block), jnp.float32),
+            jax.ShapeDtypeStruct(squares.shape, jnp.float32),
         ),
         in_specs=[SMEM] + [VMEM] * (7 + len(held)),
         out_specs=(VMEM,) * 4,
@@ -383,9 +379,14 @@
 
 
 def middle_kernel(
-    z, z_cols, z_far, d_far, d_near, base_near, e_near, mask_near, refined, base, e_part, square, tiles,
-    cells, sem,
+    z, squares, z_cols, z_far, d_far, d_near, base_near, e_near, mask_near, refined, base, e_part, spread,
+    square, tiles, cells, sem,
 ):
+    lanes = jnp.sum(squares[...], axis=0, keepdims=True)
+    folded = lanes[:, : z.block]
+    for t in range(1, z.half):
+        folded = folded + lanes[:, t * z.block : (t + 1) * z.block]
+    spread[...] = jnp.broadcast_to(folded[None], spread.shape)
     near_first, _ = half_starts(z)
     factor = (z_far, z_cols.at[0], z_cols.at[1], z_cols.at[2])
     defect = (None, d_far, d_near)
@@ -406,7 +407,7 @@
     copy.wait()
 
 
-def middle_step(z, z_cols, z_far, d_far, d_near, base_near, e_near, mask_near):
+def middle_step(z, squares, z_cols, z_far, d_far, d_near, base_near, e_near, mask_near):
     kind = z_far.dtype
     shape = (z.columns, z.offsets, z.block, z.block)
     return pl.pallas_call(
@@ -415,9 +416,10 @@
             jax.ShapeDtypeStruct(shape, kind),
             z.tiles(3, jnp.float32),
             z.tiles(3, jnp.float32),
+            jax.ShapeDtypeStruct((z.devices, 1, z.block), jnp.float32),
         ),
-        in_specs=[VMEM] * 7,
-        out_specs=(HBM, VMEM, VMEM),
+        in_specs=[VMEM] * 8,
+        out_specs=(HBM, VMEM, VMEM, VMEM),
         scratch_shapes=[
             pltpu.VMEM((3, z.tile, z.tile), kind),
             pltpu.VMEM((3, z.tile, z.tile), jnp.float32),
@@ -427,7 +429,7 @@
         compiler_params=PARAMS,
         cost_estimate=z.cost(21, 6),
         name="middle",
-    )(z_cols, z_far, d_far, d_near, base_near, e_near, mask_near)
+    )(squares, z_cols, z_far, d_far, d_near, base_near, e_near, mask_near)
 
 
 def last_kernel(
@@ -500,14 +502,14 @@
         z, pattern, near, far, beside
     )
     held = (d_near, base_near, e_near, mask_near, mask_far)
-    d_far, d_out, z_far, spread = outer_step(
+    d_far, d_out, z_far, squares = outer_step(
         z, pattern, beyond, across, z_cols, turned, p_part, d_part, squares, held
     )
     d_in = lax.ppermute(d_out, AXES, swaps(far_pairs))
+    refined, base, e_part, spread = middle_step(
+        z, squares, z_cols, z_far, d_far, d_near, base_near, e_near, mask_near
+    )
     gathered = lax.all_to_all(spread, AXES, 0, 0, tiled=True)
-    refined, base, e_part = middle_step(
-        z, z_cols, z_far, d_far, d_near, base_near, e_near, mask_near
-    )
     refined, norm = last_step(
         z, z_cols, z_far, d_far, d_in, base, e_part, mask_far, gathered, refined
     )

time: 44.8 us -> 38.7 us (0.86)
  blocking collectives: 0 us -> 23.4 us
  starting transfers between devices: 19 us -> 2.55 us
  local copies, waits for them, and re-layouts: 11.8 us -> 1.21 us
  Pallas kernels: 11.3 us -> 9.67 us
  waiting for transfers between devices: 1.4 us -> 0.87 us
    all_to_all x0 -> x1, blocking collectives: none -> 23.4 us  [per_device(): gathered = lax.all_to_all(spread, AXES, 0, 0, tiled=True)]
    all_to_all x1 -> x0, starting transfers between devices: 15.8 us -> none  [per_device(): gathered = lax.all_to_all(spread, AXES, 0, 0, tiled=True)]
    unnamed x32 -> x6, local copies, waits for them, and re-layouts: 11.8 us -> 1.21 us
    pallas_call x1, Pallas kernels: 2.95 us -> 2.01 us  [last_step(): pl.pallas_call(functools.partial(last_kernel, z), out_shape=(jax.ShapeDty...]
    pallas_call x1, Pallas kernels: 2.03 us -> 1.32 us  [outer_step(): pl.pallas_call(functools.partial(outer_kernel, z), out_shape=(z.tiles(3,...]
    ppermute x1, starting transfers between devices: 1.36 us -> 0.68 us  [per_device(): d_in = lax.ppermute(d_out, AXES, swaps(far_pairs))]
    all_to_all x1 -> x0, waiting for transfers between devices: 0.53 us -> none  [per_device(): gathered = lax.all_to_all(spread, AXES, 0, 0, tiled=True)]
  transfers between devices with their start and end apart: 5 -> 4, of which waited for: 2 -> 1; matrix products, arithmetic and copies ran while one was open for 0% -> 0% of each run, Pallas kernels for 11% -> 12%
where the time goes in v5:
time: 38.7 us; the launch traced here: 38.5 us
  blocking collectives  23.4 us (60%)
  Pallas kernels  9.67 us (25%)
  starting transfers between devices  2.55 us (7%)
  local copies, waits for them, and re-layouts  1.21 us (3%)
  waiting for transfers between devices  0.87 us (2%)
  between operations  0.74 us (2%)
    all_to_all x1, blocking collectives, per_device(): gathered = lax.all_to_all(spread, AXES, 0, 0, tiled=True)  23.4 us
    pallas_call x1, Pallas kernels, inner_step(): pl.pallas_call(functools.partial(inner_kernel, z), out_shape=(jax.ShapeDt...  2.96 us
    pallas_call x1, Pallas kernels, last_step(): pl.pallas_call(functools.partial(last_kernel, z), out_shape=(jax.ShapeDty...  2.01 us
    pallas_call x1, Pallas kernels, middle_step(): pl.pallas_call(functools.partial(middle_kernel, z), out_shape=(jax.ShapeD...  1.81 us
    pallas_call x1, Pallas kernels, outer_step(): pl.pallas_call(functools.partial(outer_kernel, z), out_shape=(z.tiles(3,...  1.32 us
    unnamed x6, local copies, waits for them, and re-layouts  1.21 us
    pallas_call x1, Pallas kernels, pack(): pl.pallas_call(functools.partial(pack_kernel, z), out_shape=(jax.ShapeDty...  0.93 us
    ppermute x1, waiting for transfers between devices, per_device(): beside = lax.ppermute(near, AXES, swaps(near_pairs))  0.86 us
  transfers between devices with their start and end apart: 4, of which 1 were waited for; matrix products, arithmetic and copies ran while one was open for 0% of the time, Pallas kernels for 12%

profile of v5, /device:TPU:0, one launch (start us, length us, event | category | flops | bytes accessed | tf_op | source)
XLA Modules:
  0.0 38.5 jit_solution(2048849406298460463)
XLA Ops:
  0.6 0.0 copy-start
  0.6 0.0 copy-start.2
  0.6 0.7 %copy-done.2 = s32[4,5]{1,0:T(4,128)S(1)} copy-done((s32[4,5]{1,0:T(4,128)S(1)}, s32[4,5]{1,0:T(4,128)}, u32[]{:S(2)}) %copy-start.2) | copy-done | bytes 104
  1.4 0.0 copy-start.1
  1.4 0.7 %masks.1 = (bf16[3,256,256]{2,1,0:T(8,128)(2,1)S(1)}, bf16[3,256,256]{2,1,0:T(8,128)(2,1)S(1)}) custom-call(s32[4,5]{1,0:T(4,128)S(1)} %copy-done.2), custom_call_target="tpu_custom_call" | custom-call | flops 671088640 | bytes 1048576 | tf_op jit(solution)/shard_map/masks/pallas_call | solution.py:151
  2.0 0.0 copy-done
  2.1 0.5 %copy-done.1 = bf16[4,5,128,128]{3,2,1,0:T(8,128)(2,1)S(1)} copy-done((bf16[4,5,128,128]{3,2,1,0:T(8,128)(2,1)S(1)}, bf16[4,5,128,128]{3,2,1,0:T(8,128)(2,1)}, u32[]{:S(2)}) %copy-start.1) | copy-done | bytes 655384
  2.5 0.9 %pack.1 = (bf16[31,128,128]{2,1,0:T(8,128)(2,1)S(1)}, bf16[20,128,128]{2,1,0:T(8,128)(2,1)S(1)}, bf16[2,2,128,128]{3,2,1,0:T(8,128)(2,1)S(1)}) custom-call(bf16[4,5,128,128]{3,2,1,0:T(8,128)(2,1)S(1)} %copy-done, bf16[4,5,128,128]{3,2,1,0:T(8,128)(2,1)S(1)} %copy-done.1, s32[4,5]{1,0:T(4,128)S(1)} %copy-done.2, ...), custom_call_target="tpu_custom_call" | custom-call | tf_op jit(solution)/shard_map/pack/pallas_call | solution.py:198
  3.5 0.5 %collective-permute-start = (bf16[31,128,128]{2,1,0:T(8,128)(2,1)S(1)}, bf16[31,128,128]{2,1,0:T(8,128)(2,1)S(1)}, u32[]{:S(2)}, u32[]{:S(2)}) collective-permute-start(bf16[31,128,128]{2,1,0:T(8,128)(2,1)S(1)} %get-tuple-element.27.near), channel_id=1, source_target_pairs={{0,1},{1,0},{2,3},{3,2},{4,5},{5,4},{6,7},{7,6},{8,9},{9,8},{10,11... | collective-permute-start | bytes 3047432 | tf_op jit(solution)/shard_map/ppermute | solution.py:500
  4.0 0.7 %collective-permute-start.1 = (bf16[20,128,128]{2,1,0:T(8,128)(2,1)S(1)}, bf16[20,128,128]{2,1,0:T(8,128)(2,1)S(1)}, u32[]{:S(2)}, u32[]{:S(2)}) collective-permute-start(bf16[20,128,128]{2,1,0:T(8,128)(2,1)S(1)} %get-tuple-element.28.far), channel_id=1, source_target_pairs={{1,2},{2,1},{3,4},{4,3},{5,6},{6,5},{9,10},{10,9},{11,12},{12,11},... | collective-permute-start | bytes 1966088 | tf_op jit(solution)/shard_map/ppermute | solution.py:498
  4.7 0.7 %collective-permute-start.2 = (bf16[2,2,128,128]{3,2,1,0:T(8,128)(2,1)S(1)}, bf16[2,2,128,128]{3,2,1,0:T(8,128)(2,1)S(1)}, u32[]{:S(2)}, u32[]{:S(2)}) collective-permute-start(bf16[2,2,128,128]{3,2,1,0:T(8,128)(2,1)S(1)} %get-tuple-element.30), channel_id=1, source_target_pairs={{7,8},{8,7},{15,16},{16,15},{23,24},{24,23}} | collective-permute-start | bytes 393224 | tf_op jit(solution)/shard_map/ppermute | solution.py:499
  5.4 0.9 %collective-permute-done.beside = bf16[31,128,128]{2,1,0:T(8,128)(2,1)S(1)} collective-permute-done((bf16[31,128,128]{2,1,0:T(8,128)(2,1)S(1)}, bf16[31,128,128]{2,1,0:T(8,128)(2,1)S(1)}, u32[]{:S(2)}, u32[]{:S(2)}) %collective-permute-start) | collective-permute-done | bytes 1015840 | tf_op jit(solution)/shard_map/ppermute | solution.py:500
  6.2 3.0 %inner.1 = (bf16[3,3,256,256]{3,2,1,0:T(8,128)(2,1)S(1)}, bf16[3,256,256]{2,1,0:T(8,128)(2,1)S(1)}, f32[2,256,256]{2,1,0:T(8,128)S(1)}, f32[2,256,256]{2,1,0:T(8...) custom-call(s32[4,5]{1,0:T(4,128)S(1)} %copy-done.2, ...), custom_call_target="tpu_custom_call" | custom-call | flops 1811939328 | bytes 8388608 | tf_op jit(solution)/shard_map/inner/pallas_call | solution.py:299
  9.2 0.0 collective-permute-done.2.cross
  9.2 0.0 collective-permute-done.1.far
  9.2 1.3 %outer.1 = (bf16[3,256,256]{2,1,0:T(8,128)(2,1)S(1)}, bf16[2,256,256]{2,1,0:T(8,128)(2,1)S(1)}, bf16[3,256,256]{2,1,0:T(8,128)(2,1)S(1)}, f32[8,256]{1,0:T(8,128)S(1)}) custom-call(s32[4,5]{1,0:T(4,128)S(1)} %copy-done.2, bf16[20,128,128]{2,1,0:T(8,128)(2,1)S(1)} %collective-permute-done.1.far, bf16[2,2,128,128]{3,2,1,0:T(8,128)(2,1)S(1)} %collective-permute-done.2.cross, ...), custom_call_target="tpu_custom_call" | custom-call | flops 301989888 | bytes 4194304 | tf_op jit(solution)/shard_map/outer/pallas_call | solution.py:364
  10.5 0.7 %collective-permute-start.3 = (bf16[2,256,256]{2,1,0:T(8,128)(2,1)S(1)}, bf16[2,256,256]{2,1,0:T(8,128)(2,1)S(1)}, u32[]{:S(2)}, u32[]{:S(2)}) collective-permute-start(bf16[2,256,256]{2,1,0:T(8,128)(2,1)S(1)} %get-tuple-element.40), channel_id=1, source_target_pairs={{1,2},{2,1},{3,4},{4,3},{5,6},{6,5},{7,8},{8,7},{9,10},{10,9},{11,... | collective-permute-start | bytes 786440 | tf_op jit(solution)/shard_map/ppermute | solution.py:508
  11.2 1.8 %middle.1 = (bf16[4,5,128,128]{3,2,1,0:T(8,128)(2,1)}, f32[3,256,256]{2,1,0:T(8,128)S(1)}, f32[3,256,256]{2,1,0:T(8,128)S(1)}, f32[32,1,128]{2,1,0:T(1,128)S(1)}) custom-call(f32[8,256]{1,0:T(8,128)S(1)} %get-tuple-element.41.squares, bf16[3,3,256,256]{3,2,1,0:T(8,128)(2,1)S(1)} %get-tuple-element.29.z_cols, ...), custom_call_target="tpu_custom_call" | custom-call | flops 704643072 | bytes 6291456 | tf_op jit(solution)/shard_map/middle/pallas_call | solution.py:413
  13.0 23.4 %all_to_all.5.gathered = f32[32,1,128]{2,1,0:T(1,128)S(1)} all-to-all(f32[32,1,128]{2,1,0:T(1,128)S(1)} %get-tuple-element.44), channel_id=1, replica_groups=mesh['grp'=4,'slab'=8] {'grp','slab'}, dimensions={0} | all-to-all | bytes 32768 | tf_op jit(solution)/shard_map/all_to_all | solution.py:512
  36.4 0.0 collective-permute-done.3.d_in
  36.4 2.0 %last.1 = (bf16[4,5,128,128]{3,2,1,0:T(8,128)(2,1)}, f32[1,128]{1,0:T(1,128)}) custom-call(bf16[3,3,256,256]{3,2,1,0:T(8,128)(2,1)S(1)} %get-tuple-element.29.z_cols, bf16[3,256,256]{2,1,0:T(8,128)(2,1)S(1)} %get-tuple-element.38.z_far, bf16[3,256,256]{2,1,0:T(8,128)(2,1)S(1)} %get-tuple-element.39.d_far, ...), custom_call_target="tpu_custom_call", output_to_operand_aliasing={{0}: (8, {})} | custom-call | flops 301989888 | bytes 4194304 | tf_op jit(solution)/shard_map/last/pallas_call | solution.py:461
Async XLA Ops:
  0.6 1.4 %copy-start = (bf16[4,5,128,128]{3,2,1,0:T(8,128)(2,1)S(1)}, bf16[4,5,128,128]{3,2,1,0:T(8,128)(2,1)}, u32[]{:S(2)}) copy-start(bf16[4,5,128,128]{3,2,1,0:T(8,128)(2,1)} %margin.1) | copy-start | bytes 1966084
  0.6 0.7 %copy-start.2 = (s32[4,5]{1,0:T(4,128)S(1)}, s32[4,5]{1,0:T(4,128)}, u32[]{:S(2)}) copy-start(s32[4,5]{1,0:T(4,128)} %pattern.7) | copy-start | bytes 244
  1.4 1.1 %copy-start.1 = (bf16[4,5,128,128]{3,2,1,0:T(8,128)(2,1)S(1)}, bf16[4,5,128,128]{3,2,1,0:T(8,128)(2,1)}, u32[]{:S(2)}) copy-start(bf16[4,5,128,128]{3,2,1,0:T(8,128)(2,1)} %factor.1) | copy-start | bytes 1966084
  3.5 2.8 %collective-permute-start = (bf16[31,128,128]{2,1,0:T(8,128)(2,1)S(1)}, bf16[31,128,128]{2,1,0:T(8,128)(2,1)S(1)}, u32[]{:S(2)}, u32[]{:S(2)}) collective-permute-start(bf16[31,128,128]{2,1,0:T(8,128)(2,1)S(1)} %get-tuple-element.27.near), channel_id=1, source_target_pairs={{0,1},{1,0},{2,3},{3,2},{4,5},{5,4},{6,7},{7,6},{8,9},{9,8},{10,11... | collective-permute-start | bytes 3047432 | tf_op jit(solution)/shard_map/ppermute | solution.py:500
  4.0 5.2 %collective-permute-start.1 = (bf16[20,128,128]{2,1,0:T(8,128)(2,1)S(1)}, bf16[20,128,128]{2,1,0:T(8,128)(2,1)S(1)}, u32[]{:S(2)}, u32[]{:S(2)}) collective-permute-start(bf16[20,128,128]{2,1,0:T(8,128)(2,1)S(1)} %get-tuple-element.28.far), channel_id=1, source_target_pairs={{1,2},{2,1},{3,4},{4,3},{5,6},{6,5},{9,10},{10,9},{11,12},{12,11},... | collective-permute-start | bytes 1966088 | tf_op jit(solution)/shard_map/ppermute | solution.py:498
  4.7 4.5 %collective-permute-start.2 = (bf16[2,2,128,128]{3,2,1,0:T(8,128)(2,1)S(1)}, bf16[2,2,128,128]{3,2,1,0:T(8,128)(2,1)S(1)}, u32[]{:S(2)}, u32[]{:S(2)}) collective-permute-start(bf16[2,2,128,128]{3,2,1,0:T(8,128)(2,1)S(1)} %get-tuple-element.30), channel_id=1, source_target_pairs={{7,8},{8,7},{15,16},{16,15},{23,24},{24,23}} | collective-permute-start | bytes 393224 | tf_op jit(solution)/shard_map/ppermute | solution.py:499
  10.5 25.9 %collective-permute-start.3 = (bf16[2,256,256]{2,1,0:T(8,128)(2,1)S(1)}, bf16[2,256,256]{2,1,0:T(8,128)(2,1)S(1)}, u32[]{:S(2)}, u32[]{:S(2)}) collective-permute-start(bf16[2,256,256]{2,1,0:T(8,128)(2,1)S(1)} %get-tuple-element.40), channel_id=1, source_target_pairs={{1,2},{2,1},{3,4},{4,3},{5,6},{6,5},{7,8},{8,7},{9,10},{10,9},{11,... | collective-permute-start | bytes 786440 | tf_op jit(solution)/shard_map/ppermute | solution.py:508

commit v6 on v5

--- a/solution.py
+++ b/solution.py
@@ -379,17 +379,43 @@
 
 
 def middle_kernel(
-    z, squares, z_cols, z_far, d_far, d_near, base_near, e_near, mask_near, refined, base, e_part, spread,
-    square, tiles, cells, sem,
+    z, squares, z_cols, z_far, d_far, d_near, base_near, e_near, mask_near, mask_far, refined, narrow, wide,
+    spread, square, done, parts, tiles, cells, sems,
 ):
+    near_first, _ = half_starts(z)
+    moves = [
+        (z_far.at[pl.ds(1, 2)], narrow.at[pl.ds(0, 2)]),
+        (z_cols.at[0], narrow.at[pl.ds(2, 3)]),
+        (z_cols.at[1, pl.ds(0, 2)], narrow.at[pl.ds(5, 2)]),
+        (d_far.at[pl.ds(0, 1)], narrow.at[pl.ds(7, 1)]),
+    ]
+    copies = [
+        pltpu.make_async_copy(source, target, sems.at[k]) for k, (source, target) in enumerate(moves)
+    ]
+    for copy in copies:
+        copy.start()
+
+    def send(source, target):
+        copies.append(pltpu.make_async_copy(source, target, sems.at[len(copies)]))
+        copies[-1].start()
+
     lanes = jnp.sum(squares[...], axis=0, keepdims=True)
     folded = lanes[:, : z.block]
     for t in range(1, z.half):
         folded = folded + lanes[:, t * z.block : (t + 1) * z.block]
     spread[...] = jnp.broadcast_to(folded[None], spread.shape)
-    near_first, _ = half_starts(z)
     factor = (z_far, z_cols.at[0], z_cols.at[1], z_cols.at[2])
     defect = (None, d_far, d_near)
+    value = tile_product(defect, d_far, 2, 1, 1, 2) * mask_far[2].astype(jnp.float32)
+    done[0] = value.astype(done.dtype)
+    send(done, narrow.at[pl.ds(8, 1)])
+    for i in (0, 1):
+        parts[i] = tile_product(defect, d_far, i, 1, 1, 2)
+    for i in (0, 1, 2):
+        parts[2 + i] = z_cols[0, i].astype(jnp.float32) + 0.5 * tile_product(
+            factor, d_far, i, 1, 0, 2
+        )
+    send(parts, wide)
     for i in (1, 2, 3):
         value = e_near[i - 1]
         if i < 3:
@@ -399,84 +425,119 @@
         value = base_near[i - 1] + 0.375 * tile_product(factor, square, i, 2, 1, 3)
         tiles[i - 1] = value * mask_near[i - 1].astype(jnp.float32)
     store_half(z, tiles, cells)
-    copy = pltpu.make_async_copy(cells, refined.at[pl.ds(near_first, z.half)], sem)
-    copy.start()
-    for i in (0, 1, 2):
-        base[i] = z_cols[0, i].astype(jnp.float32) + 0.5 * tile_product(factor, d_far, i, 1, 0, 2)
-        e_part[i] = tile_product(defect, d_far, i, 1, 1, 2)
-    copy.wait()
-
-
-def middle_step(z, squares, z_cols, z_far, d_far, d_near, base_near, e_near, mask_near):
+    send(cells, refined.at[pl.ds(near_first, z.half)])
+    for copy in copies:
+        copy.wait()
+
+
+def middle_step(z, squares, z_cols, z_far, d_far, d_near, base_near, e_near, mask_near, mask_far):
     kind = z_far.dtype
     shape = (z.columns, z.offsets, z.block, z.block)
     return pl.pallas_call(
         functools.partial(middle_kernel, z),
         out_shape=(
             jax.ShapeDtypeStruct(shape, kind),
-            z.tiles(3, jnp.float32),
-            z.tiles(3, jnp.float32),
+            z.tiles(9, kind),
+            z.tiles(5, jnp.float32),
             jax.ShapeDtypeStruct((z.devices, 1, z.block), jnp.float32),
         ),
-        in_specs=[VMEM] * 8,
-        out_specs=(HBM, VMEM, VMEM, VMEM),
+        in_specs=[VMEM] * 9,
+        out_specs=(HBM, HBM, HBM, VMEM),
         scratch_shapes=[
             pltpu.VMEM((3, z.tile, z.tile), kind),
+            pltpu.VMEM((1, z.tile, z.tile), kind),
+            pltpu.VMEM((5, z.tile, z.tile), jnp.float32),
             pltpu.VMEM((3, z.tile, z.tile), jnp.float32),
             pltpu.VMEM((z.half,) + shape[1:], kind),
-            pltpu.SemaphoreType.DMA(()),
+            pltpu.SemaphoreType.DMA((7,)),
         ],
         compiler_params=PARAMS,
         cost_estimate=z.cost(21, 6),
         name="middle",
-    )(squares, z_cols, z_far, d_far, d_near, base_near, e_near, mask_near)
+    )(squares, z_cols, z_far, d_far, d_near, base_near, e_near, mask_near, mask_far)
 
 
 def last_kernel(
-    z, z_cols, z_far, d_far, d_in, base, e_part, mask_far, gathered, _, refined, norm, square, tiles,
-    cells, sem,
+    z, pattern_in, narrow_in, wide_in, d_in, _, refined, _narrow, _wide, _d, pattern, narrow, wide, d_far,
+    square, tiles, cells, sems,
 ):
-    _, far_first = half_starts(z)
-    factor = (z_far, z_cols.at[0], z_cols.at[1])
-    values = (
-        e_part[0] + dot(d_in[1], d_far[0]),
-        e_part[1] + dot(d_in[0], d_far[0]),
-        e_part[2],
-    )
-    for i, value in enumerate(values):
-        square[i] = (value * mask_far[i].astype(jnp.float32)).astype(square.dtype)
+    _, first = half_starts(z)
+    link = pl.ds(7, 2)
+    factor = pl.ds(0, 7)
+    moves = (
+        (pattern_in, pattern),
+        (d_in, d_far),
+        (narrow_in.at[link], narrow.at[link]),
+        (wide_in.at[pl.ds(0, 2)], wide.at[pl.ds(0, 2)]),
+        (narrow_in.at[factor], narrow.at[factor]),
+        (wide_in.at[pl.ds(2, 3)], wide.at[pl.ds(2, 3)]),
+    )
+    copies = [
+        pltpu.make_async_copy(source, target, sems.at[k]) for k, (source, target) in enumerate(moves)
+    ]
+    for copy in copies:
+        copy.start()
+    for copy in copies[:4]:
+        copy.wait()
+    for i in (0, 1):
+        value = wide[i] + dot(d_far[1 - i], narrow[7])
+        square[i] = own_masked(z, pattern, first, i, value).astype(square.dtype)
+    square[2] = narrow[8]
+    for copy in copies[4:]:
+        copy.wait()
+    base = (-1, 2, 5)
     for i in (0, 1, 2):
-        value = base[i] + 0.375 * tile_product(factor, square, i, 1, 0, 2)
-        tiles[i] = value * mask_far[i].astype(jnp.float32)
+        total = None
+        for k in range(max(0, i - 1), min(2, i + 1) + 1):
+            term = dot(narrow[base[k] + i - k + 1], square[k])
+            total = term if total is None else total + term
+        tiles[i] = own_masked(z, pattern, first, i, wide[2 + i] + 0.375 * total)
     store_half(z, tiles, cells)
-    copy = pltpu.make_async_copy(cells, refined.at[pl.ds(far_first, z.half)], sem)
+    copy = pltpu.make_async_copy(cells, refined.at[pl.ds(first, z.half)], sems.at[6])
     copy.start()
-    mean = jnp.sum(gathered[...]) * (1.0 / z.entries)
-    norm[...] = jnp.sqrt(jnp.full(norm.shape, mean, jnp.float32))
     copy.wait()
 
 
-def last_step(z, z_cols, z_far, d_far, d_in, base, e_part, mask_far, gathered, refined):
+def last_step(z, pattern, narrow, wide, d_in, refined):
     kind = refined.dtype
     return pl.pallas_call(
         functools.partial(last_kernel, z),
-        out_shape=(
-            jax.ShapeDtypeStruct(refined.shape, kind),
-            jax.ShapeDtypeStruct((1, z.block), jnp.float32),
+        out_shape=tuple(
+            jax.ShapeDtypeStruct(held.shape, held.dtype) for held in (refined, narrow, wide, d_in)
         ),
-        in_specs=[VMEM] * 8 + [HBM],
-        out_specs=(HBM, VMEM),
+        in_specs=[HBM] * 5,
+        out_specs=(HBM,) * 4,
         scratch_shapes=[
+            pltpu.SMEM(pattern.shape, pattern.dtype),
+            pltpu.VMEM(narrow.shape, kind),
+            pltpu.VMEM(wide.shape, jnp.float32),
+            pltpu.VMEM(d_in.shape, kind),
             pltpu.VMEM((3, z.tile, z.tile), kind),
             pltpu.VMEM((3, z.tile, z.tile), jnp.float32),
             pltpu.VMEM((z.half,) + refined.shape[1:], kind),
-            pltpu.SemaphoreType.DMA(()),
+            pltpu.SemaphoreType.DMA((7,)),
         ],
-        input_output_aliases={8: 0},
+        input_output_aliases={4: 0, 1: 1, 2: 2, 3: 3},
         compiler_params=PARAMS,
         cost_estimate=z.cost(9, 4),
         name="last",
-    )(z_cols, z_far, d_far, d_in, base, e_part, mask_far, gathered, refined)
+    )(pattern, narrow, wide, d_in, refined)[0]
+
+
+def norm_kernel(z, gathered, norm):
+    mean = jnp.sum(gathered[...]) * (1.0 / z.entries)
+    norm[...] = jnp.sqrt(jnp.full(norm.shape, mean, jnp.float32))
+
+
+def norm_step(z, gathered):
+    return pl.pallas_call(
+        functools.partial(norm_kernel, z),
+        out_shape=jax.ShapeDtypeStruct((1, z.block), jnp.float32),
+        in_specs=[VMEM],
+        out_specs=VMEM,
+        compiler_params=PARAMS,
+        name="norm",
+    )(gathered)
 
 
 def swaps(pairs):
@@ -506,13 +567,12 @@
         z, pattern, beyond, across, z_cols, turned, p_part, d_part, squares, held
     )
     d_in = lax.ppermute(d_out, AXES, swaps(far_pairs))
-    refined, base, e_part, spread = middle_step(
-        z, squares, z_cols, z_far, d_far, d_near, base_near, e_near, mask_near
+    refined, narrow, wide, spread = middle_step(
+        z, squares, z_cols, z_far, d_far, d_near, base_near, e_near, mask_near, mask_far
     )
     gathered = lax.all_to_all(spread, AXES, 0, 0, tiled=True)
-    refined, norm = last_step(
-        z, z_cols, z_far, d_far, d_in, base, e_part, mask_far, gathered, refined
-    )
+    refined = last_step(z, pattern, narrow, wide, d_in, refined)
+    norm = norm_step(z, gathered)
     return refined, norm[0, 0]
 
 

time: 38.7 us -> 40.7 us (1.052)
  Pallas kernels: 9.67 us -> 11.7 us
    pallas_call x1, Pallas kernels: 1.81 us -> 3.03 us  [middle_step(): pl.pallas_call(functools.partial(middle_kernel, z), out_shape=(jax.ShapeD...]
    pallas_call x1 -> x2, Pallas kernels: 2.01 us -> 2.82 us  [the longest x1 2.15 us: last_step(): pl.pallas_call(functools.partial(last_kernel, z), out_shape=tuple((jax.Sh...]
    unnamed x6 -> x8, local copies, waits for them, and re-layouts: 1.21 us -> 1.22 us
  transfers between devices with their start and end apart: 4 -> 4, of which waited for: 1 -> 1; matrix products, arithmetic and copies ran while one was open for 0% -> 0% of each run, Pallas kernels for 12% -> 16%
where the time goes in v6:
time: 40.7 us; the launch traced here: 40.5 us
  blocking collectives  23.4 us (57%)
  Pallas kernels  11.7 us (29%)
  starting transfers between devices  2.55 us (6%)
  local copies, waits for them, and re-layouts  1.22 us (3%)
  waiting for transfers between devices  0.87 us (2%)
  between operations  0.74 us (2%)
    all_to_all x1, blocking collectives, per_device(): gathered = lax.all_to_all(spread, AXES, 0, 0, tiled=True)  23.4 us
    pallas_call x1, Pallas kernels, middle_step(): pl.pallas_call(functools.partial(middle_kernel, z), out_shape=(jax.ShapeD...  3.03 us
    pallas_call x1, Pallas kernels, inner_step(): pl.pallas_call(functools.partial(inner_kernel, z), out_shape=(jax.ShapeDt...  2.97 us
    pallas_call x1, Pallas kernels, last_step(): pl.pallas_call(functools.partial(last_kernel, z), out_shape=tuple((jax.Sh...  2.15 us
    pallas_call x1, Pallas kernels, outer_step(): pl.pallas_call(functools.partial(outer_kernel, z), out_shape=(z.tiles(3,...  1.31 us
    unnamed x8, local copies, waits for them, and re-layouts  1.22 us
    pallas_call x1, Pallas kernels, pack(): pl.pallas_call(functools.partial(pack_kernel, z), out_shape=(jax.ShapeDty...  0.93 us
    ppermute x1, waiting for transfers between devices, per_device(): beside = lax.ppermute(near, AXES, swaps(near_pairs))  0.86 us
  transfers between devices with their start and end apart: 4, of which 1 were waited for; matrix products, arithmetic and copies ran while one was open for 0% of the time, Pallas kernels for 16%

profile of v6, /device:TPU:0, one launch (start us, length us, event | category | flops | bytes accessed | tf_op | source)
XLA Modules:
  0.0 40.5 jit_solution(12848350792916525186)
XLA Ops:
  0.6 0.0 copy-start
  0.6 0.0 copy-start.2
  0.7 0.7 %copy-done.2 = s32[4,5]{1,0:T(4,128)S(1)} copy-done((s32[4,5]{1,0:T(4,128)S(1)}, s32[4,5]{1,0:T(4,128)}, u32[]{:S(2)}) %copy-start.2) | copy-done | bytes 104
  1.4 0.0 copy-start.1
  1.4 0.7 %masks.1 = (bf16[3,256,256]{2,1,0:T(8,128)(2,1)S(1)}, bf16[3,256,256]{2,1,0:T(8,128)(2,1)S(1)}) custom-call(s32[4,5]{1,0:T(4,128)S(1)} %copy-done.2), custom_call_target="tpu_custom_call" | custom-call | flops 671088640 | bytes 1048576 | tf_op jit(solution)/shard_map/masks/pallas_call | solution.py:151
  2.0 0.0 copy-done
  2.1 0.5 %copy-done.1 = bf16[4,5,128,128]{3,2,1,0:T(8,128)(2,1)S(1)} copy-done((bf16[4,5,128,128]{3,2,1,0:T(8,128)(2,1)S(1)}, bf16[4,5,128,128]{3,2,1,0:T(8,128)(2,1)}, u32[]{:S(2)}) %copy-start.1) | copy-done | bytes 655384
  2.5 0.9 %pack.1 = (bf16[31,128,128]{2,1,0:T(8,128)(2,1)S(1)}, bf16[20,128,128]{2,1,0:T(8,128)(2,1)S(1)}, bf16[2,2,128,128]{3,2,1,0:T(8,128)(2,1)S(1)}) custom-call(bf16[4,5,128,128]{3,2,1,0:T(8,128)(2,1)S(1)} %copy-done, bf16[4,5,128,128]{3,2,1,0:T(8,128)(2,1)S(1)} %copy-done.1, s32[4,5]{1,0:T(4,128)S(1)} %copy-done.2, ...), custom_call_target="tpu_custom_call" | custom-call | tf_op jit(solution)/shard_map/pack/pallas_call | solution.py:198
  3.5 0.5 %collective-permute-start.2 = (bf16[31,128,128]{2,1,0:T(8,128)(2,1)S(1)}, bf16[31,128,128]{2,1,0:T(8,128)(2,1)S(1)}, u32[]{:S(2)}, u32[]{:S(2)}) collective-permute-start(bf16[31,128,128]{2,1,0:T(8,128)(2,1)S(1)} %get-tuple-element.28.near), channel_id=1, source_target_pairs={{0,1},{1,0},{2,3},{3,2},{4,5},{5,4},{6,7},{7,6},{8,9},{9,8},{10,11... | collective-permute-start | bytes 3047432 | tf_op jit(solution)/shard_map/ppermute | solution.py:561
  4.0 0.7 %collective-permute-start = (bf16[20,128,128]{2,1,0:T(8,128)(2,1)S(1)}, bf16[20,128,128]{2,1,0:T(8,128)(2,1)S(1)}, u32[]{:S(2)}, u32[]{:S(2)}) collective-permute-start(bf16[20,128,128]{2,1,0:T(8,128)(2,1)S(1)} %get-tuple-element.26.far), channel_id=1, source_target_pairs={{1,2},{2,1},{3,4},{4,3},{5,6},{6,5},{9,10},{10,9},{11,12},{12,11},... | collective-permute-start | bytes 1966088 | tf_op jit(solution)/shard_map/ppermute | solution.py:559
  4.7 0.7 %collective-permute-start.1 = (bf16[2,2,128,128]{3,2,1,0:T(8,128)(2,1)S(1)}, bf16[2,2,128,128]{3,2,1,0:T(8,128)(2,1)S(1)}, u32[]{:S(2)}, u32[]{:S(2)}) collective-permute-start(bf16[2,2,128,128]{3,2,1,0:T(8,128)(2,1)S(1)} %get-tuple-element.27), channel_id=1, source_target_pairs={{7,8},{8,7},{15,16},{16,15},{23,24},{24,23}} | collective-permute-start | bytes 393224 | tf_op jit(solution)/shard_map/ppermute | solution.py:560
  5.4 0.9 %collective-permute-done.2.beside = bf16[31,128,128]{2,1,0:T(8,128)(2,1)S(1)} collective-permute-done((bf16[31,128,128]{2,1,0:T(8,128)(2,1)S(1)}, bf16[31,128,128]{2,1,0:T(8,128)(2,1)S(1)}, u32[]{:S(2)}, u32[]{:S(2)}) %collective-permute-start.2) | collective-permute-done | bytes 1015840 | tf_op jit(solution)/shard_map/ppermute | solution.py:561
  6.2 3.0 %inner.1 = (bf16[3,3,256,256]{3,2,1,0:T(8,128)(2,1)S(1)}, bf16[3,256,256]{2,1,0:T(8,128)(2,1)S(1)}, f32[2,256,256]{2,1,0:T(8,128)S(1)}, f32[2,256,256]{2,1,0:T(8...) custom-call(s32[4,5]{1,0:T(4,128)S(1)} %copy-done.2, ...), custom_call_target="tpu_custom_call" | custom-call | flops 1811939328 | bytes 8388608 | tf_op jit(solution)/shard_map/inner/pallas_call | solution.py:299
  9.2 0.0 collective-permute-done.1.cross
  9.2 0.0 collective-permute-done.far
  9.2 1.3 %outer.1 = (bf16[3,256,256]{2,1,0:T(8,128)(2,1)S(1)}, bf16[2,256,256]{2,1,0:T(8,128)(2,1)S(1)}, bf16[3,256,256]{2,1,0:T(8,128)(2,1)S(1)}, f32[8,256]{1,0:T(8,128)S(1)}) custom-call(s32[4,5]{1,0:T(4,128)S(1)} %copy-done.2, bf16[20,128,128]{2,1,0:T(8,128)(2,1)S(1)} %collective-permute-done.far, bf16[2,2,128,128]{3,2,1,0:T(8,128)(2,1)S(1)} %collective-permute-done.1.cross, ...), custom_call_target="tpu_custom_call" | custom-call | flops 301989888 | bytes 4194304 | tf_op jit(solution)/shard_map/outer/pallas_call | solution.py:364
  10.5 0.7 %collective-permute-start.3 = (bf16[2,256,256]{2,1,0:T(8,128)(2,1)S(1)}, bf16[2,256,256]{2,1,0:T(8,128)(2,1)S(1)}, u32[]{:S(2)}, u32[]{:S(2)}) collective-permute-start(bf16[2,256,256]{2,1,0:T(8,128)(2,1)S(1)} %get-tuple-element.42), channel_id=1, source_target_pairs={{1,2},{2,1},{3,4},{4,3},{5,6},{6,5},{7,8},{8,7},{9,10},{10,9},{11,... | collective-permute-start | bytes 786440 | tf_op jit(solution)/shard_map/ppermute | solution.py:569
  11.2 0.0 copy-start.3
  11.2 3.0 %middle.1 = (bf16[4,5,128,128]{3,2,1,0:T(8,128)(2,1)}, bf16[9,256,256]{2,1,0:T(8,128)(2,1)S(1)}, f32[5,256,256]{2,1,0:T(8,128)S(1)}, f32[32,1,128]{2,1,0:T(1,128)S(1)}) custom-call(f32[8,256]{1,0:T(8,128)S(1)} %get-tuple-element.37.squares, bf16[3,3,256,256]{3,2,1,0:T(8,128)(2,1)S(1)} %get-tuple-element.29.z_cols, ...), custom_call_target="tpu_custom_call" | custom-call | flops 704643072 | bytes 6291456 | tf_op jit(solution)/shard_map/middle/pallas_call | solution.py:436
  14.3 23.4 %all_to_all.5.gathered = f32[32,1,128]{2,1,0:T(1,128)S(1)} all-to-all(f32[32,1,128]{2,1,0:T(1,128)S(1)} %get-tuple-element.45), channel_id=1, replica_groups=mesh['grp'=4,'slab'=8] {'grp','slab'}, dimensions={0} | all-to-all | bytes 32768 | tf_op jit(solution)/shard_map/all_to_all | solution.py:573
  37.7 0.7 %norm.1 = f32[1,128]{1,0:T(1,128)} custom-call(f32[32,1,128]{2,1,0:T(1,128)S(1)} %all_to_all.5.gathered), custom_call_target="tpu_custom_call" | custom-call | tf_op jit(solution)/shard_map/norm/pallas_call | solution.py:533
  38.3 0.0 collective-permute-done.3.d_in
  38.3 0.0 copy-done.3
  38.4 2.2 %last.1 = (bf16[4,5,128,128]{3,2,1,0:T(8,128)(2,1)}, bf16[9,256,256]{2,1,0:T(8,128)(2,1)S(1)}, f32[5,256,256]{2,1,0:T(8,128)S(1)}, bf16[2,256,256]{2,1,0:T(8,128)(2,1)S(1)}) custom-call(s32[4,5]{1,0:T(4,128)S(1)} %copy-done.3, ...), custom_call_target="tpu_custom_call", output_to_operand_aliasing={{0}: (4, {}), {1}: (1, {}), {2}: (2, {}), {3}: (3, {})} | custom-call | flops 301989888 | bytes 4194304 | tf_op jit(solution)/shard_map/last/pallas_call | solution.py:503
Async XLA Ops:
  0.6 1.4 %copy-start = (bf16[4,5,128,128]{3,2,1,0:T(8,128)(2,1)S(1)}, bf16[4,5,128,128]{3,2,1,0:T(8,128)(2,1)}, u32[]{:S(2)}) copy-start(bf16[4,5,128,128]{3,2,1,0:T(8,128)(2,1)} %margin.1) | copy-start | bytes 1966084
  0.6 0.7 %copy-start.2 = (s32[4,5]{1,0:T(4,128)S(1)}, s32[4,5]{1,0:T(4,128)}, u32[]{:S(2)}) copy-start(s32[4,5]{1,0:T(4,128)} %pattern_in.1) | copy-start | bytes 244
  1.4 1.1 %copy-start.1 = (bf16[4,5,128,128]{3,2,1,0:T(8,128)(2,1)S(1)}, bf16[4,5,128,128]{3,2,1,0:T(8,128)(2,1)}, u32[]{:S(2)}) copy-start(bf16[4,5,128,128]{3,2,1,0:T(8,128)(2,1)} %factor.1) | copy-start | bytes 1966084
  3.5 2.8 %collective-permute-start.2 = (bf16[31,128,128]{2,1,0:T(8,128)(2,1)S(1)}, bf16[31,128,128]{2,1,0:T(8,128)(2,1)S(1)}, u32[]{:S(2)}, u32[]{:S(2)}) collective-permute-start(bf16[31,128,128]{2,1,0:T(8,128)(2,1)S(1)} %get-tuple-element.28.near), channel_id=1, source_target_pairs={{0,1},{1,0},{2,3},{3,2},{4,5},{5,4},{6,7},{7,6},{8,9},{9,8},{10,11... | collective-permute-start | bytes 3047432 | tf_op jit(solution)/shard_map/ppermute | solution.py:561
  4.0 5.2 %collective-permute-start = (bf16[20,128,128]{2,1,0:T(8,128)(2,1)S(1)}, bf16[20,128,128]{2,1,0:T(8,128)(2,1)S(1)}, u32[]{:S(2)}, u32[]{:S(2)}) collective-permute-start(bf16[20,128,128]{2,1,0:T(8,128)(2,1)S(1)} %get-tuple-element.26.far), channel_id=1, source_target_pairs={{1,2},{2,1},{3,4},{4,3},{5,6},{6,5},{9,10},{10,9},{11,12},{12,11},... | collective-permute-start | bytes 1966088 | tf_op jit(solution)/shard_map/ppermute | solution.py:559
  4.7 4.5 %collective-permute-start.1 = (bf16[2,2,128,128]{3,2,1,0:T(8,128)(2,1)S(1)}, bf16[2,2,128,128]{3,2,1,0:T(8,128)(2,1)S(1)}, u32[]{:S(2)}, u32[]{:S(2)}) collective-permute-start(bf16[2,2,128,128]{3,2,1,0:T(8,128)(2,1)S(1)} %get-tuple-element.27), channel_id=1, source_target_pairs={{7,8},{8,7},{15,16},{16,15},{23,24},{24,23}} | collective-permute-start | bytes 393224 | tf_op jit(solution)/shard_map/ppermute | solution.py:560
  10.5 27.8 %collective-permute-start.3 = (bf16[2,256,256]{2,1,0:T(8,128)(2,1)S(1)}, bf16[2,256,256]{2,1,0:T(8,128)(2,1)S(1)}, u32[]{:S(2)}, u32[]{:S(2)}) collective-permute-start(bf16[2,256,256]{2,1,0:T(8,128)(2,1)S(1)} %get-tuple-element.42), channel_id=1, source_target_pairs={{1,2},{2,1},{3,4},{4,3},{5,6},{6,5},{7,8},{8,7},{9,10},{10,9},{11,... | collective-permute-start | bytes 786440 | tf_op jit(solution)/shard_map/ppermute | solution.py:569
  11.2 27.1 %copy-start.3 = (s32[4,5]{1,0:T(4,128)S(1)}, s32[4,5]{1,0:T(4,128)}, u32[]{:S(2)}) copy-start(s32[4,5]{1,0:T(4,128)} %pattern_in.1) | copy-start | bytes 244

commit v7 on v6

--- a/solution.py
+++ b/solution.py
@@ -140,26 +140,26 @@
             cells[t, o] = value.astype(cells.dtype)
 
 
-def mask_kernel(z, pattern, mask_near, mask_far):
+def mask_kernel(z, pattern, mask_near):
+    first, _ = half_starts(z)
     ones = jnp.ones((z.tile, z.tile), jnp.float32)
-    for out, first in zip((mask_near, mask_far), half_starts(z)):
-        for e in range(3):
-            out[e] = own_masked(z, pattern, first, e, ones).astype(out.dtype)
+    for e in range(3):
+        mask_near[e] = own_masked(z, pattern, first, e, ones).astype(mask_near.dtype)
 
 
 def masks(z, pattern, kind):
     return pl.pallas_call(
         functools.partial(mask_kernel, z),
-        out_shape=(z.tiles(3, kind), z.tiles(3, kind)),
+        out_shape=z.tiles(3, kind),
         in_specs=[SMEM],
-        out_specs=(VMEM, VMEM),
+        out_specs=VMEM,
         compiler_params=PARAMS,
         cost_estimate=z.cost(20, 1),
         name="masks",
     )(pattern)
 
 
-def pack_kernel(z, margin, factor, pattern, _near, _far, near, far, cross):
+def pack_kernel(z, margin, factor, pattern, _, near, far, cross):
     near_first, far_first = half_starts(z)
     first_row = lax.axis_index("slab") * z.columns
     plan = ((margin, far_first), (factor, far_first), (margin, near_first), (factor, near_first))
@@ -193,7 +193,7 @@
         near[3 * z.cells + f // per_block, low : low + FLAG_ROWS] = value
 
 
-def pack(z, margin, factor, pattern, mask_near, mask_far):
+def pack(z, margin, factor, pattern, mask_near):
     kind = margin.dtype
     return pl.pallas_call(
         functools.partial(pack_kernel, z),
@@ -202,11 +202,11 @@
             jax.ShapeDtypeStruct((2 * z.cells, z.block, z.block), kind),
             jax.ShapeDtypeStruct((z.half, z.half, z.block, z.block), kind),
         ),
-        in_specs=[VMEM, VMEM, SMEM, VMEM, VMEM],
+        in_specs=[VMEM, VMEM, SMEM, VMEM],
         out_specs=(VMEM, VMEM, VMEM),
         compiler_params=PARAMS,
         name="pack",
-    )(margin, factor, pattern, mask_near, mask_far)
+    )(margin, factor, pattern, mask_near)
 
 
 def inner_kernel(
@@ -379,43 +379,28 @@
 
 
 def middle_kernel(
-    z, squares, z_cols, z_far, d_far, d_near, base_near, e_near, mask_near, mask_far, refined, narrow, wide,
-    spread, square, done, parts, tiles, cells, sems,
+    z, squares, z_cols, z_far, d_far, d_near, base_near, e_near, mask_near, refined, narrow, spread,
+    square, tiles, cells, sems,
 ):
     near_first, _ = half_starts(z)
     moves = [
-        (z_far.at[pl.ds(1, 2)], narrow.at[pl.ds(0, 2)]),
-        (z_cols.at[0], narrow.at[pl.ds(2, 3)]),
-        (z_cols.at[1, pl.ds(0, 2)], narrow.at[pl.ds(5, 2)]),
-        (d_far.at[pl.ds(0, 1)], narrow.at[pl.ds(7, 1)]),
+        (d_far, narrow.at[pl.ds(0, 3)]),
+        (d_near.at[pl.ds(0, 2)], narrow.at[pl.ds(3, 2)]),
+        (z_far.at[pl.ds(1, 2)], narrow.at[pl.ds(5, 2)]),
+        (z_cols.at[0], narrow.at[pl.ds(7, 3)]),
+        (z_cols.at[1, pl.ds(0, 2)], narrow.at[pl.ds(10, 2)]),
     ]
     copies = [
         pltpu.make_async_copy(source, target, sems.at[k]) for k, (source, target) in enumerate(moves)
     ]
     for copy in copies:
         copy.start()
-
-    def send(source, target):
-        copies.append(pltpu.make_async_copy(source, target, sems.at[len(copies)]))
-        copies[-1].start()
-
     lanes = jnp.sum(squares[...], axis=0, keepdims=True)
     folded = lanes[:, : z.block]
     for t in range(1, z.half):
         folded = folded + lanes[:, t * z.block : (t + 1) * z.block]
     spread[...] = jnp.broadcast_to(folded[None], spread.shape)
-    factor = (z_far, z_cols.at[0], z_cols.at[1], z_cols.at[2])
-    defect = (None, d_far, d_near)
-    value = tile_product(defect, d_far, 2, 1, 1, 2) * mask_far[2].astype(jnp.float32)
-    done[0] = value.astype(done.dtype)
-    send(done, narrow.at[pl.ds(8, 1)])
-    for i in (0, 1):
-        parts[i] = tile_product(defect, d_far, i, 1, 1, 2)
-    for i in (0, 1, 2):
-        parts[2 + i] = z_cols[0, i].astype(jnp.float32) + 0.5 * tile_product(
-            factor, d_far, i, 1, 0, 2
-        )
-    send(parts, wide)
+    factor = (None, z_cols.at[0], z_cols.at[1], z_cols.at[2])
     for i in (1, 2, 3):
         value = e_near[i - 1]
         if i < 3:
@@ -425,119 +410,121 @@
         value = base_near[i - 1] + 0.375 * tile_product(factor, square, i, 2, 1, 3)
         tiles[i - 1] = value * mask_near[i - 1].astype(jnp.float32)
     store_half(z, tiles, cells)
-    send(cells, refined.at[pl.ds(near_first, z.half)])
+    copies.append(
+        pltpu.make_async_copy(cells, refined.at[pl.ds(near_first, z.half)], sems.at[len(moves)])
+    )
+    copies[-1].start()
     for copy in copies:
         copy.wait()
 
 
-def middle_step(z, squares, z_cols, z_far, d_far, d_near, base_near, e_near, mask_near, mask_far):
+def middle_step(z, squares, z_cols, z_far, d_far, d_near, base_near, e_near, mask_near):
     kind = z_far.dtype
     shape = (z.columns, z.offsets, z.block, z.block)
     return pl.pallas_call(
         functools.partial(middle_kernel, z),
         out_shape=(
             jax.ShapeDtypeStruct(shape, kind),
-            z.tiles(9, kind),
-            z.tiles(5, jnp.float32),
+            z.tiles(12, kind),
             jax.ShapeDtypeStruct((z.devices, 1, z.block), jnp.float32),
         ),
-        in_specs=[VMEM] * 9,
-        out_specs=(HBM, HBM, HBM, VMEM),
+        in_specs=[VMEM] * 8,
+        out_specs=(HBM, HBM, VMEM),
         scratch_shapes=[
             pltpu.VMEM((3, z.tile, z.tile), kind),
-            pltpu.VMEM((1, z.tile, z.tile), kind),
-            pltpu.VMEM((5, z.tile, z.tile), jnp.float32),
             pltpu.VMEM((3, z.tile, z.tile), jnp.float32),
             pltpu.VMEM((z.half,) + shape[1:], kind),
-            pltpu.SemaphoreType.DMA((7,)),
+            pltpu.SemaphoreType.DMA((6,)),
         ],
         compiler_params=PARAMS,
-        cost_estimate=z.cost(21, 6),
+        cost_estimate=z.cost(9, 6),
         name="middle",
-    )(squares, z_cols, z_far, d_far, d_near, base_near, e_near, mask_near, mask_far)
+    )(squares, z_cols, z_far, d_far, d_near, base_near, e_near, mask_near)
 
 
 def last_kernel(
-    z, pattern_in, narrow_in, wide_in, d_in, _, refined, _narrow, _wide, _d, pattern, narrow, wide, d_far,
-    square, tiles, cells, sems,
+    z, pattern_in, narrow_in, d_in, _, refined, _narrow, _d, pattern, narrow, d_beyond, square, tiles,
+    cells, sems,
 ):
     _, first = half_starts(z)
-    link = pl.ds(7, 2)
-    factor = pl.ds(0, 7)
     moves = (
         (pattern_in, pattern),
-        (d_in, d_far),
-        (narrow_in.at[link], narrow.at[link]),
-        (wide_in.at[pl.ds(0, 2)], wide.at[pl.ds(0, 2)]),
-        (narrow_in.at[factor], narrow.at[factor]),
-        (wide_in.at[pl.ds(2, 3)], wide.at[pl.ds(2, 3)]),
+        (d_in, d_beyond),
+        (narrow_in.at[pl.ds(0, 5)], narrow.at[pl.ds(0, 5)]),
+        (narrow_in.at[pl.ds(5, 7)], narrow.at[pl.ds(5, 7)]),
     )
     copies = [
         pltpu.make_async_copy(source, target, sems.at[k]) for k, (source, target) in enumerate(moves)
     ]
     for copy in copies:
         copy.start()
-    for copy in copies[:4]:
+    for copy in copies[:3]:
         copy.wait()
-    for i in (0, 1):
-        value = wide[i] + dot(d_far[1 - i], narrow[7])
+    values = (
+        dot(d_beyond[1], narrow[0]) + dot(narrow[0], narrow[1]),
+        dot(d_beyond[0], narrow[0]) + dot(narrow[1], narrow[1]) + dot(narrow[3], narrow[2]),
+        dot(narrow[2], narrow[1]) + dot(narrow[4], narrow[2]),
+    )
+    for i, value in enumerate(values):
         square[i] = own_masked(z, pattern, first, i, value).astype(square.dtype)
-    square[2] = narrow[8]
-    for copy in copies[4:]:
-        copy.wait()
-    base = (-1, 2, 5)
+    copies[3].wait()
+    base = (4, 7, 10)
     for i in (0, 1, 2):
-        total = None
+        half = None
+        rest = None
         for k in range(max(0, i - 1), min(2, i + 1) + 1):
-            term = dot(narrow[base[k] + i - k + 1], square[k])
-            total = term if total is None else total + term
-        tiles[i] = own_masked(z, pattern, first, i, wide[2 + i] + 0.375 * total)
+            left = narrow[base[k] + i - k + 1]
+            term = dot(left, narrow[k])
+            half = term if half is None else half + term
+            term = dot(left, square[k])
+            rest = term if rest is None else rest + term
+        value = narrow[7 + i].astype(jnp.float32) + 0.5 * half + 0.375 * rest
+        tiles[i] = own_masked(z, pattern, first, i, value)
     store_half(z, tiles, cells)
-    copy = pltpu.make_async_copy(cells, refined.at[pl.ds(first, z.half)], sems.at[6])
+    copy = pltpu.make_async_copy(cells, refined.at[pl.ds(first, z.half)], sems.at[4])
     copy.start()
     copy.wait()
 
 
-def last_step(z, pattern, narrow, wide, d_in, refined):
+def last_step(z, pattern, narrow, d_in, refined):
     kind = refined.dtype
     return pl.pallas_call(
         functools.partial(last_kernel, z),
         out_shape=tuple(
-            jax.ShapeDtypeStruct(held.shape, held.dtype) for held in (refined, narrow, wide, d_in)
+            jax.ShapeDtypeStruct(held.shape, held.dtype) for held in (refined, narrow, d_in)
         ),
-        in_specs=[HBM] * 5,
-        out_specs=(HBM,) * 4,
+        in_specs=[HBM] * 4,
+        out_specs=(HBM,) * 3,
         scratch_shapes=[
             pltpu.SMEM(pattern.shape, pattern.dtype),
             pltpu.VMEM(narrow.shape, kind),
-            pltpu.VMEM(wide.shape, jnp.float32),
             pltpu.VMEM(d_in.shape, kind),
             pltpu.VMEM((3, z.tile, z.tile), kind),
             pltpu.VMEM((3, z.tile, z.tile), jnp.float32),
             pltpu.VMEM((z.half,) + refined.shape[1:], kind),
-            pltpu.SemaphoreType.DMA((7,)),
+            pltpu.SemaphoreType.DMA((5,)),
         ],
-        input_output_aliases={4: 0, 1: 1, 2: 2, 3: 3},
-        compiler_params=PARAMS,
-        cost_estimate=z.cost(9, 4),
+        input_output_aliases={3: 0, 1: 1, 2: 2},
+        compiler_params=PARAMS,
+        cost_estimate=z.cost(21, 4),
         name="last",
-    )(pattern, narrow, wide, d_in, refined)[0]
-
-
-def norm_kernel(z, gathered, norm):
+    )(pattern, narrow, d_in, refined)
+
+
+def norm_kernel(z, gathered, _, norm):
     mean = jnp.sum(gathered[...]) * (1.0 / z.entries)
     norm[...] = jnp.sqrt(jnp.full(norm.shape, mean, jnp.float32))
 
 
-def norm_step(z, gathered):
+def norm_step(z, gathered, after):
     return pl.pallas_call(
         functools.partial(norm_kernel, z),
         out_shape=jax.ShapeDtypeStruct((1, z.block), jnp.float32),
-        in_specs=[VMEM],
+        in_specs=[VMEM, HBM],
         out_specs=VMEM,
         compiler_params=PARAMS,
         name="norm",
-    )(gathered)
+    )(gathered, after)
 
 
 def swaps(pairs):
@@ -554,25 +541,25 @@
     far_pairs = [(i, i + 1) for i in range(1, devices - 1, 2)]
     inner_pairs = [(i, j) for i, j in far_pairs if j % slabs]
     cross_pairs = [(i, j) for i, j in far_pairs if not j % slabs]
-    mask_near, mask_far = masks(z, pattern, margin.dtype)
-    near, far, cross = pack(z, margin, factor, pattern, mask_near, mask_far)
+    mask_near = masks(z, pattern, margin.dtype)
+    near, far, cross = pack(z, margin, factor, pattern, mask_near)
     beyond = lax.ppermute(far, AXES, swaps(inner_pairs))
     across = lax.ppermute(cross, AXES, swaps(cross_pairs))
     beside = lax.ppermute(near, AXES, swaps(near_pairs))
     z_cols, turned, p_part, d_part, d_near, squares, base_near, e_near = inner_step(
         z, pattern, near, far, beside
     )
-    held = (d_near, base_near, e_near, mask_near, mask_far)
+    held = (d_near, base_near, e_near, mask_near)
     d_far, d_out, z_far, squares = outer_step(
         z, pattern, beyond, across, z_cols, turned, p_part, d_part, squares, held
     )
     d_in = lax.ppermute(d_out, AXES, swaps(far_pairs))
-    refined, narrow, wide, spread = middle_step(
-        z, squares, z_cols, z_far, d_far, d_near, base_near, e_near, mask_near, mask_far
+    refined, narrow, spread = middle_step(
+        z, squares, z_cols, z_far, d_far, d_near, base_near, e_near, mask_near
     )
     gathered = lax.all_to_all(spread, AXES, 0, 0, tiled=True)
-    refined = last_step(z, pattern, narrow, wide, d_in, refined)
-    norm = norm_step(z, gathered)
+    refined, narrow, _ = last_step(z, pattern, narrow, d_in, refined)
+    norm = norm_step(z, gathered, narrow)
     return refined, norm[0, 0]
 
 

time: 40.7 us -> 38.3 us (0.941)
  blocking collectives: 23.4 us -> 0 us
  starting transfers between devices: 2.55 us -> 19 us
  waiting for transfers between devices: 0.87 us -> 5.5 us
    all_to_all x1 -> x0, blocking collectives: 23.4 us -> none  [per_device(): gathered = lax.all_to_all(spread, AXES, 0, 0, tiled=True)]
    all_to_all x0 -> x1, starting transfers between devices: none -> 16.5 us  [per_device(): gathered = lax.all_to_all(spread, AXES, 0, 0, tiled=True)]
    all_to_all x0 -> x1, waiting for transfers between devices: none -> 4.62 us  [per_device(): gathered = lax.all_to_all(spread, AXES, 0, 0, tiled=True)]
    pallas_call x1, Pallas kernels: 3.03 us -> 2.56 us  [middle_step(): pl.pallas_call(functools.partial(middle_kernel, z), out_shape=(jax.ShapeD...]
  transfers between devices with their start and end apart: 4 -> 5, of which waited for: 1 -> 2; matrix products, arithmetic and copies ran while one was open for 0% -> 0% of each run, Pallas kernels for 16% -> 21%
where the time goes in v7:
time: 38.3 us; the launch traced here: 38.1 us
  starting transfers between devices  19 us (50%)
  Pallas kernels  11.6 us (30%)
  waiting for transfers between devices  5.5 us (14%)
  local copies, waits for them, and re-layouts  1.25 us (3%)
  between operations  0.77 us (2%)
    all_to_all x1, starting transfers between devices, per_device(): gathered = lax.all_to_all(spread, AXES, 0, 0, tiled=True)  16.5 us
    all_to_all x1, waiting for transfers between devices, per_device(): gathered = lax.all_to_all(spread, AXES, 0, 0, tiled=True)  4.62 us
    pallas_call x1, Pallas kernels, inner_step(): pl.pallas_call(functools.partial(inner_kernel, z), out_shape=(jax.ShapeDt...  2.97 us
    pallas_call x1, Pallas kernels, middle_step(): pl.pallas_call(functools.partial(middle_kernel, z), out_shape=(jax.ShapeD...  2.56 us
    pallas_call x1, Pallas kernels, last_step(): pl.pallas_call(functools.partial(last_kernel, z), out_shape=tuple((jax.Sh...  2.48 us
    pallas_call x1, Pallas kernels, outer_step(): pl.pallas_call(functools.partial(outer_kernel, z), out_shape=(z.tiles(3,...  1.32 us
    unnamed x8, local copies, waits for them, and re-layouts  1.25 us
    pallas_call x1, Pallas kernels, pack(): pl.pallas_call(functools.partial(pack_kernel, z), out_shape=(jax.ShapeDty...  0.93 us
  transfers between devices with their start and end apart: 5, of which 2 were waited for; matrix products, arithmetic and copies ran while one was open for 0% of the time, Pallas kernels for 21%

profile of v7, /device:TPU:0, one launch (start us, length us, event | category | flops | bytes accessed | tf_op | source)
XLA Modules:
  0.0 38.1 jit_solution(10640753143810847966)
XLA Ops:
  0.6 0.0 copy-start
  0.6 0.0 copy-start.2
  0.7 0.7 %copy-done.2 = s32[4,5]{1,0:T(4,128)S(1)} copy-done((s32[4,5]{1,0:T(4,128)S(1)}, s32[4,5]{1,0:T(4,128)}, u32[]{:S(2)}) %copy-start.2) | copy-done | bytes 104
  1.4 0.0 copy-start.1
  1.4 0.6 %masks.1._.refs_3_.mask_near = bf16[3,256,256]{2,1,0:T(8,128)(2,1)S(1)} custom-call(s32[4,5]{1,0:T(4,128)S(1)} %copy-done.2), custom_call_target="tpu_custom_call" | custom-call | flops 671088640 | bytes 1048576 | tf_op jit(solution)/shard_map/masks/pallas_call | solution.py:151
  2.0 0.0 copy-done
  2.0 0.5 %copy-done.1 = bf16[4,5,128,128]{3,2,1,0:T(8,128)(2,1)S(1)} copy-done((bf16[4,5,128,128]{3,2,1,0:T(8,128)(2,1)S(1)}, bf16[4,5,128,128]{3,2,1,0:T(8,128)(2,1)}, u32[]{:S(2)}) %copy-start.1) | copy-done | bytes 655384
  2.5 0.9 %pack.1 = (bf16[31,128,128]{2,1,0:T(8,128)(2,1)S(1)}, bf16[20,128,128]{2,1,0:T(8,128)(2,1)S(1)}, bf16[2,2,128,128]{3,2,1,0:T(8,128)(2,1)S(1)}) custom-call(bf16[4,5,128,128]{3,2,1,0:T(8,128)(2,1)S(1)} %copy-done, bf16[4,5,128,128]{3,2,1,0:T(8,128)(2,1)S(1)} %copy-done.1, s32[4,5]{1,0:T(4,128)S(1)} %copy-done.2, bf16[3,256,256]{2,1,0:T(8,128)(2,1)S(1)} %masks.1._.refs_3_.mask_near), custom_call_target="tpu_custom_call" | custom-call | tf_op jit(solution)/shard_map/pack/pallas_call | solution.py:198
  3.5 0.5 %collective-permute-start.2 = (bf16[31,128,128]{2,1,0:T(8,128)(2,1)S(1)}, bf16[31,128,128]{2,1,0:T(8,128)(2,1)S(1)}, u32[]{:S(2)}, u32[]{:S(2)}) collective-permute-start(bf16[31,128,128]{2,1,0:T(8,128)(2,1)S(1)} %get-tuple-element.24.near), channel_id=1, source_target_pairs={{0,1},{1,0},{2,3},{3,2},{4,5},{5,4},{6,7},{7,6},{8,9},{9,8},{10,11... | collective-permute-start | bytes 3047432 | tf_op jit(solution)/shard_map/ppermute | solution.py:548
  4.0 0.7 %collective-permute-start = (bf16[20,128,128]{2,1,0:T(8,128)(2,1)S(1)}, bf16[20,128,128]{2,1,0:T(8,128)(2,1)S(1)}, u32[]{:S(2)}, u32[]{:S(2)}) collective-permute-start(bf16[20,128,128]{2,1,0:T(8,128)(2,1)S(1)} %get-tuple-element.22.far), channel_id=1, source_target_pairs={{1,2},{2,1},{3,4},{4,3},{5,6},{6,5},{9,10},{10,9},{11,12},{12,11},... | collective-permute-start | bytes 1966088 | tf_op jit(solution)/shard_map/ppermute | solution.py:546
  4.7 0.7 %collective-permute-start.1 = (bf16[2,2,128,128]{3,2,1,0:T(8,128)(2,1)S(1)}, bf16[2,2,128,128]{3,2,1,0:T(8,128)(2,1)S(1)}, u32[]{:S(2)}, u32[]{:S(2)}) collective-permute-start(bf16[2,2,128,128]{3,2,1,0:T(8,128)(2,1)S(1)} %get-tuple-element.23), channel_id=1, source_target_pairs={{7,8},{8,7},{15,16},{16,15},{23,24},{24,23}} | collective-permute-start | bytes 393224 | tf_op jit(solution)/shard_map/ppermute | solution.py:547
  5.4 0.9 %collective-permute-done.2.beside = bf16[31,128,128]{2,1,0:T(8,128)(2,1)S(1)} collective-permute-done((bf16[31,128,128]{2,1,0:T(8,128)(2,1)S(1)}, bf16[31,128,128]{2,1,0:T(8,128)(2,1)S(1)}, u32[]{:S(2)}, u32[]{:S(2)}) %collective-permute-start.2) | collective-permute-done | bytes 1015840 | tf_op jit(solution)/shard_map/ppermute | solution.py:548
  6.2 3.0 %inner.1 = (bf16[3,3,256,256]{3,2,1,0:T(8,128)(2,1)S(1)}, bf16[3,256,256]{2,1,0:T(8,128)(2,1)S(1)}, f32[2,256,256]{2,1,0:T(8,128)S(1)}, f32[2,256,256]{2,1,0:T(8...) custom-call(s32[4,5]{1,0:T(4,128)S(1)} %copy-done.2, ...), custom_call_target="tpu_custom_call" | custom-call | flops 1811939328 | bytes 8388608 | tf_op jit(solution)/shard_map/inner/pallas_call | solution.py:299
  9.2 0.0 collective-permute-done.1.cross
  9.2 0.0 collective-permute-done.far
  9.2 1.3 %outer.1 = (bf16[3,256,256]{2,1,0:T(8,128)(2,1)S(1)}, bf16[2,256,256]{2,1,0:T(8,128)(2,1)S(1)}, bf16[3,256,256]{2,1,0:T(8,128)(2,1)S(1)}, f32[8,256]{1,0:T(8,128)S(1)}) custom-call(s32[4,5]{1,0:T(4,128)S(1)} %copy-done.2, bf16[20,128,128]{2,1,0:T(8,128)(2,1)S(1)} %collective-permute-done.far, bf16[2,2,128,128]{3,2,1,0:T(8,128)(2,1)S(1)} %collective-permute-done.1.cross, ...), custom_call_target="tpu_custom_call" | custom-call | flops 301989888 | bytes 4194304 | tf_op jit(solution)/shard_map/outer/pallas_call | solution.py:364
  10.5 0.7 %collective-permute-start.3 = (bf16[2,256,256]{2,1,0:T(8,128)(2,1)S(1)}, bf16[2,256,256]{2,1,0:T(8,128)(2,1)S(1)}, u32[]{:S(2)}, u32[]{:S(2)}) collective-permute-start(bf16[2,256,256]{2,1,0:T(8,128)(2,1)S(1)} %get-tuple-element.37), channel_id=1, source_target_pairs={{1,2},{2,1},{3,4},{4,3},{5,6},{6,5},{7,8},{8,7},{9,10},{10,9},{11,... | collective-permute-start | bytes 786440 | tf_op jit(solution)/shard_map/ppermute | solution.py:556
  11.2 0.0 copy-start.3
  11.2 2.6 %middle.1 = (bf16[4,5,128,128]{3,2,1,0:T(8,128)(2,1)}, bf16[12,256,256]{2,1,0:T(8,128)(2,1)S(1)}, f32[32,1,128]{2,1,0:T(1,128)}) custom-call(f32[8,256]{1,0:T(8,128)S(1)} %get-tuple-element.33.squares, bf16[3,3,256,256]{3,2,1,0:T(8,128)(2,1)S(1)} %get-tuple-element.25.z_cols, bf16[3,256,256]{2,1,0:T(8,128)(2,1)S(1)} %get-tuple-element.34.z_far, ...), custom_call_target="tpu_custom_call" | custom-call | flops 301989888 | bytes 6291456 | tf_op jit(solution)/shard_map/middle/pallas_call | solution.py:424
  13.8 16.5 %all-to-all-start = ((f32[32,1,128]{2,1,0:T(1,128)}), f32[32,1,128]{2,1,0:T(1,128)S(1)}, u32[]{:S(2)}, u32[]{:S(2)}) async-start(f32[32,1,128]{2,1,0:T(1,128)} %get-tuple-element.40), calls=%async_computation | async-start | bytes 32768 | tf_op jit(solution)/shard_map/all_to_all | solution.py:560
  30.3 0.0 collective-permute-done.3.d_in
  30.3 0.0 copy-done.3
  30.3 2.5 %last.1 = (bf16[4,5,128,128]{3,2,1,0:T(8,128)(2,1)}, bf16[12,256,256]{2,1,0:T(8,128)(2,1)S(1)}, bf16[2,256,256]{2,1,0:T(8,128)(2,1)S(1)}) custom-call(s32[4,5]{1,0:T(4,128)S(1)} %copy-done.3, bf16[12,256,256]{2,1,0:T(8,128)(2,1)S(1)} %get-tuple-element.36.narrow_in, ...), custom_call_target="tpu_custom_call", output_to_operand_aliasing={{0}: (3, {}), {1}: (1, {}), {2}: (2, {})} | custom-call | flops 704643072 | bytes 4194304 | tf_op jit(solution)/shard_map/last/pallas_call | solution.py:491
  32.8 4.6 %all-to-all-done.gathered = f32[32,1,128]{2,1,0:T(1,128)S(1)} async-done(((f32[32,1,128]{2,1,0:T(1,128)}), f32[32,1,128]{2,1,0:T(1,128)S(1)}, u32[]{:S(2)}, u32[]{:S(2)}) %all-to-all-start) | async-done | bytes 16416 | tf_op jit(solution)/shard_map/all_to_all | solution.py:560
  37.4 0.7 %norm.1 = f32[1,128]{1,0:T(1,128)} custom-call(f32[32,1,128]{2,1,0:T(1,128)S(1)} %all-to-all-done.gathered, bf16[12,256,256]{2,1,0:T(8,128)(2,1)S(1)} %get-tuple-element.41._), custom_call_target="tpu_custom_call" | custom-call | tf_op jit(solution)/shard_map/norm/pallas_call | solution.py:520
Async XLA Ops:
  0.6 1.4 %copy-start = (bf16[4,5,128,128]{3,2,1,0:T(8,128)(2,1)S(1)}, bf16[4,5,128,128]{3,2,1,0:T(8,128)(2,1)}, u32[]{:S(2)}) copy-start(bf16[4,5,128,128]{3,2,1,0:T(8,128)(2,1)} %margin.1) | copy-start | bytes 1966084
  0.6 0.7 %copy-start.2 = (s32[4,5]{1,0:T(4,128)S(1)}, s32[4,5]{1,0:T(4,128)}, u32[]{:S(2)}) copy-start(s32[4,5]{1,0:T(4,128)} %pattern_in.1) | copy-start | bytes 244
  1.4 1.1 %copy-start.1 = (bf16[4,5,128,128]{3,2,1,0:T(8,128)(2,1)S(1)}, bf16[4,5,128,128]{3,2,1,0:T(8,128)(2,1)}, u32[]{:S(2)}) copy-start(bf16[4,5,128,128]{3,2,1,0:T(8,128)(2,1)} %factor.1) | copy-start | bytes 1966084
  3.5 2.8 %collective-permute-start.2 = (bf16[31,128,128]{2,1,0:T(8,128)(2,1)S(1)}, bf16[31,128,128]{2,1,0:T(8,128)(2,1)S(1)}, u32[]{:S(2)}, u32[]{:S(2)}) collective-permute-start(bf16[31,128,128]{2,1,0:T(8,128)(2,1)S(1)} %get-tuple-element.24.near), channel_id=1, source_target_pairs={{0,1},{1,0},{2,3},{3,2},{4,5},{5,4},{6,7},{7,6},{8,9},{9,8},{10,11... | collective-permute-start | bytes 3047432 | tf_op jit(solution)/shard_map/ppermute | solution.py:548
  4.0 5.2 %collective-permute-start = (bf16[20,128,128]{2,1,0:T(8,128)(2,1)S(1)}, bf16[20,128,128]{2,1,0:T(8,128)(2,1)S(1)}, u32[]{:S(2)}, u32[]{:S(2)}) collective-permute-start(bf16[20,128,128]{2,1,0:T(8,128)(2,1)S(1)} %get-tuple-element.22.far), channel_id=1, source_target_pairs={{1,2},{2,1},{3,4},{4,3},{5,6},{6,5},{9,10},{10,9},{11,12},{12,11},... | collective-permute-start | bytes 1966088 | tf_op jit(solution)/shard_map/ppermute | solution.py:546
  4.7 4.5 %collective-permute-start.1 = (bf16[2,2,128,128]{3,2,1,0:T(8,128)(2,1)S(1)}, bf16[2,2,128,128]{3,2,1,0:T(8,128)(2,1)S(1)}, u32[]{:S(2)}, u32[]{:S(2)}) collective-permute-start(bf16[2,2,128,128]{3,2,1,0:T(8,128)(2,1)S(1)} %get-tuple-element.23), channel_id=1, source_target_pairs={{7,8},{8,7},{15,16},{16,15},{23,24},{24,23}} | collective-permute-start | bytes 393224 | tf_op jit(solution)/shard_map/ppermute | solution.py:547
  10.5 19.7 %collective-permute-start.3 = (bf16[2,256,256]{2,1,0:T(8,128)(2,1)S(1)}, bf16[2,256,256]{2,1,0:T(8,128)(2,1)S(1)}, u32[]{:S(2)}, u32[]{:S(2)}) collective-permute-start(bf16[2,256,256]{2,1,0:T(8,128)(2,1)S(1)} %get-tuple-element.37), channel_id=1, source_target_pairs={{1,2},{2,1},{3,4},{4,3},{5,6},{6,5},{7,8},{8,7},{9,10},{10,9},{11,... | collective-permute-start | bytes 786440 | tf_op jit(solution)/shard_map/ppermute | solution.py:556
  11.2 19.1 %copy-start.3 = (s32[4,5]{1,0:T(4,128)S(1)}, s32[4,5]{1,0:T(4,128)}, u32[]{:S(2)}) copy-start(s32[4,5]{1,0:T(4,128)} %pattern_in.1) | copy-start | bytes 244
  13.8 23.6 %all-to-all-start = ((f32[32,1,128]{2,1,0:T(1,128)}), f32[32,1,128]{2,1,0:T(1,128)S(1)}, u32[]{:S(2)}, u32[]{:S(2)}) async-start(f32[32,1,128]{2,1,0:T(1,128)} %get-tuple-element.40), calls=%async_computation | async-start | bytes 32768 | tf_op jit(solution)/shard_map/all_to_all | solution.py:560
